TPU v7x, 32 devices: a whole 2x2x4 slice. The times are simulated.
32 devices in a mesh: grp: 2 (over y), space: 4 (over z), tm: 2 (over x), sub: 2 (over core).
Axes of the slice: x: 2, y: 2, z: 4, core: 2. Of those that a mesh axis runs over, the one named last changes fastest.
Arguments:
- gauge_links: float32 [4, 18, 8, 16, 4, 128], P(None, None, ('grp', 'tm'), 'space', 'sub'), parts along dimension 2, may hold values from -1 to 1, as said below
- active_blocks: int32 [4, 4, 2, 4, 4], P('grp'), parts along dimension 0, may hold values from 0 to 1, as said below
- conv_in: bfloat16 [2, 81, 12, 64], replicated, may hold values from -0.1875 to 0.1875
- bias_in: float32 [2, 64], replicated, may hold values from -3 to 3
- conv_out: bfloat16 [2, 64, 24], replicated, may hold values from -0.75 to 0.75
- bias_out: float32 [2, 24], replicated, may hold values from -3 to 3
Outputs:
- flowed_links: float32 [4, 18, 8, 16, 4, 128], P(None, None, ('grp', 'tm'), 'space', 'sub'), parts along dimension 2
There are 2 independent parts, one for each index of `grp`. A program takes and returns all parts, laid end to end along the dimension named above; an argument that names none is the same for every part. Nothing has to cross between parts.
Inputs may be any that keep to these rules, and one draw needn't show every extreme that they name: For every direction and site the 3x3 complex matrix of gauge_links is unitary. `active_blocks`: for each layer and direction the active blocks form a checkerboard over time, x and y blocks; which of its two colours is active is drawn for each layer and direction.
All inputs are finite; a program needn't handle non-finite values.
Results may differ from a plain program's by a relative error of at most 0.0019.
Values may be sent and summed in bfloat16 or wider, within the bound.
No kernel may reach another device: no remote copies, remote signals or barrier semaphores. Data moves between devices by JAX's collectives and lax.ppermute only.
A program may use at most 128 MiB of HBM per device.

v0:
```python
import jax
import jax.numpy as jnp
from jax import lax
from jax.experimental import pallas as pl
from jax.experimental.pallas import tpu as pltpu
from jax.sharding import PartitionSpec as P

PAIRS = ((0, 1), (0, 2), (0, 3), (1, 2), (1, 3), (2, 3))
F32 = jnp.float32
BF16 = jnp.bfloat16
BASE = 8
LIMIT = 56 * 1024 * 1024


def mm(a, b, a_dag=False, b_dag=False):
    out_re, out_im = [], []
    for i in range(3):
        row_re, row_im = [], []
        for j in range(3):
            re = im = None
            for k in range(3):
                ar, ai = (a[0][k][i], a[1][k][i]) if a_dag else (a[0][i][k], a[1][i][k])
                br, bi = (b[0][j][k], b[1][j][k]) if b_dag else (b[0][k][j], b[1][k][j])
                if a_dag:
                    r, m = ar * br + ai * bi, ar * bi - ai * br
                elif b_dag:
                    r, m = ar * br + ai * bi, ai * br - ar * bi
                else:
                    r, m = ar * br - ai * bi, ar * bi + ai * br
                re = r if re is None else re + r
                im = m if im is None else im + m
            row_re.append(re)
            row_im.append(im)
        out_re.append(row_re)
        out_im.append(row_im)
    return out_re, out_im


def as_matrix(parts):
    return (
        [[parts[3 * i + j] for j in range(3)] for i in range(3)],
        [[parts[9 + 3 * i + j] for j in range(3)] for i in range(3)],
    )


def flat(matrix):
    return [matrix[0][i][j] for i in range(3) for j in range(3)] + [
        matrix[1][i][j] for i in range(3) for j in range(3)
    ]


def cmul(a, b):
    return a[0] * b[0] - a[1] * b[1], a[0] * b[1] + a[1] * b[0]


def zroll(value, step):
    return pltpu.roll(value, (-step) % value.shape[-1], value.ndim - 1)


def trace_kernel(own, own_s, tp, h, pm, out, v0, vup, trs):
    even = lax.broadcasted_iota(jnp.int32, (8, 128), 0) % 2 == 0

    def prep(i, _):
        for y in range(2):
            o = own[i, y]
            t = tp[i, y]
            v0[i, y, BASE : BASE + 8] = o
            v0[i, y, BASE + 8 : BASE + 10] = h[i, y, 2:4]
            vup[i, y] = jnp.where(even, pltpu.roll(o, 7, 0), pltpu.roll(t, 1, 0))
        v0[i, 2, BASE : BASE + 8] = own_s[i, 0]
        return 0

    lax.fori_loop(0, 72, prep, 0, unroll=4)
    trs[192:256] = jnp.zeros((64, 128), F32)

    def at_y(y, _):
        def look(d, step):
            if step == 0:
                parts = [vup[18 * d + c, y] for c in range(18)]
            elif step == 1:
                parts = [v0[18 * d + c, y, BASE + 2 : BASE + 10] for c in range(18)]
            elif step == 2:
                parts = [v0[18 * d + c, y + 1, BASE : BASE + 8] for c in range(18)]
            else:
                parts = [v0[18 * d + c, y, BASE : BASE + 8] for c in range(18)]
                if step == 3:
                    parts = [zroll(p, 1) for p in parts]
            return as_matrix(parts)

        for p, (m, n) in enumerate(PAIRS):
            a = flat(mm(look(m, None), look(n, m)))
            b = flat(mm(look(n, None), look(m, n)))
            re = im = None
            for k in range(9):
                r = a[k] * b[k] + a[9 + k] * b[9 + k]
                q = a[9 + k] * b[k] - a[k] * b[9 + k]
                re = r if re is None else re + r
                im = q if im is None else im + q
            keep = pm[p, y] * (1.0 / 3.0)
            row = pl.multiple_of(y * 8, 8)
            trs[pl.ds((2 * p) * 16 + row, 8)] = re * keep
            trs[pl.ds((2 * p + 1) * 16 + row, 8)] = im * keep
        return 0

    lax.fori_loop(0, 2, at_y, 0)
    for r in range(16):
        out[r] = trs[pl.ds(r, 16, stride=16), :].astype(BF16)


def staple_kernel(ya, own, own_s, tp, tp_s, h, h_s, co, co_s, out, v0, vup, vdn):
    even = lax.broadcasted_iota(jnp.int32, (8, 128), 0) % 2 == 0
    places = ((1, 1), (0, 0), (0, 1), (1, 0))

    def prep(i, _):
        for y, (other, at) in enumerate(places):
            o = (own, own_s)[other][i, at]
            t = (tp, tp_s)[other][i, at]
            hh = (h, h_s)[other]
            v0[i, y, BASE : BASE + 8] = o
            v0[i, y, BASE - 2 : BASE] = hh[i, at, 0:2]
            v0[i, y, BASE + 8 : BASE + 10] = hh[i, at, 2:4]
            vup[i, y, BASE : BASE + 8] = jnp.where(even, pltpu.roll(o, 7, 0), pltpu.roll(t, 1, 0))
            vdn[i, y, BASE : BASE + 8] = jnp.where(even, pltpu.roll(t, 7, 0), pltpu.roll(o, 1, 0))
        return 0

    lax.fori_loop(0, 72, prep, 0, unroll=4)

    def corner(c, _):
        for y, (other, at) in enumerate(places):
            hh, cc = (h, h_s)[other], (co, co_s)[other]
            vup[18 + c, y, BASE - 2 : BASE - 1] = hh[18 + c, at, 1:2]
            vup[18 + c, y, BASE - 1 : BASE] = cc[c, at, 0:1]
            vdn[c, y, BASE + 8 : BASE + 9] = cc[c, at, 1:2]
            vdn[c, y, BASE + 9 : BASE + 10] = hh[c, at, 2:3]
        return 0

    lax.fori_loop(0, 18, corner, 0, unroll=2)

    for m in range(4):
        yy = ya[m] + 1

        def look(d, offset):
            source = {0: v0, 1: vup, -1: vdn}[offset[0]]
            row = BASE + 2 * offset[1]
            parts = [source[18 * d + c, yy + offset[2], row : row + 8] for c in range(18)]
            if offset[3] != 0:
                parts = [zroll(p, offset[3]) for p in parts]
            return as_matrix(parts)

        zero = (0, 0, 0, 0)
        others = [n for n in range(4) if n != m]
        for j, n in enumerate(others):
            step_m = tuple(int(k == m) for k in range(4))
            step_n = tuple(int(k == n) for k in range(4))
            back_n = tuple(-k for k in step_n)
            corner_mn = tuple(a - b for a, b in zip(step_m, step_n))
            up = mm(look(n, step_m), mm(look(n, zero), look(m, step_n)), b_dag=True)
            for c, value in enumerate(flat(up)):
                out[6 * m + 2 * j, c] = value
            down = mm(mm(look(m, back_n), look(n, corner_mn)), look(n, back_n), a_dag=True)
            for c, value in enumerate(flat(down)):
                out[6 * m + 2 * j + 1, c] = value


def final_kernel(ya, own, staples, f, f_s, w_in, b_in, w_out, b_out, out, wts):
    places = ((1, 1), (0, 0), (0, 1), (1, 0))
    for y in range(2):
        for x in range(4):
            columns = []
            for t in range(2):
                tiles = []
                for a in range(3):
                    for b in range(3):
                        for c in range(3):
                            other, at = places[y + c]
                            tiles.append((f, f_s)[other][at, x + b, t + a])
                columns.append(jnp.concatenate(tiles, axis=0))
            patch = jnp.concatenate(columns, axis=1)
            g = jnp.dot(w_in[...], patch, preferred_element_type=F32)
            for t in range(2):
                lanes = slice(128 * t, 128 * t + 128)
                hidden = (
                    zroll(g[0:64, lanes], -1) + g[64:128, lanes] + zroll(g[128:192, lanes], 1)
                )
                hidden = jnp.tanh(hidden + b_in[...]).astype(BF16)
                weights = jnp.dot(w_out[...], hidden, preferred_element_type=F32) + b_out[...]
                row = 24 * (2 * x + t)
                wts[y, row : row + 24] = weights

    for m in range(4):
        y = ya[m]
        link = as_matrix([own[18 * m + c, y] for c in range(18)])
        total = None
        for k in range(6 * m, 6 * m + 6):
            w = wts[y, pl.ds(k, 8, stride=24), :]
            term = [w * staples[k, c] for c in range(18)]
            total = term if total is None else [a + b for a, b in zip(total, term)]
        are, aim = mm(link, as_matrix(total))
        trace_im = (aim[0][0] + aim[1][1] + aim[2][2]) * (1.0 / 3.0)
        low = [[None] * 3 for _ in range(3)]
        for i in range(3):
            low[i][i] = (jnp.ones_like(trace_im), -0.5 * (aim[i][i] - trace_im))
            for k in range(i + 1, 3):
                qr = -0.25 * (are[i][k] - are[k][i])
                qi = -0.25 * (aim[i][k] + aim[k][i])
                low[i][k] = (qr, qi)
                low[k][i] = (-qr, qi)
        adj_re, adj_im = [], []
        for i in range(3):
            row_re, row_im = [], []
            for j in range(3):
                first = cmul(low[(j + 1) % 3][(i + 1) % 3], low[(j + 2) % 3][(i + 2) % 3])
                second = cmul(low[(j + 1) % 3][(i + 2) % 3], low[(j + 2) % 3][(i + 1) % 3])
                row_re.append(first[0] - second[0])
                row_im.append(first[1] - second[1])
            adj_re.append(row_re)
            adj_im.append(row_im)
        det_re = det_im = None
        for k in range(3):
            product = cmul(low[0][k], (adj_re[k][0], adj_im[k][0]))
            det_re = product[0] if det_re is None else det_re + product[0]
            det_im = product[1] if det_im is None else det_im + product[1]
        twice = 2.0 / (det_re * det_re + det_im * det_im)
        scale_re = det_re * twice
        scale_im = -det_im * twice
        turned = flat(mm((adj_re, adj_im), link))
        current = flat(link)
        for c in range(9):
            re, im = cmul((turned[c], turned[9 + c]), (scale_re, scale_im))
            out[18 * m + c, y] = re - current[c]
            out[18 * m + 9 + c, y] = im - current[9 + c]
        for c in range(18):
            out[18 * m + c, 1 - y] = own[18 * m + c, 1 - y]


VM = pl.BlockSpec(memory_space=pltpu.VMEM)
SM = pl.BlockSpec(memory_space=pltpu.SMEM)
PARAMS = pltpu.CompilerParams(vmem_limit_bytes=LIMIT)


def run_traces(own, own_s, tp, h, pm):
    return pl.pallas_call(
        trace_kernel,
        out_shape=jax.ShapeDtypeStruct((16, 16, 128), BF16),
        in_specs=[VM] * 5,
        out_specs=VM,
        scratch_shapes=[
            pltpu.VMEM((72, 3, 24, 128), F32),
            pltpu.VMEM((72, 2, 8, 128), F32),
            pltpu.VMEM((256, 128), F32),
        ],
        compiler_params=PARAMS,
        cost_estimate=pl.CostEstimate(flops=8_000_000, bytes_accessed=2_000_000, transcendentals=0),
        name="traces",
    )(own, own_s, tp, h, pm)


def run_staples(ya, own, own_s, tp, tp_s, h, h_s, co, co_s):
    return pl.pallas_call(
        staple_kernel,
        out_shape=jax.ShapeDtypeStruct((24, 18, 8, 128), F32),
        in_specs=[SM] + [VM] * 8,
        out_specs=VM,
        scratch_shapes=[pltpu.VMEM((72, 4, 24, 128), F32)] * 3,
        compiler_params=PARAMS,
        cost_estimate=pl.CostEstimate(flops=20_000_000, bytes_accessed=5_000_000, transcendentals=0),
        name="staples",
    )(ya, own, own_s, tp, tp_s, h, h_s, co, co_s)


def run_final(ya, own, staples, f, f_s, w_in, b_in, w_out, b_out):
    return pl.pallas_call(
        final_kernel,
        out_shape=jax.ShapeDtypeStruct((72, 2, 8, 128), F32),
        in_specs=[SM] + [VM] * 8,
        out_specs=VM,
        scratch_shapes=[pltpu.VMEM((2, 192, 128), F32)],
        compiler_params=PARAMS,
        cost_estimate=pl.CostEstimate(flops=300_000_000, bytes_accessed=4_000_000, transcendentals=131072),
        name="rotate",
    )(ya, own, staples, f, f_s, w_in, b_in, w_out, b_out)


def step(value, axis, by):
    count = lax.axis_size(axis)
    return lax.ppermute(value, axis, [((i + by) % count, i) for i in range(count)])


def other_time(value, dim):
    if lax.axis_size("tm") == 2:
        return step(value, "tm", 1)
    up = step(lax.slice_in_dim(value, 0, 1, axis=dim), "tm", 1)
    down = step(lax.slice_in_dim(value, 1, 2, axis=dim), "tm", -1)
    return jnp.concatenate([up, down], axis=dim)


def exchange(own):
    tp = other_time(own.reshape(72, 2, 4, 2, 128), 3).reshape(own.shape)
    left = step(own[:, :, 6:8], "space", -1)
    right = step(own[:, :, 0:2], "space", 1)
    h = jnp.concatenate([left, right], axis=2)
    mixed = jnp.concatenate([left[18:36, :, 0:1], right[0:18, :, 1:2]], axis=2)
    co = other_time(mixed, 2)
    return tp, h, co


def traces_rim(tr):
    tp = other_time(tr, 2)
    full = jnp.concatenate([tp[:, :, 1:2], tr, tp[:, :, 0:1]], axis=2)
    left = step(full[:, 3:4], "space", -1)
    right = step(full[:, 0:1], "space", 1)
    return jnp.concatenate([left, full, right], axis=1)


def active_window(active_blocks):
    t_len, x_len, y_len = 2, 4, 2

    def blocks(axis, length, lo, hi):
        total = lax.axis_size(axis) * length
        at = (lax.axis_index(axis) * length + jnp.arange(lo, hi, dtype=jnp.int32)) % total
        return at // length, at

    t_block, _ = blocks("tm", t_len, -1, 3)
    x_block, _ = blocks("space", x_len, -1, 5)
    _, y_at = blocks("sub", y_len, -1, 3)
    y_block = 2 * y_at // y_len
    table = (active_blocks > 0).astype(F32)

    def pick(table, at, dim):
        hot = (at[:, None] == jnp.arange(table.shape[dim])[None]).astype(F32)
        return jnp.tensordot(table, hot, axes=((dim,), (1,)), precision=lax.Precision.HIGHEST)

    table = pick(table, x_block, 3)
    table = pick(table, t_block, 2)
    return pick(table, y_block, 2)


def plane_masks(active):
    frozen = 1.0 - active

    def at(m, d):
        start = [1, 1, 1]
        if d is not None and d < 3:
            start[(1, 0, 2)[d]] += 1
        a, b, c = start
        return frozen[:, m, a : a + 4, b : b + 2, c : c + 2]

    masks = jnp.stack([at(m, None) * at(n, m) * at(m, n) * at(n, None) for m, n in PAIRS], axis=1)
    masks = jnp.transpose(masks, (0, 1, 4, 2, 3)).reshape(2, 6, 2, 8, 1)
    return jnp.broadcast_to(masks, (2, 6, 2, 8, 128))


def per_device(gauge_links, active_blocks, conv_in, bias_in, conv_out, bias_out):
    own = jnp.transpose(gauge_links, (0, 1, 4, 3, 2, 5)).reshape(72, 2, 8, 128)
    active = active_window(active_blocks)
    pm = plane_masks(active)
    ya = (active[:, :, 1, 1, 1] < 0.5).astype(jnp.int32)
    w_in = jnp.transpose(conv_in.reshape(2, 3, 3, 3, 3, 12, 64), (0, 4, 6, 1, 2, 3, 5))
    w_in = jnp.pad(w_in, [(0, 0)] * 6 + [(0, 4)]).reshape(2, 192, 432)
    w_out = jnp.transpose(conv_out, (0, 2, 1))
    b_in = jnp.broadcast_to(bias_in[:, :, None], (2, 64, 128))
    b_out = jnp.broadcast_to(bias_out[:, :, None], (2, 24, 128))

    for layer in range(2):
        if layer == 1:
            incoming = step(own[:, :, 0:4], "space", 1)
            own = jnp.concatenate([own[:, :, 4:8], incoming], axis=2)
        own_s = step(own, "sub", 1)
        tp, h, co = exchange(own)
        h_s = step(h, "sub", 1)
        co_s = step(co, "sub", 1)
        tp_s = step(tp, "sub", 1)
        tr = run_traces(own, own_s, tp, h, pm[layer])
        f = traces_rim(tr.reshape(2, 4, 2, 16, 128))
        f_s = step(f, "sub", 1)
        staples = run_staples(ya[layer], own, own_s, tp, tp_s, h, h_s, co, co_s)
        own = run_final(
            ya[layer], own, staples, f, f_s, w_in[layer], b_in[layer], w_out[layer], b_out[layer]
        )
    out = own.reshape(4, 18, 2, 4, 2, 128)
    return jnp.transpose(out, (0, 1, 4, 3, 2, 5))


def solution(mesh):
    placed = (
        P(None, None, ("grp", "tm"), "space", "sub", None),
        P("grp", None, None, None, None),
        P(),
        P(),
        P(),
        P(),
    )
    return jax.shard_map(
        per_device,
        mesh=mesh,
        in_specs=placed,
        out_specs=P(None, None, ("grp", "tm"), "space", "sub", None),
        check_vma=False,
    )
```

profile of v0, /device:TPU:0, one launch (start us, length us, event | category | flops | bytes accessed | tf_op | source)
XLA Modules:
  0.0 121.0 jit_solution(18274542151109216017)
XLA Ops:
  0.0 1.4 %copy.15 = f32[4,18,2,4,2,128]{5,4,3,2,1,0:T(2,128)S(1)} copy(f32[4,18,2,4,2,128]{5,2,3,4,1,0:T(2,128)} %bitcast.66) | data formatting | bytes 1179648 | tf_op jit(solution)/shard_map/transpose | solution.py:354
  1.9 1.4 %copy.16 = f32[72,2,4,2,128]{4,3,2,1,0:T(2,128)S(1)} copy(f32[72,2,4,2,128]{4,1,2,3,0:T(2,128)} %bitcast.67) | data formatting | bytes 1179648 | tf_op jit(solution)/shard_map/reshape;reshape | solution.py:298
  3.3 2.7 %collective-permute-start.1 = (f32[72,2,4,2,128]{4,3,2,1,0:T(2,128)S(1)}, f32[72,2,4,2,128]{4,3,2,1,0:T(2,128)S(1)}, u32[]{:S(2)}, u32[]{:S(2)}) collective-permute-start(f32[72,2,4,2,128]{4,3,2,1,0:T(2,128)S(1)} %copy.16), channel_id=1, source_target_pairs={{2,0},{0,2},{3,1},{1,3},{6,4},{4,6},{7,5},{5,7},{10,8},{8,10},{11,... | collective-permute-start | bytes 1769480 | tf_op jit(solution)/shard_map/ppermute | solution.py:286
  6.8 3.6 %collective-permute-start.4 = (f32[72,2,2,128]{3,2,1,0:T(2,128)}, f32[72,2,2,128]{3,2,1,0:T(2,128)S(1)}, u32[]{:S(2)}, u32[]{:S(2)}) collective-permute-start(f32[72,2,2,128]{3,2,1,0:T(2,128)} %get-tuple-element.10), channel_id=1, source_target_pairs={{4,0},{8,4},{12,8},{0,12},{5,1},{9,5},{13,9},{1,13},{6,2},{10,6},{... | collective-permute-start | bytes 442376 | tf_op jit(solution)/shard_map/ppermute | solution.py:286
  12.7 2.3 %collective-permute-done.4 = f32[72,2,2,128]{3,2,1,0:T(2,128)S(1)} collective-permute-done((f32[72,2,2,128]{3,2,1,0:T(2,128)}, f32[72,2,2,128]{3,2,1,0:T(2,128)S(1)}, u32[]{:S(2)}, u32[]{:S(2)}) %collective-permute-start.4) | collective-permute-done | bytes 147488 | tf_op jit(solution)/shard_map/ppermute | solution.py:286
  15.0 3.0 %collective-permute-done.3 = f32[72,2,2,128]{3,2,1,0:T(2,128)S(1)} collective-permute-done((f32[72,2,2,128]{3,2,1,0:T(2,128)S(1)}, f32[72,2,2,128]{3,2,1,0:T(2,128)S(1)}, u32[]{:S(2)}, u32[]{:S(2)}) %collective-permute-start.3) | collective-permute-done | bytes 147488 | tf_op jit(solution)/shard_map/ppermute | solution.py:286
  20.7 3.3 %traces.2 = bf16[16,16,128]{2,1,0:T(8,128)(2,1)} custom-call(f32[72,2,8,128]{3,2,1,0:T(8,128)} %bitcast.55, f32[72,2,8,128]{3,2,1,0:T(8,128)} %copy-done.4, f32[72,2,8,128]{3,2,1,0:T(8,128)} %bitcast.59, f32[72,2,4,128]{3,2,1,0:T(4,128)} %pad_maximum_fusion.1.h, f32[6,2,8,128]{3,2,1,0:T(8,128)} %broadcast_in_dim.42.pm), custom_call_target="tpu_custom_call" | custom-call | flops 8000000 | bytes 2000000 | tf_op jit(solution)/shard_map/traces/pallas_call | solution.py:242
  24.0 1.7 %collective-permute-start.8 = (bf16[2,4,2,16,128]{4,3,2,1,0:T(8,128)(2,1)}, bf16[2,4,2,16,128]{4,3,2,1,0:T(8,128)(2,1)S(1)}, u32[]{:S(2)}, u32[]{:S(2)}) collective-permute-start(bf16[2,4,2,16,128]{4,3,2,1,0:T(8,128)(2,1)} %bitcast.69), channel_id=1, source_target_pairs={{2,0},{0,2},{3,1},{1,3},{6,4},{4,6},{7,5},{5,7},{10,8},{8,10},{11,... | collective-permute-start | bytes 196616 | tf_op jit(solution)/shard_map/ppermute | solution.py:286
  26.9 1.6 %collective-permute-done.8 = bf16[2,4,2,16,128]{4,3,2,1,0:T(8,128)(2,1)S(1)} collective-permute-done((bf16[2,4,2,16,128]{4,3,2,1,0:T(8,128)(2,1)}, bf16[2,4,2,16,128]{4,3,2,1,0:T(8,128)(2,1)S(1)}, u32[]{:S(2)}, u32[]{:S(2)}) %collective-permute-start.8) | collective-permute-done | bytes 65568 | tf_op jit(solution)/shard_map/ppermute | solution.py:286
  29.2 3.9 %collective-permute-start.10 = (bf16[2,1,4,16,128]{4,3,2,1,0:T(8,128)(2,1)S(1)}, bf16[2,1,4,16,128]{4,3,2,1,0:T(8,128)(2,1)S(1)}, u32[]{:S(2)}, u32[]{:S(2)}) collective-permute-start(bf16[2,1,4,16,128]{4,3,2,1,0:T(8,128)(2,1)S(1)} %get-tuple-element.16), channel_id=1, source_target_pairs={{4,0},{8,4},{12,8},{0,12},{5,1},{9,5},{13,9},{1,13},{6,2},{10,6},{... | collective-permute-start | bytes 98312 | tf_op jit(solution)/shard_map/ppermute | solution.py:286
  33.2 1.6 %collective-permute-start.6 = (f32[18,2,2,128]{3,2,1,0:T(2,128)S(1)}, f32[18,2,2,128]{3,2,1,0:T(2,128)S(1)}, u32[]{:S(2)}, u32[]{:S(2)}) collective-permute-start(f32[18,2,2,128]{3,2,1,0:T(2,128)S(1)} %pad_maximum_fusion.5), channel_id=1, source_target_pairs={{2,0},{0,2},{3,1},{1,3},{6,4},{4,6},{7,5},{5,7},{10,8},{8,10},{11,... | collective-permute-start | bytes 110600 | tf_op jit(solution)/shard_map/ppermute | solution.py:286
  34.7 4.1 %collective-permute-done.9 = bf16[2,1,4,16,128]{4,3,2,1,0:T(8,128)(2,1)S(1)} collective-permute-done((bf16[2,1,4,16,128]{4,3,2,1,0:T(8,128)(2,1)S(1)}, bf16[2,1,4,16,128]{4,3,2,1,0:T(8,128)(2,1)S(1)}, u32[]{:S(2)}, u32[]{:S(2)}) %collective-permute-start.9) | collective-permute-done | bytes 32800 | tf_op jit(solution)/shard_map/ppermute | solution.py:286
  44.6 5.1 %staples.2 = f32[24,18,8,128]{3,2,1,0:T(8,128)} custom-call(s32[4]{0:T(128)} %get-tuple-element.5.ya, f32[72,2,8,128]{3,2,1,0:T(8,128)} %bitcast.56, f32[72,2,8,128]{3,2,1,0:T(8,128)} %copy-done.4, f32[72,2,8,128]{3,2,1,0:T(8,128)} %bitcast.61, f32[72,2,8,128]{3,2,1,0:T(8,128)} %copy-done.11, f32[72,2,4,128]{3,2,1,0:T(4,128)} %pad_maximum_fusion.1.h, ...), custom_call_target="tpu_custom_call" | custom-call | flops 20000000 | bytes 5000000 | tf_op jit(solution)/shard_map/staples/pallas_call | solution.py:259
  51.1 5.2 %rotate.2 = f32[72,2,8,128]{3,2,1,0:T(8,128)} custom-call(s32[4]{0:T(128)} %get-tuple-element.5.ya, f32[72,2,8,128]{3,2,1,0:T(8,128)} %bitcast.57, f32[24,18,8,128]{3,2,1,0:T(8,128)} %staples.2, bf16[2,6,4,16,128]{4,3,2,1,0:T(8,128)(2,1)} %copy-done.9, bf16[2,6,4,16,128]{4,3,2,1,0:T(8,128)(2,1)} %copy-done.16, bf16[192,432]{1,0:T(8,128)(2,1)} %copy.21.w_in, ...), custom_call_target="tpu_custom_call" | custom-call | flops 300000000 | bytes 4000000 | tf_op jit(solution)/shard_map/rotate/pallas_call | solution.py:272
  56.2 1.3 %fusion.26 = (f32[72,2,4,128]{3,2,1,0:T(4,128)S(1)}, f32[72,2,4,128]{3,2,1,0:T(4,128)S(1)}) fusion(f32[72,2,8,128]{3,2,1,0:T(8,128)} %rotate.2), kind=kLoop, calls=%fused_computation.90 | loop fusion | bytes 1179648 | tf_op jit(solution)/shard_map/slice | solution.py:367
  57.7 8.9 %collective-permute-done.12 = f32[72,2,4,128]{3,2,1,0:T(4,128)S(1)} collective-permute-done((f32[72,2,4,128]{3,2,1,0:T(4,128)S(1)}, f32[72,2,4,128]{3,2,1,0:T(4,128)S(1)}, u32[]{:S(2)}, u32[]{:S(2)}) %collective-permute-start.12) | collective-permute-done | bytes 294944 | tf_op jit(solution)/shard_map/ppermute | solution.py:286
  66.8 1.6 %collective-permute-start.14 = (f32[72,2,4,2,128]{4,3,2,1,0:T(2,128)S(1)}, f32[72,2,4,2,128]{4,3,2,1,0:T(2,128)S(1)}, u32[]{:S(2)}, u32[]{:S(2)}) collective-permute-start(f32[72,2,4,2,128]{4,3,2,1,0:T(2,128)S(1)} %bitcast.58), channel_id=1, source_target_pairs={{2,0},{0,2},{3,1},{1,3},{6,4},{4,6},{7,5},{5,7},{10,8},{8,10},{11,... | collective-permute-start | bytes 1769480 | tf_op jit(solution)/shard_map/ppermute | solution.py:286
  69.6 2.1 %collective-permute-start.17 = (f32[72,2,2,128]{3,2,1,0:T(2,128)S(1)}, f32[72,2,2,128]{3,2,1,0:T(2,128)S(1)}, u32[]{:S(2)}, u32[]{:S(2)}) collective-permute-start(f32[72,2,2,128]{3,2,1,0:T(2,128)S(1)} %slice.231), channel_id=1, source_target_pairs={{4,0},{8,4},{12,8},{0,12},{5,1},{9,5},{13,9},{1,13},{6,2},{10,6},{... | collective-permute-start | bytes 442376 | tf_op jit(solution)/shard_map/ppermute | solution.py:286
  72.0 3.9 %collective-permute-done.17 = f32[72,2,2,128]{3,2,1,0:T(2,128)S(1)} collective-permute-done((f32[72,2,2,128]{3,2,1,0:T(2,128)S(1)}, f32[72,2,2,128]{3,2,1,0:T(2,128)S(1)}, u32[]{:S(2)}, u32[]{:S(2)}) %collective-permute-start.17) | collective-permute-done | bytes 147488 | tf_op jit(solution)/shard_map/ppermute | solution.py:286
  75.9 3.3 %collective-permute-done.16 = f32[72,2,2,128]{3,2,1,0:T(2,128)S(1)} collective-permute-done((f32[72,2,2,128]{3,2,1,0:T(2,128)S(1)}, f32[72,2,2,128]{3,2,1,0:T(2,128)S(1)}, u32[]{:S(2)}, u32[]{:S(2)}) %collective-permute-start.16) | collective-permute-done | bytes 147488 | tf_op jit(solution)/shard_map/ppermute | solution.py:286
  80.1 2.4 %collective-permute-done.14 = f32[72,2,4,2,128]{4,3,2,1,0:T(2,128)S(1)} collective-permute-done((f32[72,2,4,2,128]{4,3,2,1,0:T(2,128)S(1)}, f32[72,2,4,2,128]{4,3,2,1,0:T(2,128)S(1)}, u32[]{:S(2)}, u32[]{:S(2)}) %collective-permute-start.14) | collective-permute-done | bytes 589856 | tf_op jit(solution)/shard_map/ppermute | solution.py:286
  83.4 3.3 %traces.3 = bf16[16,16,128]{2,1,0:T(8,128)(2,1)} custom-call(f32[72,2,8,128]{3,2,1,0:T(8,128)} %copy-done.1, f32[72,2,8,128]{3,2,1,0:T(8,128)} %copy-done.6, f32[72,2,8,128]{3,2,1,0:T(8,128)} %bitcast.62, f32[72,2,4,128]{3,2,1,0:T(4,128)} %pad_maximum_fusion.2.h, f32[6,2,8,128]{3,2,1,0:T(8,128)} %broadcast_in_dim.48.pm), custom_call_target="tpu_custom_call" | custom-call | flops 8000000 | bytes 2000000 | tf_op jit(solution)/shard_map/traces/pallas_call | solution.py:242
  86.7 1.5 %collective-permute-start.21 = (bf16[2,4,2,16,128]{4,3,2,1,0:T(8,128)(2,1)}, bf16[2,4,2,16,128]{4,3,2,1,0:T(8,128)(2,1)S(1)}, u32[]{:S(2)}, u32[]{:S(2)}) collective-permute-start(bf16[2,4,2,16,128]{4,3,2,1,0:T(8,128)(2,1)} %bitcast.72), channel_id=1, source_target_pairs={{2,0},{0,2},{3,1},{1,3},{6,4},{4,6},{7,5},{5,7},{10,8},{8,10},{11,... | collective-permute-start | bytes 196616 | tf_op jit(solution)/shard_map/ppermute | solution.py:286
  88.2 2.9 %collective-permute-done.21 = bf16[2,4,2,16,128]{4,3,2,1,0:T(8,128)(2,1)S(1)} collective-permute-done((bf16[2,4,2,16,128]{4,3,2,1,0:T(8,128)(2,1)}, bf16[2,4,2,16,128]{4,3,2,1,0:T(8,128)(2,1)S(1)}, u32[]{:S(2)}, u32[]{:S(2)}) %collective-permute-start.21) | collective-permute-done | bytes 65568 | tf_op jit(solution)/shard_map/ppermute | solution.py:286
  91.9 2.1 %collective-permute-start.23 = (bf16[2,1,4,16,128]{4,3,2,1,0:T(8,128)(2,1)S(1)}, bf16[2,1,4,16,128]{4,3,2,1,0:T(8,128)(2,1)S(1)}, u32[]{:S(2)}, u32[]{:S(2)}) collective-permute-start(bf16[2,1,4,16,128]{4,3,2,1,0:T(8,128)(2,1)S(1)} %get-tuple-element.14), channel_id=1, source_target_pairs={{4,0},{8,4},{12,8},{0,12},{5,1},{9,5},{13,9},{1,13},{6,2},{10,6},{... | collective-permute-start | bytes 98312 | tf_op jit(solution)/shard_map/ppermute | solution.py:286
  94.0 1.8 %collective-permute-done.23 = bf16[2,1,4,16,128]{4,3,2,1,0:T(8,128)(2,1)S(1)} collective-permute-done((bf16[2,1,4,16,128]{4,3,2,1,0:T(8,128)(2,1)S(1)}, bf16[2,1,4,16,128]{4,3,2,1,0:T(8,128)(2,1)S(1)}, u32[]{:S(2)}, u32[]{:S(2)}) %collective-permute-start.23) | collective-permute-done | bytes 32800 | tf_op jit(solution)/shard_map/ppermute | solution.py:286
  95.9 3.9 %collective-permute-done.22 = bf16[2,1,4,16,128]{4,3,2,1,0:T(8,128)(2,1)S(1)} collective-permute-done((bf16[2,1,4,16,128]{4,3,2,1,0:T(8,128)(2,1)S(1)}, bf16[2,1,4,16,128]{4,3,2,1,0:T(8,128)(2,1)S(1)}, u32[]{:S(2)}, u32[]{:S(2)}) %collective-permute-start.22) | collective-permute-done | bytes 32800 | tf_op jit(solution)/shard_map/ppermute | solution.py:286
  100.8 1.6 %collective-permute-start.19 = (f32[18,2,2,128]{3,2,1,0:T(2,128)S(1)}, f32[18,2,2,128]{3,2,1,0:T(2,128)S(1)}, u32[]{:S(2)}, u32[]{:S(2)}) collective-permute-start(f32[18,2,2,128]{3,2,1,0:T(2,128)S(1)} %pad_maximum_fusion.6), channel_id=1, source_target_pairs={{2,0},{0,2},{3,1},{1,3},{6,4},{4,6},{7,5},{5,7},{10,8},{8,10},{11,... | collective-permute-start | bytes 110600 | tf_op jit(solution)/shard_map/ppermute | solution.py:286
  102.4 2.4 %collective-permute-done.19.co = f32[18,2,2,128]{3,2,1,0:T(2,128)S(1)} collective-permute-done((f32[18,2,2,128]{3,2,1,0:T(2,128)S(1)}, f32[18,2,2,128]{3,2,1,0:T(2,128)S(1)}, u32[]{:S(2)}, u32[]{:S(2)}) %collective-permute-start.19) | collective-permute-done | bytes 36896 | tf_op jit(solution)/shard_map/ppermute | solution.py:286
  107.2 5.1 %staples.3 = f32[24,18,8,128]{3,2,1,0:T(8,128)} custom-call(s32[4]{0:T(128)} %get-tuple-element.6.ya, f32[72,2,8,128]{3,2,1,0:T(8,128)} %copy-done.1, f32[72,2,8,128]{3,2,1,0:T(8,128)} %copy-done.6, f32[72,2,8,128]{3,2,1,0:T(8,128)} %bitcast.64, f32[72,2,8,128]{3,2,1,0:T(8,128)} %copy-done.10, f32[72,2,4,128]{3,2,1,0:T(4,128)} %pad_maximum_fusion.2.h, ...), custom_call_target="tpu_custom_call" | custom-call | flops 20000000 | bytes 5000000 | tf_op jit(solution)/shard_map/staples/pallas_call | solution.py:259
  113.7 5.2 %rotate.3 = f32[72,2,8,128]{3,2,1,0:T(8,128)} custom-call(s32[4]{0:T(128)} %get-tuple-element.6.ya, f32[72,2,8,128]{3,2,1,0:T(8,128)} %copy-done.1, f32[24,18,8,128]{3,2,1,0:T(8,128)} %staples.3, bf16[2,6,4,16,128]{4,3,2,1,0:T(8,128)(2,1)} %copy-done.8, bf16[2,6,4,16,128]{4,3,2,1,0:T(8,128)(2,1)} %copy-done.15, bf16[192,432]{1,0:T(8,128)(2,1)} %copy.25.w_in, ...), custom_call_target="tpu_custom_call" | custom-call | flops 300000000 | bytes 4000000 | tf_op jit(solution)/shard_map/rotate/pallas_call | solution.py:272
  118.8 2.2 %copy.39 = f32[4,18,2,4,2,128]{5,2,3,4,1,0:T(2,128)} copy(f32[4,18,2,4,2,128]{5,4,3,2,1,0:T(2,128)} %bitcast.65) | data formatting | bytes 1179648 | tf_op jit(solution)/shard_map/reshape | solution.py:380
  (132 shorter events, 24.2 us)
Async XLA Ops:
  0.0 11.8 %copy-start.22 = (bf16[2,64,24]{1,2,0:T(8,128)(2,1)S(1)}, bf16[2,64,24]{1,2,0:T(8,128)(2,1)}, u32[]{:S(2)}) copy-start(bf16[2,64,24]{1,2,0:T(8,128)(2,1)} %param.10) | copy-start | bytes 18436
  0.0 12.7 %copy-start.23 = (f32[2,64]{1,0:T(2,128)S(1)}, f32[2,64]{1,0:T(2,128)}, u32[]{:S(2)}) copy-start(f32[2,64]{1,0:T(2,128)} %param.9) | copy-start | bytes 1540
  1.4 19.3 %copy-start = (f32[4,18,2,4,2,128]{5,4,3,2,1,0:T(2,128)}, f32[4,18,2,4,2,128]{5,4,3,2,1,0:T(2,128)S(1)}, u32[]{:S(2)}) copy-start(f32[4,18,2,4,2,128]{5,4,3,2,1,0:T(2,128)S(1)} %copy.15) | copy-start | bytes 1769476
  1.4 17.5 %collective-permute-start = (f32[72,2,8,128]{3,2,1,0:T(8,128)S(1)}, f32[72,2,8,128]{3,2,1,0:T(8,128)S(1)}, u32[]{:S(2)}, u32[]{:S(2)}) collective-permute-start(f32[72,2,8,128]{3,2,1,0:T(8,128)S(1)} %bitcast.53), channel_id=1, source_target_pairs={{1,0},{0,1},{3,2},{2,3},{5,4},{4,5},{7,6},{6,7},{9,8},{8,9},{11,10... | collective-permute-start | bytes 1769480 | tf_op jit(solution)/shard_map/ppermute | solution.py:286
  3.3 16.6 %collective-permute-start.1 = (f32[72,2,4,2,128]{4,3,2,1,0:T(2,128)S(1)}, f32[72,2,4,2,128]{4,3,2,1,0:T(2,128)S(1)}, u32[]{:S(2)}, u32[]{:S(2)}) collective-permute-start(f32[72,2,4,2,128]{4,3,2,1,0:T(2,128)S(1)} %copy.16), channel_id=1, source_target_pairs={{2,0},{0,2},{3,1},{1,3},{6,4},{4,6},{7,5},{5,7},{10,8},{8,10},{11,... | collective-permute-start | bytes 1769480 | tf_op jit(solution)/shard_map/ppermute | solution.py:286
  6.8 18.9 %copy-start.24 = (f32[2,24]{1,0:T(2,128)S(1)}, f32[2,24]{1,0:T(2,128)}, u32[]{:S(2)}) copy-start(f32[2,24]{1,0:T(2,128)} %param.11) | copy-start | bytes 580
  6.8 18.9 %copy-start.12 = (bf16[2,81,12,64]{1,3,2,0:T(8,128)(2,1)S(1)}, bf16[2,81,12,64]{1,3,2,0:T(8,128)(2,1)}, u32[]{:S(2)}) copy-start(bf16[2,81,12,64]{1,3,2,0:T(8,128)(2,1)} %param.8) | copy-start | bytes 746500
  6.8 8.2 %collective-permute-start.4 = (f32[72,2,2,128]{3,2,1,0:T(2,128)}, f32[72,2,2,128]{3,2,1,0:T(2,128)S(1)}, u32[]{:S(2)}, u32[]{:S(2)}) collective-permute-start(f32[72,2,2,128]{3,2,1,0:T(2,128)} %get-tuple-element.10), channel_id=1, source_target_pairs={{4,0},{8,4},{12,8},{0,12},{5,1},{9,5},{13,9},{1,13},{6,2},{10,6},{... | collective-permute-start | bytes 442376 | tf_op jit(solution)/shard_map/ppermute | solution.py:286
  10.4 7.6 %collective-permute-start.3 = (f32[72,2,2,128]{3,2,1,0:T(2,128)S(1)}, f32[72,2,2,128]{3,2,1,0:T(2,128)S(1)}, u32[]{:S(2)}, u32[]{:S(2)}) collective-permute-start(f32[72,2,2,128]{3,2,1,0:T(2,128)S(1)} %get-tuple-element.9), channel_id=1, source_target_pairs={{12,0},{0,4},{4,8},{8,12},{13,1},{1,5},{5,9},{9,13},{14,2},{2,6},{... | collective-permute-start | bytes 442376 | tf_op jit(solution)/shard_map/ppermute | solution.py:286
  24.0 4.5 %collective-permute-start.8 = (bf16[2,4,2,16,128]{4,3,2,1,0:T(8,128)(2,1)}, bf16[2,4,2,16,128]{4,3,2,1,0:T(8,128)(2,1)S(1)}, u32[]{:S(2)}, u32[]{:S(2)}) collective-permute-start(bf16[2,4,2,16,128]{4,3,2,1,0:T(8,128)(2,1)} %bitcast.69), channel_id=1, source_target_pairs={{2,0},{0,2},{3,1},{1,3},{6,4},{4,6},{7,5},{5,7},{10,8},{8,10},{11,... | collective-permute-start | bytes 196616 | tf_op jit(solution)/shard_map/ppermute | solution.py:286
  26.2 17.5 %collective-permute-start.5 = (f32[72,2,4,128]{3,2,1,0:T(4,128)S(1)}, f32[72,2,4,128]{3,2,1,0:T(4,128)S(1)}, u32[]{:S(2)}, u32[]{:S(2)}) collective-permute-start(f32[72,2,4,128]{3,2,1,0:T(4,128)S(1)} %copy-done.2), channel_id=1, source_target_pairs={{1,0},{0,1},{3,2},{2,3},{5,4},{4,5},{7,6},{6,7},{9,8},{8,9},{11,10... | collective-permute-start | bytes 884744 | tf_op jit(solution)/shard_map/ppermute | solution.py:286
  26.3 17.4 %collective-permute-start.2 = (f32[72,2,8,128]{3,2,1,0:T(8,128)}, f32[72,2,8,128]{3,2,1,0:T(8,128)S(1)}, u32[]{:S(2)}, u32[]{:S(2)}) collective-permute-start(f32[72,2,8,128]{3,2,1,0:T(8,128)} %bitcast.60), channel_id=1, source_target_pairs={{1,0},{0,1},{3,2},{2,3},{5,4},{4,5},{7,6},{6,7},{9,8},{8,9},{11,10... | collective-permute-start | bytes 1769480 | tf_op jit(solution)/shard_map/ppermute | solution.py:286
  29.2 5.5 %collective-permute-start.10 = (bf16[2,1,4,16,128]{4,3,2,1,0:T(8,128)(2,1)S(1)}, bf16[2,1,4,16,128]{4,3,2,1,0:T(8,128)(2,1)S(1)}, u32[]{:S(2)}, u32[]{:S(2)}) collective-permute-start(bf16[2,1,4,16,128]{4,3,2,1,0:T(8,128)(2,1)S(1)} %get-tuple-element.16), channel_id=1, source_target_pairs={{4,0},{8,4},{12,8},{0,12},{5,1},{9,5},{13,9},{1,13},{6,2},{10,6},{... | collective-permute-start | bytes 98312 | tf_op jit(solution)/shard_map/ppermute | solution.py:286
  33.1 5.7 %collective-permute-start.9 = (bf16[2,1,4,16,128]{4,3,2,1,0:T(8,128)(2,1)S(1)}, bf16[2,1,4,16,128]{4,3,2,1,0:T(8,128)(2,1)S(1)}, u32[]{:S(2)}, u32[]{:S(2)}) collective-permute-start(bf16[2,1,4,16,128]{4,3,2,1,0:T(8,128)(2,1)S(1)} %get-tuple-element.15), channel_id=1, source_target_pairs={{12,0},{0,4},{4,8},{8,12},{13,1},{1,5},{5,9},{9,13},{14,2},{2,6},{... | collective-permute-start | bytes 98312 | tf_op jit(solution)/shard_map/ppermute | solution.py:286
  33.2 7.7 %collective-permute-start.6 = (f32[18,2,2,128]{3,2,1,0:T(2,128)S(1)}, f32[18,2,2,128]{3,2,1,0:T(2,128)S(1)}, u32[]{:S(2)}, u32[]{:S(2)}) collective-permute-start(f32[18,2,2,128]{3,2,1,0:T(2,128)S(1)} %pad_maximum_fusion.5), channel_id=1, source_target_pairs={{2,0},{0,2},{3,1},{1,3},{6,4},{4,6},{7,5},{5,7},{10,8},{8,10},{11,... | collective-permute-start | bytes 110600 | tf_op jit(solution)/shard_map/ppermute | solution.py:286
  39.7 10.0 %collective-permute-start.11 = (bf16[2,6,4,16,128]{4,3,2,1,0:T(8,128)(2,1)S(1)}, bf16[2,6,4,16,128]{4,3,2,1,0:T(8,128)(2,1)S(1)}, u32[]{:S(2)}, u32[]{:S(2)}) collective-permute-start(bf16[2,6,4,16,128]{4,3,2,1,0:T(8,128)(2,1)S(1)} %pad_maximum_fusion.3.f), channel_id=1, source_target_pairs={{1,0},{0,1},{3,2},{2,3},{5,4},{4,5},{7,6},{6,7},{9,8},{8,9},{11,10... | collective-permute-start | bytes 589832 | tf_op jit(solution)/shard_map/ppermute | solution.py:286
  40.9 2.8 %collective-permute-start.7 = (f32[18,2,2,128]{3,2,1,0:T(2,128)S(1)}, f32[18,2,2,128]{3,2,1,0:T(2,128)S(1)}, u32[]{:S(2)}, u32[]{:S(2)}) collective-permute-start(f32[18,2,2,128]{3,2,1,0:T(2,128)S(1)} %collective-permute-done.6.co), channel_id=1, source_target_pairs={{1,0},{0,1},{3,2},{2,3},{5,4},{4,5},{7,6},{6,7},{9,8},{8,9},{11,10... | collective-permute-start | bytes 110600 | tf_op jit(solution)/shard_map/ppermute | solution.py:286
  57.6 9.0 %collective-permute-start.12 = (f32[72,2,4,128]{3,2,1,0:T(4,128)S(1)}, f32[72,2,4,128]{3,2,1,0:T(4,128)S(1)}, u32[]{:S(2)}, u32[]{:S(2)}) collective-permute-start(f32[72,2,4,128]{3,2,1,0:T(4,128)S(1)} %get-tuple-element.8), channel_id=1, source_target_pairs={{4,0},{8,4},{12,8},{0,12},{5,1},{9,5},{13,9},{1,13},{6,2},{10,6},{... | collective-permute-start | bytes 884744 | tf_op jit(solution)/shard_map/ppermute | solution.py:286
  66.7 16.6 %copy-start.1 = (f32[72,2,8,128]{3,2,1,0:T(8,128)}, f32[72,2,8,128]{3,2,1,0:T(8,128)S(1)}, u32[]{:S(2)}) copy-start(f32[72,2,8,128]{3,2,1,0:T(8,128)S(1)} %pad_maximum_fusion.own) | copy-start | bytes 1769476
  66.7 13.4 %collective-permute-start.13 = (f32[72,2,8,128]{3,2,1,0:T(8,128)S(1)}, f32[72,2,8,128]{3,2,1,0:T(8,128)S(1)}, u32[]{:S(2)}, u32[]{:S(2)}) collective-permute-start(f32[72,2,8,128]{3,2,1,0:T(8,128)S(1)} %pad_maximum_fusion.own), channel_id=1, source_target_pairs={{1,0},{0,1},{3,2},{2,3},{5,4},{4,5},{7,6},{6,7},{9,8},{8,9},{11,10... | collective-permute-start | bytes 1769480 | tf_op jit(solution)/shard_map/ppermute | solution.py:286
  66.8 15.7 %collective-permute-start.14 = (f32[72,2,4,2,128]{4,3,2,1,0:T(2,128)S(1)}, f32[72,2,4,2,128]{4,3,2,1,0:T(2,128)S(1)}, u32[]{:S(2)}, u32[]{:S(2)}) collective-permute-start(f32[72,2,4,2,128]{4,3,2,1,0:T(2,128)S(1)} %bitcast.58), channel_id=1, source_target_pairs={{2,0},{0,2},{3,1},{1,3},{6,4},{4,6},{7,5},{5,7},{10,8},{8,10},{11,... | collective-permute-start | bytes 1769480 | tf_op jit(solution)/shard_map/ppermute | solution.py:286
  69.6 6.4 %collective-permute-start.17 = (f32[72,2,2,128]{3,2,1,0:T(2,128)S(1)}, f32[72,2,2,128]{3,2,1,0:T(2,128)S(1)}, u32[]{:S(2)}, u32[]{:S(2)}) collective-permute-start(f32[72,2,2,128]{3,2,1,0:T(2,128)S(1)} %slice.231), channel_id=1, source_target_pairs={{4,0},{8,4},{12,8},{0,12},{5,1},{9,5},{13,9},{1,13},{6,2},{10,6},{... | collective-permute-start | bytes 442376 | tf_op jit(solution)/shard_map/ppermute | solution.py:286
  71.8 7.5 %collective-permute-start.16 = (f32[72,2,2,128]{3,2,1,0:T(2,128)S(1)}, f32[72,2,2,128]{3,2,1,0:T(2,128)S(1)}, u32[]{:S(2)}, u32[]{:S(2)}) collective-permute-start(f32[72,2,2,128]{3,2,1,0:T(2,128)S(1)} %slice.230), channel_id=1, source_target_pairs={{12,0},{0,4},{4,8},{8,12},{13,1},{1,5},{5,9},{9,13},{14,2},{2,6},{... | collective-permute-start | bytes 442376 | tf_op jit(solution)/shard_map/ppermute | solution.py:286
  80.1 13.9 %copy-start.3 = (f32[72,2,4,128]{3,2,1,0:T(4,128)S(1)}, f32[72,2,4,128]{3,2,1,0:T(4,128)}, u32[]{:S(2)}) copy-start(f32[72,2,4,128]{3,2,1,0:T(4,128)} %pad_maximum_fusion.2.h) | copy-start | bytes 884740
  86.7 4.5 %collective-permute-start.21 = (bf16[2,4,2,16,128]{4,3,2,1,0:T(8,128)(2,1)}, bf16[2,4,2,16,128]{4,3,2,1,0:T(8,128)(2,1)S(1)}, u32[]{:S(2)}, u32[]{:S(2)}) collective-permute-start(bf16[2,4,2,16,128]{4,3,2,1,0:T(8,128)(2,1)} %bitcast.72), channel_id=1, source_target_pairs={{2,0},{0,2},{3,1},{1,3},{6,4},{4,6},{7,5},{5,7},{10,8},{8,10},{11,... | collective-permute-start | bytes 196616 | tf_op jit(solution)/shard_map/ppermute | solution.py:286
  88.2 18.1 %collective-permute-start.15 = (f32[72,2,8,128]{3,2,1,0:T(8,128)}, f32[72,2,8,128]{3,2,1,0:T(8,128)S(1)}, u32[]{:S(2)}, u32[]{:S(2)}) collective-permute-start(f32[72,2,8,128]{3,2,1,0:T(8,128)} %bitcast.63), channel_id=1, source_target_pairs={{1,0},{0,1},{3,2},{2,3},{5,4},{4,5},{7,6},{6,7},{9,8},{8,9},{11,10... | collective-permute-start | bytes 1769480 | tf_op jit(solution)/shard_map/ppermute | solution.py:286
  91.9 4.0 %collective-permute-start.23 = (bf16[2,1,4,16,128]{4,3,2,1,0:T(8,128)(2,1)S(1)}, bf16[2,1,4,16,128]{4,3,2,1,0:T(8,128)(2,1)S(1)}, u32[]{:S(2)}, u32[]{:S(2)}) collective-permute-start(bf16[2,1,4,16,128]{4,3,2,1,0:T(8,128)(2,1)S(1)} %get-tuple-element.14), channel_id=1, source_target_pairs={{4,0},{8,4},{12,8},{0,12},{5,1},{9,5},{13,9},{1,13},{6,2},{10,6},{... | collective-permute-start | bytes 98312 | tf_op jit(solution)/shard_map/ppermute | solution.py:286
  94.0 5.7 %collective-permute-start.22 = (bf16[2,1,4,16,128]{4,3,2,1,0:T(8,128)(2,1)S(1)}, bf16[2,1,4,16,128]{4,3,2,1,0:T(8,128)(2,1)S(1)}, u32[]{:S(2)}, u32[]{:S(2)}) collective-permute-start(bf16[2,1,4,16,128]{4,3,2,1,0:T(8,128)(2,1)S(1)} %get-tuple-element.13), channel_id=1, source_target_pairs={{12,0},{0,4},{4,8},{8,12},{13,1},{1,5},{5,9},{9,13},{14,2},{2,6},{... | collective-permute-start | bytes 98312 | tf_op jit(solution)/shard_map/ppermute | solution.py:286
  94.0 12.2 %collective-permute-start.18 = (f32[72,2,4,128]{3,2,1,0:T(4,128)S(1)}, f32[72,2,4,128]{3,2,1,0:T(4,128)S(1)}, u32[]{:S(2)}, u32[]{:S(2)}) collective-permute-start(f32[72,2,4,128]{3,2,1,0:T(4,128)S(1)} %copy-done.3), channel_id=1, source_target_pairs={{1,0},{0,1},{3,2},{2,3},{5,4},{4,5},{7,6},{6,7},{9,8},{8,9},{11,10... | collective-permute-start | bytes 884744 | tf_op jit(solution)/shard_map/ppermute | solution.py:286
  100.6 11.7 %collective-permute-start.24 = (bf16[2,6,4,16,128]{4,3,2,1,0:T(8,128)(2,1)S(1)}, bf16[2,6,4,16,128]{4,3,2,1,0:T(8,128)(2,1)S(1)}, u32[]{:S(2)}, u32[]{:S(2)}) collective-permute-start(bf16[2,6,4,16,128]{4,3,2,1,0:T(8,128)(2,1)S(1)} %pad_maximum_fusion.4.f), channel_id=1, source_target_pairs={{1,0},{0,1},{3,2},{2,3},{5,4},{4,5},{7,6},{6,7},{9,8},{8,9},{11,10... | collective-permute-start | bytes 589832 | tf_op jit(solution)/shard_map/ppermute | solution.py:286
  100.8 4.0 %collective-permute-start.19 = (f32[18,2,2,128]{3,2,1,0:T(2,128)S(1)}, f32[18,2,2,128]{3,2,1,0:T(2,128)S(1)}, u32[]{:S(2)}, u32[]{:S(2)}) collective-permute-start(f32[18,2,2,128]{3,2,1,0:T(2,128)S(1)} %pad_maximum_fusion.6), channel_id=1, source_target_pairs={{2,0},{0,2},{3,1},{1,3},{6,4},{4,6},{7,5},{5,7},{10,8},{8,10},{11,... | collective-permute-start | bytes 110600 | tf_op jit(solution)/shard_map/ppermute | solution.py:286
  104.8 1.4 %collective-permute-start.20 = (f32[18,2,2,128]{3,2,1,0:T(2,128)S(1)}, f32[18,2,2,128]{3,2,1,0:T(2,128)S(1)}, u32[]{:S(2)}, u32[]{:S(2)}) collective-permute-start(f32[18,2,2,128]{3,2,1,0:T(2,128)S(1)} %collective-permute-done.19.co), channel_id=1, source_target_pairs={{1,0},{0,1},{3,2},{2,3},{5,4},{4,5},{7,6},{6,7},{9,8},{8,9},{11,10... | collective-permute-start | bytes 110600 | tf_op jit(solution)/shard_map/ppermute | solution.py:286
  (18 other events, 51.0 us)
where the time goes:
time: 122 us; the launch traced here: 121 us
  waiting for transfers between devices  41.6 us (34%)
  Pallas kernels  27 us (22%)
  starting transfers between devices  24.7 us (20%)
  local copies, waits for them, and re-layouts  20.7 us (17%)
  other arithmetic  5.82 us (5%)
    ppermute x25, waiting for transfers between devices, step(): lax.ppermute(value, axis, [((i + by) % count, i) for i in range(count)])  41.6 us
    ppermute x25, starting transfers between devices, step(): lax.ppermute(value, axis, [((i + by) % count, i) for i in range(count)])  24.7 us
    pallas_call x2, Pallas kernels, run_final(): pl.pallas_call(final_kernel, out_shape=jax.ShapeDtypeStruct((72, 2, 8, 12...  10.3 us
    pallas_call x2, Pallas kernels, run_staples(): pl.pallas_call(staple_kernel, out_shape=jax.ShapeDtypeStruct((24, 18, 8,...  10.2 us
    pallas_call x2, Pallas kernels, run_traces(): pl.pallas_call(trace_kernel, out_shape=jax.ShapeDtypeStruct((16, 16, 128)...  6.5 us
  transfers between devices with their start and end apart: 25, of which 13 were waited for; matrix products, arithmetic and copies ran while one was open for 13% of the time, Pallas kernels for 8%

commit v1 on v0

--- a/solution.py
+++ b/solution.py
@@ -9,7 +9,6 @@
 F32 = jnp.float32
 BF16 = jnp.bfloat16
 BASE = 8
-LIMIT = 56 * 1024 * 1024
 
 
 def mm(a, b, a_dag=False, b_dag=False):
@@ -57,7 +56,7 @@
     return pltpu.roll(value, (-step) % value.shape[-1], value.ndim - 1)
 
 
-def trace_kernel(own, own_s, tp, h, pm, out, v0, vup, trs):
+def trace_kernel(ya, own, own_s, tp, h, out, v0, vup, trs):
     even = lax.broadcasted_iota(jnp.int32, (8, 128), 0) % 2 == 0
 
     def prep(i, _):
@@ -72,8 +71,12 @@
 
     lax.fori_loop(0, 72, prep, 0, unroll=4)
     trs[192:256] = jnp.zeros((64, 128), F32)
+    row_of = lax.broadcasted_iota(jnp.int32, (8, 128), 0)
+    leaves = (row_of % 2, jnp.where(row_of >= 6, 1, 0), 1, 0)
 
     def at_y(y, _):
+        active = [jnp.where(ya[m] == y, 1, 0) for m in range(4)]
+
         def look(d, step):
             if step == 0:
                 parts = [vup[18 * d + c, y] for c in range(18)]
@@ -96,10 +99,11 @@
                 q = a[9 + k] * b[k] - a[k] * b[9 + k]
                 re = r if re is None else re + r
                 im = q if im is None else im + q
-            keep = pm[p, y] * (1.0 / 3.0)
+            moved = (active[n] ^ leaves[m]) | (active[m] ^ leaves[n]) | active[m] | active[n]
+            frozen = jnp.broadcast_to(moved, (8, 128)) == 0
             row = pl.multiple_of(y * 8, 8)
-            trs[pl.ds((2 * p) * 16 + row, 8)] = re * keep
-            trs[pl.ds((2 * p + 1) * 16 + row, 8)] = im * keep
+            trs[pl.ds((2 * p) * 16 + row, 8)] = jnp.where(frozen, re * (1.0 / 3.0), 0.0)
+            trs[pl.ds((2 * p + 1) * 16 + row, 8)] = jnp.where(frozen, im * (1.0 / 3.0), 0.0)
         return 0
 
     lax.fori_loop(0, 2, at_y, 0)
@@ -160,6 +164,48 @@
             down = mm(mm(look(m, back_n), look(n, corner_mn)), look(n, back_n), a_dag=True)
             for c, value in enumerate(flat(down)):
                 out[6 * m + 2 * j + 1, c] = value
+
+
+def unpack_kernel(x, own, first, last):
+    def body(i, _):
+        for y in range(2):
+            for t in range(2):
+                own[i, y, pl.ds(t, 4, stride=2)] = x[i, pl.ds(8 * t + y, 4, stride=2)]
+                first[i, y, t : t + 1] = x[i, 8 * t + y : 8 * t + y + 1]
+                last[i, y, t : t + 1] = x[i, 8 * t + 6 + y : 8 * t + 7 + y]
+        return 0
+
+    lax.fori_loop(0, 72, body, 0, unroll=8)
+
+
+def weights_kernel(conv_in, bias_in, conv_out, bias_out, *refs):
+    outs, big, small = refs[:8], refs[8], refs[9]
+    big[...] = jnp.zeros_like(big)
+    small[...] = jnp.zeros_like(small)
+    for layer in range(2):
+        w_in, b_in, w_out, b_out = outs[4 * layer : 4 * layer + 4]
+        for k in range(27):
+            taps = [conv_in[layer, 3 * k + z].astype(F32) for z in range(3)]
+            big[16 * k : 16 * k + 12, 0:192] = jnp.concatenate(taps, axis=1)
+        w_in[...] = jnp.transpose(big[...])[0:192, 0:432].astype(BF16)
+        small[0:64, 0:24] = conv_out[layer].astype(F32)
+        w_out[...] = jnp.transpose(small[...])[0:24, 0:64].astype(BF16)
+        small[:, 0:64] = jnp.broadcast_to(bias_in[layer : layer + 1], (128, 64))
+        b_in[...] = jnp.transpose(small[...])[0:64]
+        small[:, 0:24] = jnp.broadcast_to(bias_out[layer : layer + 1], (128, 24))
+        b_out[...] = jnp.transpose(small[...])[0:24]
+
+
+def last_kernel(ya, own, staples, f, f_s, w_in, b_in, w_out, b_out, packed, out, wts):
+    final_kernel(ya, own, staples, f, f_s, w_in, b_in, w_out, b_out, out, wts)
+
+    def body(i, _):
+        for y in range(2):
+            for t in range(2):
+                packed[i, pl.ds(8 * t + y, 4, stride=2)] = out[i, y, pl.ds(t, 4, stride=2)]
+        return 0
+
+    lax.fori_loop(0, 72, body, 0, unroll=8)
 
 
 def final_kernel(ya, own, staples, f, f_s, w_in, b_in, w_out, b_out, out, wts):
@@ -235,24 +281,54 @@
 
 VM = pl.BlockSpec(memory_space=pltpu.VMEM)
 SM = pl.BlockSpec(memory_space=pltpu.SMEM)
-PARAMS = pltpu.CompilerParams(vmem_limit_bytes=LIMIT)
-
-
-def run_traces(own, own_s, tp, h, pm):
+
+
+def params(mib):
+    return pltpu.CompilerParams(vmem_limit_bytes=mib * 1024 * 1024)
+
+
+def run_weights(conv_in, bias_in, conv_out, bias_out):
+    shapes = [((192, 432), BF16), ((64, 128), F32), ((24, 64), BF16), ((24, 128), F32)]
+    return pl.pallas_call(
+        weights_kernel,
+        out_shape=[jax.ShapeDtypeStruct(*shape) for shape in shapes * 2],
+        in_specs=[VM] * 4,
+        out_specs=[VM] * 8,
+        scratch_shapes=[pltpu.VMEM((512, 256), F32), pltpu.VMEM((128, 128), F32)],
+        compiler_params=params(8),
+        cost_estimate=pl.CostEstimate(flops=0, bytes_accessed=6_000_000, transcendentals=0),
+        name="weights",
+    )(conv_in, bias_in, conv_out, bias_out)
+
+
+def run_unpack(x):
+    rows = jax.ShapeDtypeStruct((72, 2, 2, 128), F32)
+    return pl.pallas_call(
+        unpack_kernel,
+        out_shape=[jax.ShapeDtypeStruct((72, 2, 8, 128), F32), rows, rows],
+        in_specs=[VM],
+        out_specs=[VM] * 3,
+        compiler_params=params(8),
+        cost_estimate=pl.CostEstimate(flops=0, bytes_accessed=2_000_000, transcendentals=0),
+        name="unpack",
+    )(x)
+
+
+def run_traces(ya, own, own_s, tp, h):
     return pl.pallas_call(
         trace_kernel,
         out_shape=jax.ShapeDtypeStruct((16, 16, 128), BF16),
-        in_specs=[VM] * 5,
+        in_specs=[SM] + [VM] * 4,
         out_specs=VM,
         scratch_shapes=[
             pltpu.VMEM((72, 3, 24, 128), F32),
             pltpu.VMEM((72, 2, 8, 128), F32),
             pltpu.VMEM((256, 128), F32),
         ],
-        compiler_params=PARAMS,
+        compiler_params=params(16),
         cost_estimate=pl.CostEstimate(flops=8_000_000, bytes_accessed=2_000_000, transcendentals=0),
         name="traces",
-    )(own, own_s, tp, h, pm)
+    )(ya, own, own_s, tp, h)
 
 
 def run_staples(ya, own, own_s, tp, tp_s, h, h_s, co, co_s):
@@ -262,20 +338,21 @@
         in_specs=[SM] + [VM] * 8,
         out_specs=VM,
         scratch_shapes=[pltpu.VMEM((72, 4, 24, 128), F32)] * 3,
-        compiler_params=PARAMS,
-        cost_estimate=pl.CostEstimate(flops=20_000_000, bytes_accessed=5_000_000, transcendentals=0),
+        compiler_params=params(22),
+        cost_estimate=pl.CostEstimate(flops=20_000_000, bytes_accessed=16_000_000, transcendentals=0),
         name="staples",
     )(ya, own, own_s, tp, tp_s, h, h_s, co, co_s)
 
 
-def run_final(ya, own, staples, f, f_s, w_in, b_in, w_out, b_out):
+def run_final(ya, own, staples, f, f_s, w_in, b_in, w_out, b_out, last):
+    weights = [pltpu.VMEM((2, 192, 128), F32)]
     return pl.pallas_call(
-        final_kernel,
-        out_shape=jax.ShapeDtypeStruct((72, 2, 8, 128), F32),
+        last_kernel if last else final_kernel,
+        out_shape=jax.ShapeDtypeStruct((72, 16, 128) if last else (72, 2, 8, 128), F32),
         in_specs=[SM] + [VM] * 8,
         out_specs=VM,
-        scratch_shapes=[pltpu.VMEM((2, 192, 128), F32)],
-        compiler_params=PARAMS,
+        scratch_shapes=([pltpu.VMEM((72, 2, 8, 128), F32)] if last else []) + weights,
+        compiler_params=params(14),
         cost_estimate=pl.CostEstimate(flops=300_000_000, bytes_accessed=4_000_000, transcendentals=131072),
         name="rotate",
     )(ya, own, staples, f, f_s, w_in, b_in, w_out, b_out)
@@ -294,91 +371,77 @@
     return jnp.concatenate([up, down], axis=dim)
 
 
-def exchange(own):
+def diagonal(value, x_by, t_by):
+    n_x, n_t = lax.axis_size("space"), lax.axis_size("tm")
+    pairs = [
+        ((i + x_by) % n_x * n_t + (k + t_by) % n_t, i * n_t + k)
+        for i in range(n_x)
+        for k in range(n_t)
+    ]
+    return lax.ppermute(value, ("space", "tm"), pairs)
+
+
+def exchange(own, first, last):
     tp = other_time(own.reshape(72, 2, 4, 2, 128), 3).reshape(own.shape)
-    left = step(own[:, :, 6:8], "space", -1)
-    right = step(own[:, :, 0:2], "space", 1)
-    h = jnp.concatenate([left, right], axis=2)
-    mixed = jnp.concatenate([left[18:36, :, 0:1], right[0:18, :, 1:2]], axis=2)
-    co = other_time(mixed, 2)
-    return tp, h, co
-
-
-def traces_rim(tr):
+    left = step(last, "space", -1)
+    right = step(first, "space", 1)
+    co_left = diagonal(last[18:36, :, 0:1], -1, 1)
+    co_right = diagonal(first[0:18, :, 1:2], 1, -1)
+    return tp, left, right, co_left, co_right
+
+
+def traces_rim(tr, meanwhile):
     tp = other_time(tr, 2)
     full = jnp.concatenate([tp[:, :, 1:2], tr, tp[:, :, 0:1]], axis=2)
     left = step(full[:, 3:4], "space", -1)
     right = step(full[:, 0:1], "space", 1)
-    return jnp.concatenate([left, full, right], axis=1)
-
-
-def active_window(active_blocks):
-    t_len, x_len, y_len = 2, 4, 2
-
-    def blocks(axis, length, lo, hi):
-        total = lax.axis_size(axis) * length
-        at = (lax.axis_index(axis) * length + jnp.arange(lo, hi, dtype=jnp.int32)) % total
-        return at // length, at
-
-    t_block, _ = blocks("tm", t_len, -1, 3)
-    x_block, _ = blocks("space", x_len, -1, 5)
-    _, y_at = blocks("sub", y_len, -1, 3)
-    y_block = 2 * y_at // y_len
-    table = (active_blocks > 0).astype(F32)
-
-    def pick(table, at, dim):
-        hot = (at[:, None] == jnp.arange(table.shape[dim])[None]).astype(F32)
-        return jnp.tensordot(table, hot, axes=((dim,), (1,)), precision=lax.Precision.HIGHEST)
-
-    table = pick(table, x_block, 3)
-    table = pick(table, t_block, 2)
-    return pick(table, y_block, 2)
-
-
-def plane_masks(active):
-    frozen = 1.0 - active
-
-    def at(m, d):
-        start = [1, 1, 1]
-        if d is not None and d < 3:
-            start[(1, 0, 2)[d]] += 1
-        a, b, c = start
-        return frozen[:, m, a : a + 4, b : b + 2, c : c + 2]
-
-    masks = jnp.stack([at(m, None) * at(n, m) * at(m, n) * at(n, None) for m, n in PAIRS], axis=1)
-    masks = jnp.transpose(masks, (0, 1, 4, 2, 3)).reshape(2, 6, 2, 8, 1)
-    return jnp.broadcast_to(masks, (2, 6, 2, 8, 128))
+    other = meanwhile()
+    left, right, other = lax.optimization_barrier((left, right, other))
+    return jnp.concatenate([left, full, right], axis=1), other
+
+
+def active_rows(active_blocks):
+    index = (lax.axis_index("tm"), lax.axis_index("space"), 2 * lax.axis_index("sub"))
+    at = lax.dynamic_slice(active_blocks, (0, 0) + index, active_blocks.shape[:2] + (1, 1, 1))
+    return jnp.where(at[:, :, 0, 0, 0] > 0, 0, 1).astype(jnp.int32)
 
 
 def per_device(gauge_links, active_blocks, conv_in, bias_in, conv_out, bias_out):
-    own = jnp.transpose(gauge_links, (0, 1, 4, 3, 2, 5)).reshape(72, 2, 8, 128)
-    active = active_window(active_blocks)
-    pm = plane_masks(active)
-    ya = (active[:, :, 1, 1, 1] < 0.5).astype(jnp.int32)
-    w_in = jnp.transpose(conv_in.reshape(2, 3, 3, 3, 3, 12, 64), (0, 4, 6, 1, 2, 3, 5))
-    w_in = jnp.pad(w_in, [(0, 0)] * 6 + [(0, 4)]).reshape(2, 192, 432)
-    w_out = jnp.transpose(conv_out, (0, 2, 1))
-    b_in = jnp.broadcast_to(bias_in[:, :, None], (2, 64, 128))
-    b_out = jnp.broadcast_to(bias_out[:, :, None], (2, 24, 128))
-
+    own, first, last = run_unpack(gauge_links.reshape(72, 16, 128))
+    ya = active_rows(active_blocks)
+    weights = run_weights(conv_in, bias_in, conv_out, bias_out)
     for layer in range(2):
         if layer == 1:
             incoming = step(own[:, :, 0:4], "space", 1)
             own = jnp.concatenate([own[:, :, 4:8], incoming], axis=2)
+            first, last = own[:, :, 0:2], own[:, :, 6:8]
         own_s = step(own, "sub", 1)
-        tp, h, co = exchange(own)
+        tp, left, right, co_left, co_right = exchange(own, first, last)
+        if layer == 0:
+            left, right, ya, weights = lax.optimization_barrier((left, right, ya, weights))
+            ya = [ya[0], ya[1]]
+        h = jnp.concatenate([left, right], axis=2)
+        co = jnp.concatenate([co_left, co_right], axis=2)
         h_s = step(h, "sub", 1)
         co_s = step(co, "sub", 1)
+        tp, h_s, co_s = lax.optimization_barrier((tp, h_s, co_s))
         tp_s = step(tp, "sub", 1)
-        tr = run_traces(own, own_s, tp, h, pm[layer])
-        f = traces_rim(tr.reshape(2, 4, 2, 16, 128))
+        tr = run_traces(ya[layer], own, own_s, tp, h)
+        links = (own, own_s, tp, tp_s, h, h_s, co, co_s)
+        f, staples = traces_rim(
+            tr.reshape(2, 4, 2, 16, 128), lambda: run_staples(ya[layer], *links)
+        )
         f_s = step(f, "sub", 1)
-        staples = run_staples(ya[layer], own, own_s, tp, tp_s, h, h_s, co, co_s)
         own = run_final(
-            ya[layer], own, staples, f, f_s, w_in[layer], b_in[layer], w_out[layer], b_out[layer]
+            ya[layer],
+            own,
+            staples,
+            f,
+            f_s,
+            *weights[4 * layer : 4 * layer + 4],
+            layer == 1,
         )
-    out = own.reshape(4, 18, 2, 4, 2, 128)
-    return jnp.transpose(out, (0, 1, 4, 3, 2, 5))
+    return own.reshape(4, 18, 2, 4, 2, 128)
 
 
 def solution(mesh):

time: 122 us -> 91.7 us (0.75)
  local copies, waits for them, and re-layouts: 20.7 us -> 5.11 us
  Pallas kernels: 27 us -> 16.7 us
  starting transfers between devices: 24.7 us -> 30.9 us
  waiting for transfers between devices: 41.6 us -> 36.9 us
  other arithmetic: 5.82 us -> 1.62 us
    ppermute x25 -> x23, waiting for transfers between devices: 41.6 us -> 30.6 us  [step(): lax.ppermute(value, axis, [((i + by) % count, i) for i in range(count)])]
    ppermute x0 -> x4, starting transfers between devices: none -> 7.86 us  [diagonal(): return lax.ppermute(value, ('space', 'tm'), pairs)]
    ppermute x0 -> x4, waiting for transfers between devices: none -> 6.29 us  [diagonal(): return lax.ppermute(value, ('space', 'tm'), pairs)]
    pallas_call x2, Pallas kernels: 10.2 us -> 5.27 us  [run_staples(): pl.pallas_call(staple_kernel, out_shape=jax.ShapeDtypeStruct((24, 18, 8,...]
    slice x14 -> x6, local copies, waits for them, and re-layouts: 4.83 us -> 0.22 us  [the longest x2 0.14 us: per_device(): first, last = (own[:, :, 0:2], own[:, :, 6:8])]
    broadcast_in_dim x10 -> x0, local copies, waits for them, and re-layouts: 4.46 us -> none  [the longest x4 1.76 us: plane_masks(): return jnp.broadcast_to(masks, (2, 6, 2, 8, 128))]
    pallas_call x2, Pallas kernels: 6.5 us -> 3.35 us  [run_traces(): pl.pallas_call(trace_kernel, out_shape=jax.ShapeDtypeStruct((16, 16, 128)...]
    concatenate x6 -> x8, other arithmetic: 3.54 us -> 0.44 us  [the longest x2 0.27 us: per_device(): h = jnp.concatenate([left, right], axis=2)]
  transfers between devices with their start and end apart: 25 -> 27, of which waited for: 13 -> 14; matrix products, arithmetic and copies ran while one was open for 13% -> 4% of each run, Pallas kernels for 8% -> 10%
where the time goes in v1:
time: 91.7 us; the launch traced here: 91.3 us
  waiting for transfers between devices  36.9 us (40%)
  starting transfers between devices  30.9 us (34%)
  Pallas kernels  16.7 us (18%)
  local copies, waits for them, and re-layouts  5.11 us (6%)
  other arithmetic  1.62 us (2%)
    ppermute x23, waiting for transfers between devices, step(): lax.ppermute(value, axis, [((i + by) % count, i) for i in range(count)])  30.6 us
    ppermute x23, starting transfers between devices, step(): lax.ppermute(value, axis, [((i + by) % count, i) for i in range(count)])  23 us
    ppermute x4, starting transfers between devices, diagonal(): return lax.ppermute(value, ('space', 'tm'), pairs)  7.86 us
    pallas_call x2, Pallas kernels, run_final(): pl.pallas_call(last_kernel if last else final_kernel, out_shape=jax.Shape...  7.23 us
    ppermute x4, waiting for transfers between devices, diagonal(): return lax.ppermute(value, ('space', 'tm'), pairs)  6.29 us
    pallas_call x2, Pallas kernels, run_staples(): pl.pallas_call(staple_kernel, out_shape=jax.ShapeDtypeStruct((24, 18, 8,...  5.27 us
    unnamed x8, local copies, waits for them, and re-layouts  4.78 us
    pallas_call x2, Pallas kernels, run_traces(): pl.pallas_call(trace_kernel, out_shape=jax.ShapeDtypeStruct((16, 16, 128)...  3.35 us
  transfers between devices with their start and end apart: 27, of which 14 were waited for; matrix products, arithmetic and copies ran while one was open for 4% of the time, Pallas kernels for 10%

profile of v1, /device:TPU:0, one launch (start us, length us, event | category | flops | bytes accessed | tf_op | source)
XLA Modules:
  0.0 91.3 jit_solution(12647568046835721468)
XLA Ops:
  1.5 3.0 %collective-permute-start.3 = (f32[72,2,4,2,128]{4,3,2,1,0:T(2,128)S(1)}, f32[72,2,4,2,128]{4,3,2,1,0:T(2,128)S(1)}, u32[]{:S(2)}, u32[]{:S(2)}) collective-permute-start(f32[72,2,4,2,128]{4,3,2,1,0:T(2,128)S(1)} %bitcast.13), channel_id=1, source_target_pairs={{2,0},{0,2},{3,1},{1,3},{6,4},{4,6},{7,5},{5,7},{10,8},{8,10},{11,... | collective-permute-start | bytes 1769480 | tf_op jit(solution)/shard_map/ppermute | solution.py:363
  4.5 1.6 %collective-permute-start = (f32[72,2,2,128]{3,2,1,0:T(2,128)S(1)}, f32[72,2,2,128]{3,2,1,0:T(2,128)S(1)}, u32[]{:S(2)}, u32[]{:S(2)}) collective-permute-start(f32[72,2,2,128]{3,2,1,0:T(2,128)S(1)} %get-tuple-element.39), channel_id=1, source_target_pairs={{12,0},{0,4},{4,8},{8,12},{13,1},{1,5},{5,9},{9,13},{14,2},{2,6},{... | collective-permute-start | bytes 442376 | tf_op jit(solution)/shard_map/ppermute | solution.py:363
  6.1 2.2 %collective-permute-start.1 = (f32[72,2,2,128]{3,2,1,0:T(2,128)S(1)}, f32[72,2,2,128]{3,2,1,0:T(2,128)S(1)}, u32[]{:S(2)}, u32[]{:S(2)}) collective-permute-start(f32[72,2,2,128]{3,2,1,0:T(2,128)S(1)} %get-tuple-element.40), channel_id=1, source_target_pairs={{4,0},{8,4},{12,8},{0,12},{5,1},{9,5},{13,9},{1,13},{6,2},{10,6},{... | collective-permute-start | bytes 442376 | tf_op jit(solution)/shard_map/ppermute | solution.py:363
  8.3 1.6 %copy.9.conv_in = bf16[2,81,12,64]{3,2,1,0:T(8,128)(2,1)S(1)} copy(bf16[2,81,12,64]{1,3,2,0:T(8,128)(2,1)} %param.8) | data formatting | bytes 497664 | tf_op args[2]
  14.5 1.1 %collective-permute-start.5 = (f32[18,2,1,128]{3,2,1,0:T(1,128)S(1)}, f32[18,2,1,128]{3,2,1,0:T(1,128)S(1)}, u32[]{:S(2)}, u32[]{:S(2)}) collective-permute-start(f32[18,2,1,128]{3,2,1,0:T(1,128)S(1)} %slice.59), channel_id=1, source_target_pairs={{14,0},{12,2},{2,4},{0,6},{6,8},{4,10},{10,12},{8,14},{15,1},{13,3... | collective-permute-start | bytes 55304 | tf_op jit(solution)/shard_map/ppermute | solution.py:381
  15.7 3.7 %collective-permute-start.6 = (f32[18,2,1,128]{3,2,1,0:T(1,128)S(1)}, f32[18,2,1,128]{3,2,1,0:T(1,128)S(1)}, u32[]{:S(2)}, u32[]{:S(2)}) collective-permute-start(f32[18,2,1,128]{3,2,1,0:T(1,128)S(1)} %slice.60), channel_id=1, source_target_pairs={{6,0},{4,2},{10,4},{8,6},{14,8},{12,10},{2,12},{0,14},{7,1},{5,3},... | collective-permute-start | bytes 55304 | tf_op jit(solution)/shard_map/ppermute | solution.py:381
  19.3 1.7 %collective-permute-done.5 = f32[18,2,1,128]{3,2,1,0:T(1,128)S(1)} collective-permute-done((f32[18,2,1,128]{3,2,1,0:T(1,128)S(1)}, f32[18,2,1,128]{3,2,1,0:T(1,128)S(1)}, u32[]{:S(2)}, u32[]{:S(2)}) %collective-permute-start.5) | collective-permute-done | bytes 18464 | tf_op jit(solution)/shard_map/ppermute | solution.py:381
  21.1 1.2 %collective-permute-done.7.co_s = f32[18,2,2,128]{3,2,1,0:T(2,128)S(1)} collective-permute-done((f32[18,2,2,128]{3,2,1,0:T(2,128)S(1)}, f32[18,2,2,128]{3,2,1,0:T(2,128)S(1)}, u32[]{:S(2)}, u32[]{:S(2)}) %collective-permute-start.7) | collective-permute-done | bytes 36896 | tf_op jit(solution)/shard_map/ppermute | solution.py:363
  22.5 1.7 %traces.2 = bf16[16,16,128]{2,1,0:T(8,128)(2,1)S(1)} custom-call(s32[4]{0:T(128)S(1)} %get-tuple-element.83.ya, f32[72,2,8,128]{3,2,1,0:T(8,128)S(1)} %get-tuple-element.50.own, f32[72,2,8,128]{3,2,1,0:T(8,128)S(1)} %collective-permute-done.2.own_s, f32[72,2,8,128]{3,2,1,0:T(8,128)S(1)} %bitcast.15, f32[72,2,4,128]{3,2,1,0:T(4,128)S(1)} %pad_maximum_fusion.1.h), custom_call_target="tpu_custom_call" | custom-call | flops 8000000 | bytes 2000000 | tf_op jit(solution)/shard_map/traces/pallas_call | solution.py:318
  25.1 3.5 %collective-permute-done.8 = bf16[2,4,2,16,128]{4,3,2,1,0:T(8,128)(2,1)S(1)} collective-permute-done((bf16[2,4,2,16,128]{4,3,2,1,0:T(8,128)(2,1)S(1)}, bf16[2,4,2,16,128]{4,3,2,1,0:T(8,128)(2,1)S(1)}, u32[]{:S(2)}, u32[]{:S(2)}) %collective-permute-start.8) | collective-permute-done | bytes 65568 | tf_op jit(solution)/shard_map/ppermute | solution.py:363
  28.6 3.9 %collective-permute-start.10 = (bf16[2,1,4,16,128]{4,3,2,1,0:T(8,128)(2,1)S(1)}, bf16[2,1,4,16,128]{4,3,2,1,0:T(8,128)(2,1)S(1)}, u32[]{:S(2)}, u32[]{:S(2)}) collective-permute-start(bf16[2,1,4,16,128]{4,3,2,1,0:T(8,128)(2,1)S(1)} %get-tuple-element.77), channel_id=1, source_target_pairs={{4,0},{8,4},{12,8},{0,12},{5,1},{9,5},{13,9},{1,13},{6,2},{10,6},{... | collective-permute-start | bytes 98312 | tf_op jit(solution)/shard_map/ppermute | solution.py:363
  32.5 2.6 %staples.2 = f32[24,18,8,128]{3,2,1,0:T(8,128)S(1)} custom-call(s32[4]{0:T(128)S(1)} %get-tuple-element.83.ya, f32[72,2,8,128]{3,2,1,0:T(8,128)S(1)} %get-tuple-element.50.own, f32[72,2,8,128]{3,2,1,0:T(8,128)S(1)} %collective-permute-done.2.own_s, f32[72,2,8,128]{3,2,1,0:T(8,128)S(1)} %bitcast.16, f32[72,2,8,128]{3,2,1,0:T(8,128)S(1)} %collective-permute-done.11.tp_s, ...), custom_call_target="tpu_custom_call" | custom-call | flops 20000000 | bytes 16000000 | tf_op jit(solution)/shard_map/staples/pallas_call | solution.py:335
  35.2 3.1 %collective-permute-done.9 = bf16[2,1,4,16,128]{4,3,2,1,0:T(8,128)(2,1)S(1)} collective-permute-done((bf16[2,1,4,16,128]{4,3,2,1,0:T(8,128)(2,1)S(1)}, bf16[2,1,4,16,128]{4,3,2,1,0:T(8,128)(2,1)S(1)}, u32[]{:S(2)}, u32[]{:S(2)}) %collective-permute-start.9) | collective-permute-done | bytes 32800 | tf_op jit(solution)/shard_map/ppermute | solution.py:363
  38.4 1.4 %collective-permute-done.12.f_s = bf16[2,6,4,16,128]{4,3,2,1,0:T(8,128)(2,1)S(1)} collective-permute-done((bf16[2,6,4,16,128]{4,3,2,1,0:T(8,128)(2,1)S(1)}, bf16[2,6,4,16,128]{4,3,2,1,0:T(8,128)(2,1)S(1)}, u32[]{:S(2)}, u32[]{:S(2)}) %collective-permute-start.12) | collective-permute-done | bytes 196640 | tf_op jit(solution)/shard_map/ppermute | solution.py:363
  39.8 3.1 %rotate.2 = f32[72,2,8,128]{3,2,1,0:T(8,128)S(1)} custom-call(s32[4]{0:T(128)S(1)} %get-tuple-element.83.ya, f32[72,2,8,128]{3,2,1,0:T(8,128)S(1)} %get-tuple-element.50.own, f32[24,18,8,128]{3,2,1,0:T(8,128)S(1)} %staples.2, bf16[2,6,4,16,128]{4,3,2,1,0:T(8,128)(2,1)S(1)} %pad_maximum_fusion.3.f, ...), custom_call_target="tpu_custom_call" | custom-call | flops 300000000 | bytes 4000000 | tf_op jit(solution)/shard_map/rotate/pallas_call | solution.py:349
  43.8 8.3 %collective-permute-done.13 = f32[72,2,4,128]{3,2,1,0:T(4,128)S(1)} collective-permute-done((f32[72,2,4,128]{3,2,1,0:T(4,128)S(1)}, f32[72,2,4,128]{3,2,1,0:T(4,128)S(1)}, u32[]{:S(2)}, u32[]{:S(2)}) %collective-permute-start.13) | collective-permute-done | bytes 294944 | tf_op jit(solution)/shard_map/ppermute | solution.py:363
  52.3 1.6 %collective-permute-start.15 = (f32[72,2,4,2,128]{4,3,2,1,0:T(2,128)S(1)}, f32[72,2,4,2,128]{4,3,2,1,0:T(2,128)S(1)}, u32[]{:S(2)}, u32[]{:S(2)}) collective-permute-start(f32[72,2,4,2,128]{4,3,2,1,0:T(2,128)S(1)} %bitcast.12), channel_id=1, source_target_pairs={{2,0},{0,2},{3,1},{1,3},{6,4},{4,6},{7,5},{5,7},{10,8},{8,10},{11,... | collective-permute-start | bytes 1769480 | tf_op jit(solution)/shard_map/ppermute | solution.py:363
  53.9 2.6 %collective-permute-start.17 = (f32[72,2,2,128]{3,2,1,0:T(2,128)S(1)}, f32[72,2,2,128]{3,2,1,0:T(2,128)S(1)}, u32[]{:S(2)}, u32[]{:S(2)}) collective-permute-start(f32[72,2,2,128]{3,2,1,0:T(2,128)S(1)} %slice.80), channel_id=1, source_target_pairs={{4,0},{8,4},{12,8},{0,12},{5,1},{9,5},{13,9},{1,13},{6,2},{10,6},{... | collective-permute-start | bytes 442376 | tf_op jit(solution)/shard_map/ppermute | solution.py:363
  56.7 3.7 %collective-permute-done.17 = f32[72,2,2,128]{3,2,1,0:T(2,128)S(1)} collective-permute-done((f32[72,2,2,128]{3,2,1,0:T(2,128)S(1)}, f32[72,2,2,128]{3,2,1,0:T(2,128)S(1)}, u32[]{:S(2)}, u32[]{:S(2)}) %collective-permute-start.17) | collective-permute-done | bytes 147488 | tf_op jit(solution)/shard_map/ppermute | solution.py:363
  60.4 3.2 %collective-permute-done.16 = f32[72,2,2,128]{3,2,1,0:T(2,128)S(1)} collective-permute-done((f32[72,2,2,128]{3,2,1,0:T(2,128)S(1)}, f32[72,2,2,128]{3,2,1,0:T(2,128)S(1)}, u32[]{:S(2)}, u32[]{:S(2)}) %collective-permute-start.16) | collective-permute-done | bytes 147488 | tf_op jit(solution)/shard_map/ppermute | solution.py:363
  63.8 1.2 %collective-permute-start.20 = (f32[18,2,1,128]{3,2,1,0:T(1,128)S(1)}, f32[18,2,1,128]{3,2,1,0:T(1,128)S(1)}, u32[]{:S(2)}, u32[]{:S(2)}) collective-permute-start(f32[18,2,1,128]{3,2,1,0:T(1,128)S(1)} %slice.82), channel_id=1, source_target_pairs={{6,0},{4,2},{10,4},{8,6},{14,8},{12,10},{2,12},{0,14},{7,1},{5,3},... | collective-permute-start | bytes 55304 | tf_op jit(solution)/shard_map/ppermute | solution.py:381
  65.0 1.9 %collective-permute-start.19 = (f32[18,2,1,128]{3,2,1,0:T(1,128)S(1)}, f32[18,2,1,128]{3,2,1,0:T(1,128)S(1)}, u32[]{:S(2)}, u32[]{:S(2)}) collective-permute-start(f32[18,2,1,128]{3,2,1,0:T(1,128)S(1)} %slice.81), channel_id=1, source_target_pairs={{14,0},{12,2},{2,4},{0,6},{6,8},{4,10},{10,12},{8,14},{15,1},{13,3... | collective-permute-start | bytes 55304 | tf_op jit(solution)/shard_map/ppermute | solution.py:381
  66.9 1.7 %collective-permute-done.20 = f32[18,2,1,128]{3,2,1,0:T(1,128)S(1)} collective-permute-done((f32[18,2,1,128]{3,2,1,0:T(1,128)S(1)}, f32[18,2,1,128]{3,2,1,0:T(1,128)S(1)}, u32[]{:S(2)}, u32[]{:S(2)}) %collective-permute-start.20) | collective-permute-done | bytes 18464 | tf_op jit(solution)/shard_map/ppermute | solution.py:381
  68.5 3.0 %collective-permute-done.19 = f32[18,2,1,128]{3,2,1,0:T(1,128)S(1)} collective-permute-done((f32[18,2,1,128]{3,2,1,0:T(1,128)S(1)}, f32[18,2,1,128]{3,2,1,0:T(1,128)S(1)}, u32[]{:S(2)}, u32[]{:S(2)}) %collective-permute-start.19) | collective-permute-done | bytes 18464 | tf_op jit(solution)/shard_map/ppermute | solution.py:381
  71.6 1.2 %collective-permute-done.21.co_s = f32[18,2,2,128]{3,2,1,0:T(2,128)S(1)} collective-permute-done((f32[18,2,2,128]{3,2,1,0:T(2,128)S(1)}, f32[18,2,2,128]{3,2,1,0:T(2,128)S(1)}, u32[]{:S(2)}, u32[]{:S(2)}) %collective-permute-start.21) | collective-permute-done | bytes 36896 | tf_op jit(solution)/shard_map/ppermute | solution.py:363
  73.0 1.7 %traces.3 = bf16[16,16,128]{2,1,0:T(8,128)(2,1)S(1)} custom-call(s32[4]{0:T(128)S(1)} %get-tuple-element.84.ya, f32[72,2,8,128]{3,2,1,0:T(8,128)S(1)} %pad_maximum_fusion.own, f32[72,2,8,128]{3,2,1,0:T(8,128)S(1)} %collective-permute-done.14.own_s, f32[72,2,8,128]{3,2,1,0:T(8,128)S(1)} %bitcast.18, f32[72,2,4,128]{3,2,1,0:T(4,128)S(1)} %pad_maximum_fusion.2.h), custom_call_target="tpu_custom_call" | custom-call | flops 8000000 | bytes 2000000 | tf_op jit(solution)/shard_map/traces/pallas_call | solution.py:318
  74.7 1.5 %collective-permute-start.22 = (bf16[2,4,2,16,128]{4,3,2,1,0:T(8,128)(2,1)S(1)}, bf16[2,4,2,16,128]{4,3,2,1,0:T(8,128)(2,1)S(1)}, u32[]{:S(2)}, u32[]{:S(2)}) collective-permute-start(bf16[2,4,2,16,128]{4,3,2,1,0:T(8,128)(2,1)S(1)} %bitcast.23), channel_id=1, source_target_pairs={{2,0},{0,2},{3,1},{1,3},{6,4},{4,6},{7,5},{5,7},{10,8},{8,10},{11,... | collective-permute-start | bytes 196616 | tf_op jit(solution)/shard_map/ppermute | solution.py:363
  76.2 2.9 %collective-permute-done.22 = bf16[2,4,2,16,128]{4,3,2,1,0:T(8,128)(2,1)S(1)} collective-permute-done((bf16[2,4,2,16,128]{4,3,2,1,0:T(8,128)(2,1)S(1)}, bf16[2,4,2,16,128]{4,3,2,1,0:T(8,128)(2,1)S(1)}, u32[]{:S(2)}, u32[]{:S(2)}) %collective-permute-start.22) | collective-permute-done | bytes 65568 | tf_op jit(solution)/shard_map/ppermute | solution.py:363
  79.2 3.8 %collective-permute-start.24 = (bf16[2,1,4,16,128]{4,3,2,1,0:T(8,128)(2,1)S(1)}, bf16[2,1,4,16,128]{4,3,2,1,0:T(8,128)(2,1)S(1)}, u32[]{:S(2)}, u32[]{:S(2)}) collective-permute-start(bf16[2,1,4,16,128]{4,3,2,1,0:T(8,128)(2,1)S(1)} %get-tuple-element.75), channel_id=1, source_target_pairs={{4,0},{8,4},{12,8},{0,12},{5,1},{9,5},{13,9},{1,13},{6,2},{10,6},{... | collective-permute-start | bytes 98312 | tf_op jit(solution)/shard_map/ppermute | solution.py:363
  83.0 2.6 %staples.3 = f32[24,18,8,128]{3,2,1,0:T(8,128)S(1)} custom-call(s32[4]{0:T(128)S(1)} %get-tuple-element.84.ya, f32[72,2,8,128]{3,2,1,0:T(8,128)S(1)} %pad_maximum_fusion.own, f32[72,2,8,128]{3,2,1,0:T(8,128)S(1)} %collective-permute-done.14.own_s, f32[72,2,8,128]{3,2,1,0:T(8,128)S(1)} %bitcast.19, f32[72,2,8,128]{3,2,1,0:T(8,128)S(1)} %collective-permute-done.25.tp_s, ...), custom_call_target="tpu_custom_call" | custom-call | flops 20000000 | bytes 16000000 | tf_op jit(solution)/shard_map/staples/pallas_call | solution.py:335
  85.8 1.4 %collective-permute-done.26.f_s = bf16[2,6,4,16,128]{4,3,2,1,0:T(8,128)(2,1)S(1)} collective-permute-done((bf16[2,6,4,16,128]{4,3,2,1,0:T(8,128)(2,1)S(1)}, bf16[2,6,4,16,128]{4,3,2,1,0:T(8,128)(2,1)S(1)}, u32[]{:S(2)}, u32[]{:S(2)}) %collective-permute-start.26) | collective-permute-done | bytes 196640 | tf_op jit(solution)/shard_map/ppermute | solution.py:363
  87.2 4.1 %rotate.3 = f32[72,16,128]{2,1,0:T(8,128)} custom-call(s32[4]{0:T(128)S(1)} %get-tuple-element.84.ya, f32[72,2,8,128]{3,2,1,0:T(8,128)S(1)} %pad_maximum_fusion.own, f32[24,18,8,128]{3,2,1,0:T(8,128)S(1)} %staples.3, bf16[2,6,4,16,128]{4,3,2,1,0:T(8,128)(2,1)S(1)} %pad_maximum_fusion.4.f, bf16[2,6,4,16,128]{4,3,2,1,0:T(8,128)(2,1)S(1)} %collective-permute-done.26.f_s, ...), custom_call_target="tpu_custom_call" | custom-call | flops 300000000 | bytes 4000000 | tf_op jit(solution)/shard_map/rotate/pallas_call | solution.py:349
  (58 shorter events, 9.5 us)
Async XLA Ops:
  0.0 1.1 %copy-start = (f32[4,18,2,4,2,128]{5,4,3,2,1,0:T(2,128)S(1)}, f32[4,18,2,4,2,128]{5,4,3,2,1,0:T(2,128)}, u32[]{:S(2)}) copy-start(f32[4,18,2,4,2,128]{5,4,3,2,1,0:T(2,128)} %param.6) | copy-start | bytes 1769476
  1.5 20.9 %collective-permute-start.3 = (f32[72,2,4,2,128]{4,3,2,1,0:T(2,128)S(1)}, f32[72,2,4,2,128]{4,3,2,1,0:T(2,128)S(1)}, u32[]{:S(2)}, u32[]{:S(2)}) collective-permute-start(f32[72,2,4,2,128]{4,3,2,1,0:T(2,128)S(1)} %bitcast.13), channel_id=1, source_target_pairs={{2,0},{0,2},{3,1},{1,3},{6,4},{4,6},{7,5},{5,7},{10,8},{8,10},{11,... | collective-permute-start | bytes 1769480 | tf_op jit(solution)/shard_map/ppermute | solution.py:363
  4.5 9.0 %collective-permute-start = (f32[72,2,2,128]{3,2,1,0:T(2,128)S(1)}, f32[72,2,2,128]{3,2,1,0:T(2,128)S(1)}, u32[]{:S(2)}, u32[]{:S(2)}) collective-permute-start(f32[72,2,2,128]{3,2,1,0:T(2,128)S(1)} %get-tuple-element.39), channel_id=1, source_target_pairs={{12,0},{0,4},{4,8},{8,12},{13,1},{1,5},{5,9},{9,13},{14,2},{2,6},{... | collective-permute-start | bytes 442376 | tf_op jit(solution)/shard_map/ppermute | solution.py:363
  6.1 8.2 %collective-permute-start.1 = (f32[72,2,2,128]{3,2,1,0:T(2,128)S(1)}, f32[72,2,2,128]{3,2,1,0:T(2,128)S(1)}, u32[]{:S(2)}, u32[]{:S(2)}) collective-permute-start(f32[72,2,2,128]{3,2,1,0:T(2,128)S(1)} %get-tuple-element.40), channel_id=1, source_target_pairs={{4,0},{8,4},{12,8},{0,12},{5,1},{9,5},{13,9},{1,13},{6,2},{10,6},{... | collective-permute-start | bytes 442376 | tf_op jit(solution)/shard_map/ppermute | solution.py:363
  8.3 14.2 %collective-permute-start.2 = (f32[72,2,8,128]{3,2,1,0:T(8,128)S(1)}, f32[72,2,8,128]{3,2,1,0:T(8,128)S(1)}, u32[]{:S(2)}, u32[]{:S(2)}) collective-permute-start(f32[72,2,8,128]{3,2,1,0:T(8,128)S(1)} %get-tuple-element.50.own), channel_id=1, source_target_pairs={{1,0},{0,1},{3,2},{2,3},{5,4},{4,5},{7,6},{6,7},{9,8},{8,9},{11,10... | collective-permute-start | bytes 1769480 | tf_op jit(solution)/shard_map/ppermute | solution.py:363
  10.7 0.7 copy-start.1
  11.4 0.7 copy-start.2
  14.4 7.9 %collective-permute-start.4 = (f32[72,2,4,128]{3,2,1,0:T(4,128)S(1)}, f32[72,2,4,128]{3,2,1,0:T(4,128)S(1)}, u32[]{:S(2)}, u32[]{:S(2)}) collective-permute-start(f32[72,2,4,128]{3,2,1,0:T(4,128)S(1)} %pad_maximum_fusion.1.h), channel_id=1, source_target_pairs={{1,0},{0,1},{3,2},{2,3},{5,4},{4,5},{7,6},{6,7},{9,8},{8,9},{11,10... | collective-permute-start | bytes 884744 | tf_op jit(solution)/shard_map/ppermute | solution.py:363
  14.5 6.5 %collective-permute-start.5 = (f32[18,2,1,128]{3,2,1,0:T(1,128)S(1)}, f32[18,2,1,128]{3,2,1,0:T(1,128)S(1)}, u32[]{:S(2)}, u32[]{:S(2)}) collective-permute-start(f32[18,2,1,128]{3,2,1,0:T(1,128)S(1)} %slice.59), channel_id=1, source_target_pairs={{14,0},{12,2},{2,4},{0,6},{6,8},{4,10},{10,12},{8,14},{15,1},{13,3... | collective-permute-start | bytes 55304 | tf_op jit(solution)/shard_map/ppermute | solution.py:381
  15.7 5.3 %collective-permute-start.6 = (f32[18,2,1,128]{3,2,1,0:T(1,128)S(1)}, f32[18,2,1,128]{3,2,1,0:T(1,128)S(1)}, u32[]{:S(2)}, u32[]{:S(2)}) collective-permute-start(f32[18,2,1,128]{3,2,1,0:T(1,128)S(1)} %slice.60), channel_id=1, source_target_pairs={{6,0},{4,2},{10,4},{8,6},{14,8},{12,10},{2,12},{0,14},{7,1},{5,3},... | collective-permute-start | bytes 55304 | tf_op jit(solution)/shard_map/ppermute | solution.py:381
  21.0 1.3 %collective-permute-start.7 = (f32[18,2,2,128]{3,2,1,0:T(2,128)S(1)}, f32[18,2,2,128]{3,2,1,0:T(2,128)S(1)}, u32[]{:S(2)}, u32[]{:S(2)}) collective-permute-start(f32[18,2,2,128]{3,2,1,0:T(2,128)S(1)} %pad_maximum_fusion.5.co), channel_id=1, source_target_pairs={{1,0},{0,1},{3,2},{2,3},{5,4},{4,5},{7,6},{6,7},{9,8},{8,9},{11,10... | collective-permute-start | bytes 110600 | tf_op jit(solution)/shard_map/ppermute | solution.py:363
  22.3 10.2 %collective-permute-start.11 = (f32[72,2,8,128]{3,2,1,0:T(8,128)S(1)}, f32[72,2,8,128]{3,2,1,0:T(8,128)S(1)}, u32[]{:S(2)}, u32[]{:S(2)}) collective-permute-start(f32[72,2,8,128]{3,2,1,0:T(8,128)S(1)} %bitcast.14), channel_id=1, source_target_pairs={{1,0},{0,1},{3,2},{2,3},{5,4},{4,5},{7,6},{6,7},{9,8},{8,9},{11,10... | collective-permute-start | bytes 1769480 | tf_op jit(solution)/shard_map/ppermute | solution.py:363
  24.2 4.4 %collective-permute-start.8 = (bf16[2,4,2,16,128]{4,3,2,1,0:T(8,128)(2,1)S(1)}, bf16[2,4,2,16,128]{4,3,2,1,0:T(8,128)(2,1)S(1)}, u32[]{:S(2)}, u32[]{:S(2)}) collective-permute-start(bf16[2,4,2,16,128]{4,3,2,1,0:T(8,128)(2,1)S(1)} %bitcast.20), channel_id=1, source_target_pairs={{2,0},{0,2},{3,1},{1,3},{6,4},{4,6},{7,5},{5,7},{10,8},{8,10},{11,... | collective-permute-start | bytes 196616 | tf_op jit(solution)/shard_map/ppermute | solution.py:363
  28.6 6.6 %collective-permute-start.10 = (bf16[2,1,4,16,128]{4,3,2,1,0:T(8,128)(2,1)S(1)}, bf16[2,1,4,16,128]{4,3,2,1,0:T(8,128)(2,1)S(1)}, u32[]{:S(2)}, u32[]{:S(2)}) collective-permute-start(bf16[2,1,4,16,128]{4,3,2,1,0:T(8,128)(2,1)S(1)} %get-tuple-element.77), channel_id=1, source_target_pairs={{4,0},{8,4},{12,8},{0,12},{5,1},{9,5},{13,9},{1,13},{6,2},{10,6},{... | collective-permute-start | bytes 98312 | tf_op jit(solution)/shard_map/ppermute | solution.py:363
  32.5 5.7 %collective-permute-start.9 = (bf16[2,1,4,16,128]{4,3,2,1,0:T(8,128)(2,1)S(1)}, bf16[2,1,4,16,128]{4,3,2,1,0:T(8,128)(2,1)S(1)}, u32[]{:S(2)}, u32[]{:S(2)}) collective-permute-start(bf16[2,1,4,16,128]{4,3,2,1,0:T(8,128)(2,1)S(1)} %get-tuple-element.78), channel_id=1, source_target_pairs={{12,0},{0,4},{4,8},{8,12},{13,1},{1,5},{5,9},{9,13},{14,2},{2,6},{... | collective-permute-start | bytes 98312 | tf_op jit(solution)/shard_map/ppermute | solution.py:363
  38.3 1.5 %collective-permute-start.12 = (bf16[2,6,4,16,128]{4,3,2,1,0:T(8,128)(2,1)S(1)}, bf16[2,6,4,16,128]{4,3,2,1,0:T(8,128)(2,1)S(1)}, u32[]{:S(2)}, u32[]{:S(2)}) collective-permute-start(bf16[2,6,4,16,128]{4,3,2,1,0:T(8,128)(2,1)S(1)} %pad_maximum_fusion.3.f), channel_id=1, source_target_pairs={{1,0},{0,1},{3,2},{2,3},{5,4},{4,5},{7,6},{6,7},{9,8},{8,9},{11,10... | collective-permute-start | bytes 589832 | tf_op jit(solution)/shard_map/ppermute | solution.py:363
  43.0 9.1 %collective-permute-start.13 = (f32[72,2,4,128]{3,2,1,0:T(4,128)S(1)}, f32[72,2,4,128]{3,2,1,0:T(4,128)S(1)}, u32[]{:S(2)}, u32[]{:S(2)}) collective-permute-start(f32[72,2,4,128]{3,2,1,0:T(4,128)S(1)} %get-tuple-element.74), channel_id=1, source_target_pairs={{4,0},{8,4},{12,8},{0,12},{5,1},{9,5},{13,9},{1,13},{6,2},{10,6},{... | collective-permute-start | bytes 884744 | tf_op jit(solution)/shard_map/ppermute | solution.py:363
  52.3 20.6 %collective-permute-start.15 = (f32[72,2,4,2,128]{4,3,2,1,0:T(2,128)S(1)}, f32[72,2,4,2,128]{4,3,2,1,0:T(2,128)S(1)}, u32[]{:S(2)}, u32[]{:S(2)}) collective-permute-start(f32[72,2,4,2,128]{4,3,2,1,0:T(2,128)S(1)} %bitcast.12), channel_id=1, source_target_pairs={{2,0},{0,2},{3,1},{1,3},{6,4},{4,6},{7,5},{5,7},{10,8},{8,10},{11,... | collective-permute-start | bytes 1769480 | tf_op jit(solution)/shard_map/ppermute | solution.py:363
  53.9 6.5 %collective-permute-start.17 = (f32[72,2,2,128]{3,2,1,0:T(2,128)S(1)}, f32[72,2,2,128]{3,2,1,0:T(2,128)S(1)}, u32[]{:S(2)}, u32[]{:S(2)}) collective-permute-start(f32[72,2,2,128]{3,2,1,0:T(2,128)S(1)} %slice.80), channel_id=1, source_target_pairs={{4,0},{8,4},{12,8},{0,12},{5,1},{9,5},{13,9},{1,13},{6,2},{10,6},{... | collective-permute-start | bytes 442376 | tf_op jit(solution)/shard_map/ppermute | solution.py:363
  56.6 7.0 %collective-permute-start.16 = (f32[72,2,2,128]{3,2,1,0:T(2,128)S(1)}, f32[72,2,2,128]{3,2,1,0:T(2,128)S(1)}, u32[]{:S(2)}, u32[]{:S(2)}) collective-permute-start(f32[72,2,2,128]{3,2,1,0:T(2,128)S(1)} %slice.79), channel_id=1, source_target_pairs={{12,0},{0,4},{4,8},{8,12},{13,1},{1,5},{5,9},{9,13},{14,2},{2,6},{... | collective-permute-start | bytes 442376 | tf_op jit(solution)/shard_map/ppermute | solution.py:363
  56.7 16.4 %collective-permute-start.14 = (f32[72,2,8,128]{3,2,1,0:T(8,128)S(1)}, f32[72,2,8,128]{3,2,1,0:T(8,128)S(1)}, u32[]{:S(2)}, u32[]{:S(2)}) collective-permute-start(f32[72,2,8,128]{3,2,1,0:T(8,128)S(1)} %pad_maximum_fusion.own), channel_id=1, source_target_pairs={{1,0},{0,1},{3,2},{2,3},{5,4},{4,5},{7,6},{6,7},{9,8},{8,9},{11,10... | collective-permute-start | bytes 1769480 | tf_op jit(solution)/shard_map/ppermute | solution.py:363
  63.7 9.1 %collective-permute-start.18 = (f32[72,2,4,128]{3,2,1,0:T(4,128)S(1)}, f32[72,2,4,128]{3,2,1,0:T(4,128)S(1)}, u32[]{:S(2)}, u32[]{:S(2)}) collective-permute-start(f32[72,2,4,128]{3,2,1,0:T(4,128)S(1)} %pad_maximum_fusion.2.h), channel_id=1, source_target_pairs={{1,0},{0,1},{3,2},{2,3},{5,4},{4,5},{7,6},{6,7},{9,8},{8,9},{11,10... | collective-permute-start | bytes 884744 | tf_op jit(solution)/shard_map/ppermute | solution.py:363
  63.8 4.7 %collective-permute-start.20 = (f32[18,2,1,128]{3,2,1,0:T(1,128)S(1)}, f32[18,2,1,128]{3,2,1,0:T(1,128)S(1)}, u32[]{:S(2)}, u32[]{:S(2)}) collective-permute-start(f32[18,2,1,128]{3,2,1,0:T(1,128)S(1)} %slice.82), channel_id=1, source_target_pairs={{6,0},{4,2},{10,4},{8,6},{14,8},{12,10},{2,12},{0,14},{7,1},{5,3},... | collective-permute-start | bytes 55304 | tf_op jit(solution)/shard_map/ppermute | solution.py:381
  65.0 6.5 %collective-permute-start.19 = (f32[18,2,1,128]{3,2,1,0:T(1,128)S(1)}, f32[18,2,1,128]{3,2,1,0:T(1,128)S(1)}, u32[]{:S(2)}, u32[]{:S(2)}) collective-permute-start(f32[18,2,1,128]{3,2,1,0:T(1,128)S(1)} %slice.81), channel_id=1, source_target_pairs={{14,0},{12,2},{2,4},{0,6},{6,8},{4,10},{10,12},{8,14},{15,1},{13,3... | collective-permute-start | bytes 55304 | tf_op jit(solution)/shard_map/ppermute | solution.py:381
  71.6 1.3 %collective-permute-start.21 = (f32[18,2,2,128]{3,2,1,0:T(2,128)S(1)}, f32[18,2,2,128]{3,2,1,0:T(2,128)S(1)}, u32[]{:S(2)}, u32[]{:S(2)}) collective-permute-start(f32[18,2,2,128]{3,2,1,0:T(2,128)S(1)} %pad_maximum_fusion.6.co), channel_id=1, source_target_pairs={{1,0},{0,1},{3,2},{2,3},{5,4},{4,5},{7,6},{6,7},{9,8},{8,9},{11,10... | collective-permute-start | bytes 110600 | tf_op jit(solution)/shard_map/ppermute | solution.py:363
  72.8 10.2 %collective-permute-start.25 = (f32[72,2,8,128]{3,2,1,0:T(8,128)S(1)}, f32[72,2,8,128]{3,2,1,0:T(8,128)S(1)}, u32[]{:S(2)}, u32[]{:S(2)}) collective-permute-start(f32[72,2,8,128]{3,2,1,0:T(8,128)S(1)} %bitcast.17), channel_id=1, source_target_pairs={{1,0},{0,1},{3,2},{2,3},{5,4},{4,5},{7,6},{6,7},{9,8},{8,9},{11,10... | collective-permute-start | bytes 1769480 | tf_op jit(solution)/shard_map/ppermute | solution.py:363
  74.7 4.4 %collective-permute-start.22 = (bf16[2,4,2,16,128]{4,3,2,1,0:T(8,128)(2,1)S(1)}, bf16[2,4,2,16,128]{4,3,2,1,0:T(8,128)(2,1)S(1)}, u32[]{:S(2)}, u32[]{:S(2)}) collective-permute-start(bf16[2,4,2,16,128]{4,3,2,1,0:T(8,128)(2,1)S(1)} %bitcast.23), channel_id=1, source_target_pairs={{2,0},{0,2},{3,1},{1,3},{6,4},{4,6},{7,5},{5,7},{10,8},{8,10},{11,... | collective-permute-start | bytes 196616 | tf_op jit(solution)/shard_map/ppermute | solution.py:363
  79.1 6.5 %collective-permute-start.23 = (bf16[2,1,4,16,128]{4,3,2,1,0:T(8,128)(2,1)S(1)}, bf16[2,1,4,16,128]{4,3,2,1,0:T(8,128)(2,1)S(1)}, u32[]{:S(2)}, u32[]{:S(2)}) collective-permute-start(bf16[2,1,4,16,128]{4,3,2,1,0:T(8,128)(2,1)S(1)} %get-tuple-element.76), channel_id=1, source_target_pairs={{12,0},{0,4},{4,8},{8,12},{13,1},{1,5},{5,9},{9,13},{14,2},{2,6},{... | collective-permute-start | bytes 98312 | tf_op jit(solution)/shard_map/ppermute | solution.py:363
  79.2 6.5 %collective-permute-start.24 = (bf16[2,1,4,16,128]{4,3,2,1,0:T(8,128)(2,1)S(1)}, bf16[2,1,4,16,128]{4,3,2,1,0:T(8,128)(2,1)S(1)}, u32[]{:S(2)}, u32[]{:S(2)}) collective-permute-start(bf16[2,1,4,16,128]{4,3,2,1,0:T(8,128)(2,1)S(1)} %get-tuple-element.75), channel_id=1, source_target_pairs={{4,0},{8,4},{12,8},{0,12},{5,1},{9,5},{13,9},{1,13},{6,2},{10,6},{... | collective-permute-start | bytes 98312 | tf_op jit(solution)/shard_map/ppermute | solution.py:363
  85.7 1.5 %collective-permute-start.26 = (bf16[2,6,4,16,128]{4,3,2,1,0:T(8,128)(2,1)S(1)}, bf16[2,6,4,16,128]{4,3,2,1,0:T(8,128)(2,1)S(1)}, u32[]{:S(2)}, u32[]{:S(2)}) collective-permute-start(bf16[2,6,4,16,128]{4,3,2,1,0:T(8,128)(2,1)S(1)} %pad_maximum_fusion.4.f), channel_id=1, source_target_pairs={{1,0},{0,1},{3,2},{2,3},{5,4},{4,5},{7,6},{6,7},{9,8},{8,9},{11,10... | collective-permute-start | bytes 589832 | tf_op jit(solution)/shard_map/ppermute | solution.py:363

commit v2 on v1

--- a/solution.py
+++ b/solution.py
@@ -1,3 +1,5 @@
+import functools
+
 import jax
 import jax.numpy as jnp
 from jax import lax
@@ -56,36 +58,49 @@
     return pltpu.roll(value, (-step) % value.shape[-1], value.ndim - 1)
 
 
-def trace_kernel(ya, own, own_s, tp, h, out, v0, vup, trs):
+def trace_kernel(at_right, halves, ya, *refs):
+    inputs, (out, v0, vup, trs) = refs[:-4], refs[-4:]
+    if halves == 1:
+        own, own_s, tp, right = inputs
+        parts = [(own, own_s, tp, right, at_right)]
+    else:
+        own, own_s, tp, right, tp_s, right_tp = inputs
+        parts = [(own, own_s, tp, right, at_right), (tp, tp_s, own, right_tp, 0)]
     even = lax.broadcasted_iota(jnp.int32, (8, 128), 0) % 2 == 0
+    count = 16 * halves
 
     def prep(i, _):
-        for y in range(2):
-            o = own[i, y]
-            t = tp[i, y]
-            v0[i, y, BASE : BASE + 8] = o
-            v0[i, y, BASE + 8 : BASE + 10] = h[i, y, 2:4]
-            vup[i, y] = jnp.where(even, pltpu.roll(o, 7, 0), pltpu.roll(t, 1, 0))
-        v0[i, 2, BASE : BASE + 8] = own_s[i, 0]
+        for half, (link, link_s, later, after, at) in enumerate(parts):
+            k = 72 * half + i
+            for y in range(2):
+                o = link[i, y]
+                t = later[i, y]
+                v0[k, y, BASE : BASE + 8] = o
+                v0[k, y, BASE + 8 : BASE + 10] = after[i, y, at : at + 2]
+                vup[k, y] = jnp.where(even, pltpu.roll(o, 7, 0), pltpu.roll(t, 1, 0))
+            v0[k, 2, BASE : BASE + 8] = link_s[i, 0]
         return 0
 
     lax.fori_loop(0, 72, prep, 0, unroll=4)
-    trs[192:256] = jnp.zeros((64, 128), F32)
+    trs[12 * count :] = jnp.zeros((4 * count, 128), F32)
     row_of = lax.broadcasted_iota(jnp.int32, (8, 128), 0)
     leaves = (row_of % 2, jnp.where(row_of >= 6, 1, 0), 1, 0)
 
-    def at_y(y, _):
-        active = [jnp.where(ya[m] == y, 1, 0) for m in range(4)]
+    def at_y(place, _):
+        half, y = place // 2, place % 2
+        active = [jnp.where(ya[m] == y, 1, 0) ^ half for m in range(4)]
+        first = 72 * half
 
         def look(d, step):
+            base = first + 18 * d
             if step == 0:
-                parts = [vup[18 * d + c, y] for c in range(18)]
+                parts = [vup[base + c, y] for c in range(18)]
             elif step == 1:
-                parts = [v0[18 * d + c, y, BASE + 2 : BASE + 10] for c in range(18)]
+                parts = [v0[base + c, y, BASE + 2 : BASE + 10] for c in range(18)]
             elif step == 2:
-                parts = [v0[18 * d + c, y + 1, BASE : BASE + 8] for c in range(18)]
+                parts = [v0[base + c, y + 1, BASE : BASE + 8] for c in range(18)]
             else:
-                parts = [v0[18 * d + c, y, BASE : BASE + 8] for c in range(18)]
+                parts = [v0[base + c, y, BASE : BASE + 8] for c in range(18)]
                 if step == 3:
                     parts = [zroll(p, 1) for p in parts]
             return as_matrix(parts)
@@ -101,14 +116,16 @@
                 im = q if im is None else im + q
             moved = (active[n] ^ leaves[m]) | (active[m] ^ leaves[n]) | active[m] | active[n]
             frozen = jnp.broadcast_to(moved, (8, 128)) == 0
-            row = pl.multiple_of(y * 8, 8)
-            trs[pl.ds((2 * p) * 16 + row, 8)] = jnp.where(frozen, re * (1.0 / 3.0), 0.0)
-            trs[pl.ds((2 * p + 1) * 16 + row, 8)] = jnp.where(frozen, im * (1.0 / 3.0), 0.0)
+            row = pl.multiple_of(place * 8, 8)
+            trs[pl.ds((2 * p) * count + row, 8)] = jnp.where(frozen, re * (1.0 / 3.0), 0.0)
+            trs[pl.ds((2 * p + 1) * count + row, 8)] = jnp.where(frozen, im * (1.0 / 3.0), 0.0)
         return 0
 
-    lax.fori_loop(0, 2, at_y, 0)
-    for r in range(16):
-        out[r] = trs[pl.ds(r, 16, stride=16), :].astype(BF16)
+    lax.fori_loop(0, 2 * halves, at_y, 0)
+    for r in range(count):
+        half, yx, t = r // 16, r % 16 // 2, r % 2
+        place = r if halves == 1 else 4 * yx + ((3, 0)[t] if half else 1 + t)
+        out[place] = trs[pl.ds(r, 16, stride=count), :].astype(BF16)
 
 
 def staple_kernel(ya, own, own_s, tp, tp_s, h, h_s, co, co_s, out, v0, vup, vdn):
@@ -166,12 +183,12 @@
                 out[6 * m + 2 * j + 1, c] = value
 
 
-def unpack_kernel(x, own, first, last):
+def unpack_kernel(x, own, last, head):
     def body(i, _):
         for y in range(2):
             for t in range(2):
                 own[i, y, pl.ds(t, 4, stride=2)] = x[i, pl.ds(8 * t + y, 4, stride=2)]
-                first[i, y, t : t + 1] = x[i, 8 * t + y : 8 * t + y + 1]
+                head[i, y, pl.ds(t, 3, stride=2)] = x[i, pl.ds(8 * t + y, 3, stride=2)]
                 last[i, y, t : t + 1] = x[i, 8 * t + 6 + y : 8 * t + 7 + y]
         return 0
 
@@ -197,7 +214,7 @@
 
 
 def last_kernel(ya, own, staples, f, f_s, w_in, b_in, w_out, b_out, packed, out, wts):
-    final_kernel(ya, own, staples, f, f_s, w_in, b_in, w_out, b_out, out, wts)
+    update(ya, own, staples, f, f_s, w_in, b_in, w_out, b_out, out, wts)
 
     def body(i, _):
         for y in range(2):
@@ -208,7 +225,15 @@
     lax.fori_loop(0, 72, body, 0, unroll=8)
 
 
-def final_kernel(ya, own, staples, f, f_s, w_in, b_in, w_out, b_out, out, wts):
+def final_kernel(
+    ya, own, staples, f, f_s, w_in, b_in, w_out, b_out, out, q_head, q_tail, wts
+):
+    update(
+        ya, own, staples, f, f_s, w_in, b_in, w_out, b_out, out, wts, sent=(q_head, q_tail)
+    )
+
+
+def update(ya, own, staples, f, f_s, w_in, b_in, w_out, b_out, out, wts, sent=None):
     places = ((1, 1), (0, 0), (0, 1), (1, 0))
     for y in range(2):
         for x in range(4):
@@ -243,40 +268,92 @@
             total = term if total is None else [a + b for a, b in zip(total, term)]
         are, aim = mm(link, as_matrix(total))
         trace_im = (aim[0][0] + aim[1][1] + aim[2][2]) * (1.0 / 3.0)
-        low = [[None] * 3 for _ in range(3)]
-        for i in range(3):
-            low[i][i] = (jnp.ones_like(trace_im), -0.5 * (aim[i][i] - trace_im))
-            for k in range(i + 1, 3):
-                qr = -0.25 * (are[i][k] - are[k][i])
-                qi = -0.25 * (aim[i][k] + aim[k][i])
-                low[i][k] = (qr, qi)
-                low[k][i] = (-qr, qi)
-        adj_re, adj_im = [], []
-        for i in range(3):
-            row_re, row_im = [], []
-            for j in range(3):
-                first = cmul(low[(j + 1) % 3][(i + 1) % 3], low[(j + 2) % 3][(i + 2) % 3])
-                second = cmul(low[(j + 1) % 3][(i + 2) % 3], low[(j + 2) % 3][(i + 1) % 3])
-                row_re.append(first[0] - second[0])
-                row_im.append(first[1] - second[1])
-            adj_re.append(row_re)
-            adj_im.append(row_im)
-        det_re = det_im = None
-        for k in range(3):
-            product = cmul(low[0][k], (adj_re[k][0], adj_im[k][0]))
-            det_re = product[0] if det_re is None else det_re + product[0]
-            det_im = product[1] if det_im is None else det_im + product[1]
-        twice = 2.0 / (det_re * det_re + det_im * det_im)
-        scale_re = det_re * twice
-        scale_im = -det_im * twice
-        turned = flat(mm((adj_re, adj_im), link))
-        current = flat(link)
-        for c in range(9):
-            re, im = cmul((turned[c], turned[9 + c]), (scale_re, scale_im))
-            out[18 * m + c, y] = re - current[c]
-            out[18 * m + 9 + c, y] = im - current[9 + c]
+        low = []
+        for i, k in ((0, 1), (0, 2), (1, 2)):
+            low.append(-0.25 * (are[i][k] - are[k][i]))
+            low.append(-0.25 * (aim[i][k] + aim[k][i]))
+        low += [-0.5 * (aim[i][i] - trace_im) for i in range(3)]
+        if sent is not None:
+            for c in range(9):
+                sent[0][9 * m + c] = low[c][0:6]
+                sent[1][9 * m + c] = low[c][2:8]
+        for c, value in enumerate(rotated(low, link)):
+            out[18 * m + c, y] = value
         for c in range(18):
             out[18 * m + c, 1 - y] = own[18 * m + c, 1 - y]
+
+
+def rotated(low, link):
+    one = jnp.ones_like(low[0])
+    full = [[None] * 3 for _ in range(3)]
+    for i in range(3):
+        full[i][i] = (one, low[6 + i])
+    for at, (i, k) in enumerate(((0, 1), (0, 2), (1, 2))):
+        re, im = low[2 * at], low[2 * at + 1]
+        full[i][k] = (re, im)
+        full[k][i] = (-re, im)
+    adj_re, adj_im = [], []
+    for i in range(3):
+        row_re, row_im = [], []
+        for j in range(3):
+            first = cmul(full[(j + 1) % 3][(i + 1) % 3], full[(j + 2) % 3][(i + 2) % 3])
+            second = cmul(full[(j + 1) % 3][(i + 2) % 3], full[(j + 2) % 3][(i + 1) % 3])
+            row_re.append(first[0] - second[0])
+            row_im.append(first[1] - second[1])
+        adj_re.append(row_re)
+        adj_im.append(row_im)
+    det_re = det_im = None
+    for k in range(3):
+        product = cmul(full[0][k], (adj_re[k][0], adj_im[k][0]))
+        det_re = product[0] if det_re is None else det_re + product[0]
+        det_im = product[1] if det_im is None else det_im + product[1]
+    twice = 2.0 / (det_re * det_re + det_im * det_im)
+    scale_re = det_re * twice
+    scale_im = -det_im * twice
+    turned = flat(mm((adj_re, adj_im), link))
+    current = flat(link)
+    real, imag = [], []
+    for c in range(9):
+        re, im = cmul((turned[c], turned[9 + c]), (scale_re, scale_im))
+        real.append(re - current[c])
+        imag.append(im - current[9 + c])
+    return real + imag
+
+
+def shift_kernel(ya, own, head, tp, far, q_head, q_tp, q_far, own_o, h_o, tp_o, co_o, right_tp_o):
+    for m in range(4):
+        here = ya[m]
+        there = 1 - here
+        rows = slice(18 * m, 18 * m + 18)
+
+        def turn(q, links):
+            return rotated([q[9 * m + c] for c in range(9)], as_matrix(links))
+
+        new = turn(q_head, [head[i, there] for i in range(rows.start, rows.stop)])
+        for c, i in enumerate(range(rows.start, rows.stop)):
+            for y in range(2):
+                own_o[i, y, 0:4] = own[i, y, 4:8]
+                h_o[i, y, 0:2] = own[i, y, 2:4]
+            own_o[i, there, 4:8] = new[c][0:4]
+            h_o[i, there, 2:4] = new[c][4:6]
+            own_o[i, here, 4:8] = head[i, here, 0:4]
+            h_o[i, here, 2:4] = head[i, here, 4:6]
+        new = turn(q_tp, [tp[i, there, 2:8] for i in range(rows.start, rows.stop)])
+        for c, i in enumerate(range(rows.start, rows.stop)):
+            tp_o[i, there, 0:4] = new[c][2:6]
+            tp_o[i, here, 0:4] = tp[i, here, 4:8]
+            if m == 1:
+                co_o[c, there, 0:1] = new[c][0:1]
+                co_o[c, here, 0:1] = tp[i, here, 2:3]
+        new = turn(q_far, [far[i, here] for i in range(rows.start, rows.stop)])
+        for c, i in enumerate(range(rows.start, rows.stop)):
+            tp_o[i, here, 4:8] = new[c][0:4]
+            tp_o[i, there, 4:8] = far[i, there, 0:4]
+            right_tp_o[i, here] = new[c][4:6]
+            right_tp_o[i, there] = far[i, there, 4:6]
+            if m == 0:
+                co_o[c, here, 1:2] = new[c][5:6]
+                co_o[c, there, 1:2] = far[i, there, 5:6]
 
 
 VM = pl.BlockSpec(memory_space=pltpu.VMEM)
@@ -302,10 +379,13 @@
 
 
 def run_unpack(x):
-    rows = jax.ShapeDtypeStruct((72, 2, 2, 128), F32)
     return pl.pallas_call(
         unpack_kernel,
-        out_shape=[jax.ShapeDtypeStruct((72, 2, 8, 128), F32), rows, rows],
+        out_shape=[
+            jax.ShapeDtypeStruct((72, 2, 8, 128), F32),
+            jax.ShapeDtypeStruct((72, 2, 2, 128), F32),
+            jax.ShapeDtypeStruct((72, 2, 6, 128), F32),
+        ],
         in_specs=[VM],
         out_specs=[VM] * 3,
         compiler_params=params(8),
@@ -314,21 +394,22 @@
     )(x)
 
 
-def run_traces(ya, own, own_s, tp, h):
+def run_traces(ya, at_right, *inputs):
+    halves = 1 if len(inputs) == 4 else 2
     return pl.pallas_call(
-        trace_kernel,
-        out_shape=jax.ShapeDtypeStruct((16, 16, 128), BF16),
-        in_specs=[SM] + [VM] * 4,
+        functools.partial(trace_kernel, at_right, halves),
+        out_shape=jax.ShapeDtypeStruct((16 * halves, 16, 128), BF16),
+        in_specs=[SM] + [VM] * len(inputs),
         out_specs=VM,
         scratch_shapes=[
-            pltpu.VMEM((72, 3, 24, 128), F32),
-            pltpu.VMEM((72, 2, 8, 128), F32),
-            pltpu.VMEM((256, 128), F32),
+            pltpu.VMEM((72 * halves, 3, 24, 128), F32),
+            pltpu.VMEM((72 * halves, 2, 8, 128), F32),
+            pltpu.VMEM((256 * halves, 128), F32),
         ],
-        compiler_params=params(16),
-        cost_estimate=pl.CostEstimate(flops=8_000_000, bytes_accessed=2_000_000, transcendentals=0),
+        compiler_params=params(8 + 8 * halves),
+        cost_estimate=pl.CostEstimate(flops=8_000_000, bytes_accessed=6_000_000, transcendentals=0),
         name="traces",
-    )(ya, own, own_s, tp, h)
+    )(ya, *inputs)
 
 
 def run_staples(ya, own, own_s, tp, tp_s, h, h_s, co, co_s):
@@ -346,11 +427,12 @@
 
 def run_final(ya, own, staples, f, f_s, w_in, b_in, w_out, b_out, last):
     weights = [pltpu.VMEM((2, 192, 128), F32)]
+    shapes = [(72, 16, 128)] if last else [(72, 2, 8, 128), (36, 6, 128), (36, 6, 128)]
     return pl.pallas_call(
         last_kernel if last else final_kernel,
-        out_shape=jax.ShapeDtypeStruct((72, 16, 128) if last else (72, 2, 8, 128), F32),
+        out_shape=[jax.ShapeDtypeStruct(shape, F32) for shape in shapes],
         in_specs=[SM] + [VM] * 8,
-        out_specs=VM,
+        out_specs=[VM] * len(shapes),
         scratch_shapes=([pltpu.VMEM((72, 2, 8, 128), F32)] if last else []) + weights,
         compiler_params=params(14),
         cost_estimate=pl.CostEstimate(flops=300_000_000, bytes_accessed=4_000_000, transcendentals=131072),
@@ -358,17 +440,22 @@
     )(ya, own, staples, f, f_s, w_in, b_in, w_out, b_out)
 
 
+def run_shift(ya, *arrays):
+    shapes = [(72, 2, 8, 128), (72, 2, 4, 128), (72, 2, 8, 128), (18, 2, 2, 128), (72, 2, 2, 128)]
+    return pl.pallas_call(
+        shift_kernel,
+        out_shape=[jax.ShapeDtypeStruct(shape, F32) for shape in shapes],
+        in_specs=[SM] + [VM] * 7,
+        out_specs=[VM] * 5,
+        compiler_params=params(10),
+        cost_estimate=pl.CostEstimate(flops=8_000_000, bytes_accessed=6_000_000, transcendentals=0),
+        name="shift",
+    )(ya, *arrays)
+
+
 def step(value, axis, by):
     count = lax.axis_size(axis)
     return lax.ppermute(value, axis, [((i + by) % count, i) for i in range(count)])
-
-
-def other_time(value, dim):
-    if lax.axis_size("tm") == 2:
-        return step(value, "tm", 1)
-    up = step(lax.slice_in_dim(value, 0, 1, axis=dim), "tm", 1)
-    down = step(lax.slice_in_dim(value, 1, 2, axis=dim), "tm", -1)
-    return jnp.concatenate([up, down], axis=dim)
 
 
 def diagonal(value, x_by, t_by):
@@ -381,23 +468,17 @@
     return lax.ppermute(value, ("space", "tm"), pairs)
 
 
-def exchange(own, first, last):
-    tp = other_time(own.reshape(72, 2, 4, 2, 128), 3).reshape(own.shape)
-    left = step(last, "space", -1)
-    right = step(first, "space", 1)
-    co_left = diagonal(last[18:36, :, 0:1], -1, 1)
-    co_right = diagonal(first[0:18, :, 1:2], 1, -1)
-    return tp, left, right, co_left, co_right
-
-
-def traces_rim(tr, meanwhile):
-    tp = other_time(tr, 2)
-    full = jnp.concatenate([tp[:, :, 1:2], tr, tp[:, :, 0:1]], axis=2)
-    left = step(full[:, 3:4], "space", -1)
-    right = step(full[:, 0:1], "space", 1)
-    other = meanwhile()
-    left, right, other = lax.optimization_barrier((left, right, other))
-    return jnp.concatenate([left, full, right], axis=1), other
+def other_time(value, dim, x_by=0):
+    if lax.axis_size("tm") == 2:
+        return diagonal(value, x_by, 1)
+    up = diagonal(lax.slice_in_dim(value, 0, 1, axis=dim), x_by, 1)
+    down = diagonal(lax.slice_in_dim(value, 1, 2, axis=dim), x_by, -1)
+    return jnp.concatenate([up, down], axis=dim)
+
+
+def other_rows(value, x_by=0):
+    split = value.reshape(value.shape[:-2] + (value.shape[-2] // 2, 2, 128))
+    return other_time(split, split.ndim - 2, x_by).reshape(value.shape)
 
 
 def active_rows(active_blocks):
@@ -407,41 +488,62 @@
 
 
 def per_device(gauge_links, active_blocks, conv_in, bias_in, conv_out, bias_out):
-    own, first, last = run_unpack(gauge_links.reshape(72, 16, 128))
+    own, last, head = run_unpack(gauge_links.reshape(72, 16, 128))
     ya = active_rows(active_blocks)
     weights = run_weights(conv_in, bias_in, conv_out, bias_out)
-    for layer in range(2):
-        if layer == 1:
-            incoming = step(own[:, :, 0:4], "space", 1)
-            own = jnp.concatenate([own[:, :, 4:8], incoming], axis=2)
-            first, last = own[:, :, 0:2], own[:, :, 6:8]
-        own_s = step(own, "sub", 1)
-        tp, left, right, co_left, co_right = exchange(own, first, last)
-        if layer == 0:
-            left, right, ya, weights = lax.optimization_barrier((left, right, ya, weights))
-            ya = [ya[0], ya[1]]
-        h = jnp.concatenate([left, right], axis=2)
-        co = jnp.concatenate([co_left, co_right], axis=2)
-        h_s = step(h, "sub", 1)
-        co_s = step(co, "sub", 1)
-        tp, h_s, co_s = lax.optimization_barrier((tp, h_s, co_s))
+
+    tp = other_rows(own)
+    head = step(head, "space", 1)
+    left = step(last, "space", -1)
+    own_s = step(own, "sub", 1)
+    head, left, ya, weights = lax.optimization_barrier((head, left, ya, weights))
+    ya = [ya[0], ya[1]]
+    mixed = jnp.concatenate([left[18:36, :, 0:1], head[0:18, :, 1:2]], axis=2)
+    h = jnp.concatenate([left, head[:, :, 0:2]], axis=2)
+    co = other_time(mixed, 2)
+    tr = run_traces(ya[0], 0, own, own_s, tp, head).reshape(2, 4, 2, 16, 128)
+    full = other_traces(tr)
+    full, co, h = lax.optimization_barrier((full, co, h))
+    own, q_head, q_tail = rest(full, own, own_s, tp, h, co, ya[0], weights[:4], False)
+    far = other_rows(head)
+
+    own, h, tp, co, right_tp = run_shift(
+        ya[0],
+        own,
+        head,
+        tp,
+        far,
+        step(q_head, "space", 1),
+        other_rows(q_tail),
+        other_rows(q_head, 1),
+    )
+
+    own_s, tp_s = step(own, "sub", 1), step(tp, "sub", 1)
+    if lax.axis_size("tm") == 2:
+        full = run_traces(ya[1], 2, own, own_s, tp, h, tp_s, right_tp)
+        full = full.reshape(2, 4, 4, 16, 128)
+    else:
+        full = other_traces(run_traces(ya[1], 2, own, own_s, tp, h).reshape(2, 4, 2, 16, 128))
+    (own,) = rest(full, own, own_s, tp, h, co, ya[1], weights[4:], True, tp_s)
+    return own.reshape(4, 18, 2, 4, 2, 128)
+
+
+def other_traces(tr):
+    times = other_time(tr, 2)
+    return jnp.concatenate([times[:, :, 1:2], tr, times[:, :, 0:1]], axis=2)
+
+
+def rest(full, own, own_s, tp, h, co, ya, weights, last, tp_s=None):
+    before = step(full[:, 3:4], "space", -1)
+    after = step(full[:, 0:1], "space", 1)
+    if tp_s is None:
         tp_s = step(tp, "sub", 1)
-        tr = run_traces(ya[layer], own, own_s, tp, h)
-        links = (own, own_s, tp, tp_s, h, h_s, co, co_s)
-        f, staples = traces_rim(
-            tr.reshape(2, 4, 2, 16, 128), lambda: run_staples(ya[layer], *links)
-        )
-        f_s = step(f, "sub", 1)
-        own = run_final(
-            ya[layer],
-            own,
-            staples,
-            f,
-            f_s,
-            *weights[4 * layer : 4 * layer + 4],
-            layer == 1,
-        )
-    return own.reshape(4, 18, 2, 4, 2, 128)
+    h_s, co_s = step(h, "sub", 1), step(co, "sub", 1)
+    staples = run_staples(ya, own, own_s, tp, tp_s, h, h_s, co, co_s)
+    before, after, staples = lax.optimization_barrier((before, after, staples))
+    f = jnp.concatenate([before, full, after], axis=1)
+    f_s = step(f, "sub", 1)
+    return run_final(ya, own, staples, f, f_s, *weights, last)
 
 
 def solution(mesh):

time: 91.7 us -> 71.5 us (0.78)
  waiting for transfers between devices: 36.9 us -> 21.9 us
  starting transfers between devices: 30.9 us -> 23.6 us
  Pallas kernels: 16.7 us -> 19.2 us
  local copies, waits for them, and re-layouts: 5.11 us -> 4.14 us
    ppermute x23 -> x17, waiting for transfers between devices: 30.6 us -> 14.6 us  [step(): lax.ppermute(value, axis, [((i + by) % count, i) for i in range(count)])]
    ppermute x23 -> x17, starting transfers between devices: 23 us -> 15.3 us  [step(): lax.ppermute(value, axis, [((i + by) % count, i) for i in range(count)])]
    pallas_call x4 -> x5, Pallas kernels: 10.6 us -> 13 us  [the longest x2 7.23 us: run_final(): pl.pallas_call(last_kernel if last else final_kernel, out_shape=[jax.Shap...]
    unnamed x8 -> x12, local copies, waits for them, and re-layouts: 4.78 us -> 2.77 us
    ppermute x4 -> x6, waiting for transfers between devices: 6.29 us -> 7.33 us  [diagonal(): return lax.ppermute(value, ('space', 'tm'), pairs)]
    ppermute x4 -> x6, starting transfers between devices: 7.86 us -> 8.25 us  [diagonal(): return lax.ppermute(value, ('space', 'tm'), pairs)]
  transfers between devices with their start and end apart: 27 -> 23, of which waited for: 14 -> 9; matrix products, arithmetic and copies ran while one was open for 4% -> 7% of each run, Pallas kernels for 10% -> 19%
where the time goes in v2:
time: 71.5 us; the launch traced here: 71.3 us
  starting transfers between devices  23.6 us (33%)
  waiting for transfers between devices  21.9 us (31%)
  Pallas kernels  19.2 us (27%)
  local copies, waits for them, and re-layouts  4.14 us (6%)
  other arithmetic  2.16 us (3%)
    ppermute x17, starting transfers between devices, step(): lax.ppermute(value, axis, [((i + by) % count, i) for i in range(count)])  15.3 us
    ppermute x17, waiting for transfers between devices, step(): lax.ppermute(value, axis, [((i + by) % count, i) for i in range(count)])  14.6 us
    ppermute x6, starting transfers between devices, diagonal(): return lax.ppermute(value, ('space', 'tm'), pairs)  8.25 us
    ppermute x6, waiting for transfers between devices, diagonal(): return lax.ppermute(value, ('space', 'tm'), pairs)  7.33 us
    pallas_call x2, Pallas kernels, run_final(): pl.pallas_call(last_kernel if last else final_kernel, out_shape=[jax.Shap...  7.23 us
    pallas_call x2, Pallas kernels, run_staples(): pl.pallas_call(staple_kernel, out_shape=jax.ShapeDtypeStruct((24, 18, 8,...  5.28 us
    pallas_call x2, Pallas kernels, run_traces(): pl.pallas_call(functools.partial(trace_kernel, at_right, halves), out_sha...  4.45 us
    unnamed x12, local copies, waits for them, and re-layouts  2.77 us
  transfers between devices with their start and end apart: 23, of which 9 were waited for; matrix products, arithmetic and copies ran while one was open for 7% of the time, Pallas kernels for 19%

profile of v2, /device:TPU:0, one launch (start us, length us, event | category | flops | bytes accessed | tf_op | source)
XLA Modules:
  0.0 71.3 jit_solution(12867457598210789474)
XLA Ops:
  0.0 1.1 %copy-done = f32[4,18,2,4,2,128]{5,4,3,2,1,0:T(2,128)S(1)} copy-done((f32[4,18,2,4,2,128]{5,4,3,2,1,0:T(2,128)S(1)}, f32[4,18,2,4,2,128]{5,4,3,2,1,0:T(2,128)}, u32[]{:S(2)}) %copy-start) | copy-done | bytes 589848
  1.7 5.1 %collective-permute-start = (f32[72,2,6,128]{3,0,2,1:T(8,128)S(1)}, f32[72,2,6,128]{3,0,2,1:T(8,128)S(1)}, u32[]{:S(2)}, u32[]{:S(2)}) collective-permute-start(f32[72,2,6,128]{3,0,2,1:T(8,128)S(1)} %copy.17), channel_id=1, source_target_pairs={{4,0},{8,4},{12,8},{0,12},{5,1},{9,5},{13,9},{1,13},{6,2},{10,6},{... | collective-permute-start | bytes 1327112 | tf_op jit(solution)/shard_map/ppermute | solution.py:458
  6.8 1.5 %collective-permute-start.3 = (f32[72,2,4,2,128]{4,3,2,1,0:T(2,128)S(1)}, f32[72,2,4,2,128]{4,3,2,1,0:T(2,128)S(1)}, u32[]{:S(2)}, u32[]{:S(2)}) collective-permute-start(f32[72,2,4,2,128]{4,3,2,1,0:T(2,128)S(1)} %bitcast.20), channel_id=1, source_target_pairs={{2,0},{0,2},{6,4},{4,6},{10,8},{8,10},{14,12},{12,14},{3,1},{1,3},... | collective-permute-start | bytes 1769480 | tf_op jit(solution)/shard_map/ppermute | solution.py:468
  8.3 1.6 %copy.18.conv_in = bf16[2,81,12,64]{3,2,1,0:T(8,128)(2,1)S(1)} copy(bf16[2,81,12,64]{1,3,2,0:T(8,128)(2,1)} %param.8) | data formatting | bytes 497664 | tf_op args[2]
  10.4 1.0 %fusion = s32[2,4]{1,0:T(2,128)S(1)} fusion(s32[2,4,2,4,4]{4,3,2,1,0:T(4,128)} %param.7, s32[]{:T(128)S(6)} %select_n.16, s32[]{:T(128)S(6)} %select_n.17, s32[]{:T(128)S(6)} %select_n.18), kind=kLoop, calls=%fused_computation.8 | loop fusion | flops 16 | bytes 76 | tf_op jit(solution)/shard_map/jit(_where)/select_n | solution.py:487
  11.4 9.0 %collective-permute-done.1 = f32[72,2,2,128]{3,2,1,0:T(2,128)} collective-permute-done((f32[72,2,2,128]{3,2,1,0:T(2,128)S(1)}, f32[72,2,2,128]{3,2,1,0:T(2,128)}, u32[]{:S(2)}, u32[]{:S(2)}) %collective-permute-start.1) | collective-permute-done | bytes 147488 | tf_op jit(solution)/shard_map/ppermute | solution.py:458
  20.6 0.8 %slice.37 = f32[18,2,1,128]{3,2,1,0:T(1,128)S(1)} slice(f32[72,2,2,128]{3,2,1,0:T(2,128)} %collective-permute-done.1), slice={[18:36], [0:2], [0:1], [0:128]} | slice | bytes 36864 | tf_op jit(solution)/shard_map/slice | solution.py:501
  21.5 1.6 %collective-permute-start.5 = (f32[18,2,2,128]{3,2,1,0:T(2,128)S(1)}, f32[18,2,2,128]{3,2,1,0:T(2,128)S(1)}, u32[]{:S(2)}, u32[]{:S(2)}) collective-permute-start(f32[18,2,2,128]{3,2,1,0:T(2,128)S(1)} %pad_maximum_fusion.3), channel_id=1, source_target_pairs={{2,0},{0,2},{6,4},{4,6},{10,8},{8,10},{14,12},{12,14},{3,1},{1,3},... | collective-permute-start | bytes 110600 | tf_op jit(solution)/shard_map/ppermute | solution.py:468
  23.0 1.7 %traces.2 = bf16[16,16,128]{2,1,0:T(8,128)(2,1)S(1)} custom-call(s32[4]{0:T(128)S(1)} %get-tuple-element.89.ya, f32[72,2,8,128]{3,2,1,0:T(8,128)S(1)} %get-tuple-element.55.refs_0_.own, f32[72,2,8,128]{3,2,1,0:T(8,128)S(1)} %collective-permute-done.2.refs_1_.own_s, f32[72,2,8,128]{3,2,1,0:T(8,128)S(1)} %bitcast.16, f32[72,2,6,128]{3,2,1,0:T(8,128)S(1)} %copy.20.refs_3_.head), custom_call_target="tpu_custom_call" | custom-call | flops 8000000 | bytes 6000000 | tf_op jit(solution)/shard_map/traces/pallas_call | solution.py:399
  24.7 0.6 collective-permute-start.4
  25.3 1.0 %pad_maximum_fusion.h = f32[72,2,4,128]{3,2,1,0:T(4,128)S(1)} fusion(f32[72,2,2,128]{3,2,1,0:T(2,128)S(1)} %slice.46, f32[72,2,2,128]{3,2,1,0:T(2,128)} %collective-permute-done.1), kind=kLoop, calls=%fused_computation | loop fusion | flops 73728 | bytes 589824 | tf_op jit(solution)/shard_map/concatenate | solution.py:502
  26.4 2.6 %collective-permute-done.4 = bf16[2,4,2,16,128]{4,3,2,1,0:T(8,128)(2,1)S(1)} collective-permute-done((bf16[2,4,2,16,128]{4,3,2,1,0:T(8,128)(2,1)S(1)}, bf16[2,4,2,16,128]{4,3,2,1,0:T(8,128)(2,1)S(1)}, u32[]{:S(2)}, u32[]{:S(2)}) %collective-permute-start.4) | collective-permute-done | bytes 65568 | tf_op jit(solution)/shard_map/ppermute | solution.py:468
  29.2 0.5 collective-permute-start.10
  29.7 1.6 %collective-permute-start.6 = (bf16[2,1,4,16,128]{4,3,2,1,0:T(8,128)(2,1)S(1)}, bf16[2,1,4,16,128]{4,3,2,1,0:T(8,128)(2,1)S(1)}, u32[]{:S(2)}, u32[]{:S(2)}) collective-permute-start(bf16[2,1,4,16,128]{4,3,2,1,0:T(8,128)(2,1)S(1)} %get-tuple-element.86), channel_id=1, source_target_pairs={{12,0},{0,4},{4,8},{8,12},{13,1},{1,5},{5,9},{9,13},{14,2},{2,6},{... | collective-permute-start | bytes 98312 | tf_op jit(solution)/shard_map/ppermute | solution.py:458
  31.3 2.2 %collective-permute-start.7 = (bf16[2,1,4,16,128]{4,3,2,1,0:T(8,128)(2,1)S(1)}, bf16[2,1,4,16,128]{4,3,2,1,0:T(8,128)(2,1)S(1)}, u32[]{:S(2)}, u32[]{:S(2)}) collective-permute-start(bf16[2,1,4,16,128]{4,3,2,1,0:T(8,128)(2,1)S(1)} %get-tuple-element.85), channel_id=1, source_target_pairs={{4,0},{8,4},{12,8},{0,12},{5,1},{9,5},{13,9},{1,13},{6,2},{10,6},{... | collective-permute-start | bytes 98312 | tf_op jit(solution)/shard_map/ppermute | solution.py:458
  33.5 0.5 collective-permute-start.12
  34.0 2.6 %staples.2 = f32[24,18,8,128]{3,2,1,0:T(8,128)S(1)} custom-call(s32[4]{0:T(128)S(1)} %get-tuple-element.89.ya, f32[72,2,8,128]{3,2,1,0:T(8,128)S(1)} %get-tuple-element.55.refs_0_.own, f32[72,2,8,128]{3,2,1,0:T(8,128)S(1)} %collective-permute-done.2.refs_1_.own_s, f32[72,2,8,128]{3,2,1,0:T(8,128)S(1)} %bitcast.18, ...), custom_call_target="tpu_custom_call" | custom-call | flops 20000000 | bytes 16000000 | tf_op jit(solution)/shard_map/staples/pallas_call | solution.py:416
  36.8 1.4 %collective-permute-done.11.f_s = bf16[2,6,4,16,128]{4,3,2,1,0:T(8,128)(2,1)S(1)} collective-permute-done((bf16[2,6,4,16,128]{4,3,2,1,0:T(8,128)(2,1)S(1)}, bf16[2,6,4,16,128]{4,3,2,1,0:T(8,128)(2,1)S(1)}, u32[]{:S(2)}, u32[]{:S(2)}) %collective-permute-start.11) | collective-permute-done | bytes 196640 | tf_op jit(solution)/shard_map/ppermute | solution.py:458
  38.3 3.1 %rotate.2 = (f32[72,2,8,128]{3,2,1,0:T(8,128)S(1)}, f32[36,6,128]{2,1,0:T(8,128)S(1)}, f32[36,6,128]{2,1,0:T(8,128)S(1)}) custom-call(s32[4]{0:T(128)S(1)} %get-tuple-element.89.ya, f32[72,2,8,128]{3,2,1,0:T(8,128)S(1)} %get-tuple-element.55.refs_0_.own, f32[24,18,8,128]{3,2,1,0:T(8,128)S(1)} %staples.2, ...), custom_call_target="tpu_custom_call" | custom-call | flops 300000000 | bytes 4000000 | tf_op jit(solution)/shard_map/rotate/pallas_call | solution.py:431
  41.4 1.6 %collective-permute-start.14 = (f32[36,3,2,128]{3,0,2,1:T(8,128)S(1)}, f32[36,3,2,128]{3,0,2,1:T(8,128)S(1)}, u32[]{:S(2)}, u32[]{:S(2)}) collective-permute-start(f32[36,3,2,128]{3,0,2,1:T(8,128)S(1)} %bitcast.29), channel_id=1, source_target_pairs={{2,0},{0,2},{6,4},{4,6},{10,8},{8,10},{14,12},{12,14},{3,1},{1,3},... | collective-permute-start | bytes 331784 | tf_op jit(solution)/shard_map/ppermute | solution.py:468
  43.0 2.5 %collective-permute-start.15 = (f32[36,3,2,128]{3,0,2,1:T(8,128)S(1)}, f32[36,3,2,128]{3,0,2,1:T(8,128)S(1)}, u32[]{:S(2)}, u32[]{:S(2)}) collective-permute-start(f32[36,3,2,128]{3,0,2,1:T(8,128)S(1)} %bitcast.31), channel_id=1, source_target_pairs={{6,0},{4,2},{10,4},{8,6},{14,8},{12,10},{2,12},{0,14},{7,1},{5,3},... | collective-permute-start | bytes 331784 | tf_op jit(solution)/shard_map/ppermute | solution.py:468
  46.0 4.3 %collective-permute-done.14 = f32[36,3,2,128]{3,0,2,1:T(8,128)S(1)} collective-permute-done((f32[36,3,2,128]{3,0,2,1:T(8,128)S(1)}, f32[36,3,2,128]{3,0,2,1:T(8,128)S(1)}, u32[]{:S(2)}, u32[]{:S(2)}) %collective-permute-start.14) | collective-permute-done | bytes 110624 | tf_op jit(solution)/shard_map/ppermute | solution.py:468
  50.4 0.9 %collective-permute-done.13.q_head = f32[36,6,128]{2,1,0:T(8,128)S(1)} collective-permute-done((f32[36,6,128]{2,1,0:T(8,128)S(1)}, f32[36,6,128]{2,1,0:T(8,128)S(1)}, u32[]{:S(2)}, u32[]{:S(2)}) %collective-permute-start.13) | collective-permute-done | bytes 110624 | tf_op jit(solution)/shard_map/ppermute | solution.py:458
  51.3 1.4 %shift.1 = (f32[72,2,8,128]{3,2,1,0:T(8,128)S(1)}, f32[72,2,4,128]{3,2,1,0:T(4,128)S(1)}, f32[72,2,8,128]{3,2,1,0:T(8,128)S(1)}, f32[18,2,2,128]{3,2,1,0:T(2,128)S(1)}, f32[72,2,2,128]{3,2,1,0:T(2,128)S(1)}) custom-call(s32[4]{0:T(128)S(1)} %get-tuple-element.89.ya, f32[72,2,8,128]{3,2,1,0:T(8,128)S(1)} %get-tuple-element.68.own, ...), custom_call_target="tpu_custom_call" | custom-call | flops 8000000 | bytes 6000000 | tf_op jit(solution)/shard_map/shift/pallas_call | solution.py:445
  52.7 0.5 collective-permute-start.17
  53.8 1.0 %collective-permute-done.16.refs_1_.own_s = f32[72,2,8,128]{3,2,1,0:T(8,128)S(1)} collective-permute-done((f32[72,2,8,128]{3,2,1,0:T(8,128)S(1)}, f32[72,2,8,128]{3,2,1,0:T(8,128)S(1)}, u32[]{:S(2)}, u32[]{:S(2)}) %collective-permute-start.16) | collective-permute-done | bytes 589856 | tf_op jit(solution)/shard_map/ppermute | solution.py:458
  54.7 0.8 %collective-permute-done.17.refs_4_.tp_s = f32[72,2,8,128]{3,2,1,0:T(8,128)S(1)} collective-permute-done((f32[72,2,8,128]{3,2,1,0:T(8,128)S(1)}, f32[72,2,8,128]{3,2,1,0:T(8,128)S(1)}, u32[]{:S(2)}, u32[]{:S(2)}) %collective-permute-start.17) | collective-permute-done | bytes 589856 | tf_op jit(solution)/shard_map/ppermute | solution.py:458
  55.6 2.8 %traces.3 = bf16[32,16,128]{2,1,0:T(8,128)(2,1)S(1)} custom-call(s32[4]{0:T(128)S(1)} %get-tuple-element.90.ya, f32[72,2,8,128]{3,2,1,0:T(8,128)S(1)} %get-tuple-element.71.refs_0_.own, f32[72,2,8,128]{3,2,1,0:T(8,128)S(1)} %collective-permute-done.16.refs_1_.own_s, f32[72,2,8,128]{3,2,1,0:T(8,128)S(1)} %get-tuple-element.72.refs_2_.tp, ...), custom_call_target="tpu_custom_call" | custom-call | flops 8000000 | bytes 6000000 | tf_op jit(solution)/shard_map/traces/pallas_call | solution.py:399
  58.4 4.5 %collective-permute-start.19 = (bf16[2,1,4,16,128]{4,3,2,1,0:T(8,128)(2,1)S(1)}, bf16[2,1,4,16,128]{4,3,2,1,0:T(8,128)(2,1)S(1)}, u32[]{:S(2)}, u32[]{:S(2)}) collective-permute-start(bf16[2,1,4,16,128]{4,3,2,1,0:T(8,128)(2,1)S(1)} %get-tuple-element.83), channel_id=1, source_target_pairs={{4,0},{8,4},{12,8},{0,12},{5,1},{9,5},{13,9},{1,13},{6,2},{10,6},{... | collective-permute-start | bytes 98312 | tf_op jit(solution)/shard_map/ppermute | solution.py:458
  62.9 2.6 %staples.3 = f32[24,18,8,128]{3,2,1,0:T(8,128)S(1)} custom-call(s32[4]{0:T(128)S(1)} %get-tuple-element.90.ya, f32[72,2,8,128]{3,2,1,0:T(8,128)S(1)} %get-tuple-element.71.refs_0_.own, f32[72,2,8,128]{3,2,1,0:T(8,128)S(1)} %collective-permute-done.16.refs_1_.own_s, f32[72,2,8,128]{3,2,1,0:T(8,128)S(1)} %get-tuple-element.72.refs_2_.tp, ...), custom_call_target="tpu_custom_call" | custom-call | flops 20000000 | bytes 16000000 | tf_op jit(solution)/shard_map/staples/pallas_call | solution.py:416
  65.7 1.4 %collective-permute-done.22.f_s = bf16[2,6,4,16,128]{4,3,2,1,0:T(8,128)(2,1)S(1)} collective-permute-done((bf16[2,6,4,16,128]{4,3,2,1,0:T(8,128)(2,1)S(1)}, bf16[2,6,4,16,128]{4,3,2,1,0:T(8,128)(2,1)S(1)}, u32[]{:S(2)}, u32[]{:S(2)}) %collective-permute-start.22) | collective-permute-done | bytes 196640 | tf_op jit(solution)/shard_map/ppermute | solution.py:458
  67.1 4.1 %rotate.3 = f32[72,16,128]{2,1,0:T(8,128)} custom-call(s32[4]{0:T(128)S(1)} %get-tuple-element.90.ya, f32[72,2,8,128]{3,2,1,0:T(8,128)S(1)} %get-tuple-element.71.refs_0_.own, f32[24,18,8,128]{3,2,1,0:T(8,128)S(1)} %staples.3, bf16[2,6,4,16,128]{4,3,2,1,0:T(8,128)(2,1)S(1)} %pad_maximum_fusion.1.f, ...), custom_call_target="tpu_custom_call" | custom-call | flops 300000000 | bytes 4000000 | tf_op jit(solution)/shard_map/rotate/pallas_call | solution.py:431
  (56 shorter events, 3.0 us)
Async XLA Ops:
  0.0 10.0 %copy-start.1 = (f32[2,64]{1,0:T(2,128)S(1)}, f32[2,64]{1,0:T(2,128)}, u32[]{:S(2)}) copy-start(f32[2,64]{1,0:T(2,128)} %bias_in.1) | copy-start | bytes 1540
  0.0 1.1 %copy-start = (f32[4,18,2,4,2,128]{5,4,3,2,1,0:T(2,128)S(1)}, f32[4,18,2,4,2,128]{5,4,3,2,1,0:T(2,128)}, u32[]{:S(2)}) copy-start(f32[4,18,2,4,2,128]{5,4,3,2,1,0:T(2,128)} %param.6) | copy-start | bytes 1769476
  1.1 8.8 %copy-start.3 = (bf16[2,64,24]{1,2,0:T(8,128)(2,1)S(1)}, bf16[2,64,24]{1,2,0:T(8,128)(2,1)}, u32[]{:S(2)}) copy-start(bf16[2,64,24]{1,2,0:T(8,128)(2,1)} %param.10) | copy-start | bytes 18436
  1.1 8.9 %copy-start.2 = (f32[2,24]{1,0:T(2,128)S(1)}, f32[2,24]{1,0:T(2,128)}, u32[]{:S(2)}) copy-start(f32[2,24]{1,0:T(2,128)} %bias_out.1) | copy-start | bytes 580
  1.7 18.7 %collective-permute-start = (f32[72,2,6,128]{3,0,2,1:T(8,128)S(1)}, f32[72,2,6,128]{3,0,2,1:T(8,128)S(1)}, u32[]{:S(2)}, u32[]{:S(2)}) collective-permute-start(f32[72,2,6,128]{3,0,2,1:T(8,128)S(1)} %copy.17), channel_id=1, source_target_pairs={{4,0},{8,4},{12,8},{0,12},{5,1},{9,5},{13,9},{1,13},{6,2},{10,6},{... | collective-permute-start | bytes 1327112 | tf_op jit(solution)/shard_map/ppermute | solution.py:458
  6.8 16.2 %collective-permute-start.3 = (f32[72,2,4,2,128]{4,3,2,1,0:T(2,128)S(1)}, f32[72,2,4,2,128]{4,3,2,1,0:T(2,128)S(1)}, u32[]{:S(2)}, u32[]{:S(2)}) collective-permute-start(f32[72,2,4,2,128]{4,3,2,1,0:T(2,128)S(1)} %bitcast.20), channel_id=1, source_target_pairs={{2,0},{0,2},{6,4},{4,6},{10,8},{8,10},{14,12},{12,14},{3,1},{1,3},... | collective-permute-start | bytes 1769480 | tf_op jit(solution)/shard_map/ppermute | solution.py:468
  8.3 14.7 %collective-permute-start.2 = (f32[72,2,8,128]{3,2,1,0:T(8,128)S(1)}, f32[72,2,8,128]{3,2,1,0:T(8,128)S(1)}, u32[]{:S(2)}, u32[]{:S(2)}) collective-permute-start(f32[72,2,8,128]{3,2,1,0:T(8,128)S(1)} %get-tuple-element.55.refs_0_.own), channel_id=1, source_target_pairs={{1,0},{0,1},{3,2},{2,3},{5,4},{4,5},{7,6},{6,7},{9,8},{8,9},{11,10... | collective-permute-start | bytes 1769480 | tf_op jit(solution)/shard_map/ppermute | solution.py:458
  8.3 12.1 %collective-permute-start.1 = (f32[72,2,2,128]{3,2,1,0:T(2,128)S(1)}, f32[72,2,2,128]{3,2,1,0:T(2,128)}, u32[]{:S(2)}, u32[]{:S(2)}) collective-permute-start(f32[72,2,2,128]{3,2,1,0:T(2,128)S(1)} %get-tuple-element.45), channel_id=1, source_target_pairs={{12,0},{0,4},{4,8},{8,12},{13,1},{1,5},{5,9},{9,13},{14,2},{2,6},{... | collective-permute-start | bytes 442376 | tf_op jit(solution)/shard_map/ppermute | solution.py:458
  21.5 7.6 %collective-permute-start.5 = (f32[18,2,2,128]{3,2,1,0:T(2,128)S(1)}, f32[18,2,2,128]{3,2,1,0:T(2,128)S(1)}, u32[]{:S(2)}, u32[]{:S(2)}) collective-permute-start(f32[18,2,2,128]{3,2,1,0:T(2,128)S(1)} %pad_maximum_fusion.3), channel_id=1, source_target_pairs={{2,0},{0,2},{6,4},{4,6},{10,8},{8,10},{14,12},{12,14},{3,1},{1,3},... | collective-permute-start | bytes 110600 | tf_op jit(solution)/shard_map/ppermute | solution.py:468
  24.7 4.3 %collective-permute-start.4 = (bf16[2,4,2,16,128]{4,3,2,1,0:T(8,128)(2,1)S(1)}, bf16[2,4,2,16,128]{4,3,2,1,0:T(8,128)(2,1)S(1)}, u32[]{:S(2)}, u32[]{:S(2)}) collective-permute-start(bf16[2,4,2,16,128]{4,3,2,1,0:T(8,128)(2,1)S(1)} %bitcast.24), channel_id=1, source_target_pairs={{2,0},{0,2},{6,4},{4,6},{10,8},{8,10},{14,12},{12,14},{3,1},{1,3},... | collective-permute-start | bytes 196616 | tf_op jit(solution)/shard_map/ppermute | solution.py:468
  26.4 7.7 %collective-permute-start.8 = (f32[72,2,8,128]{3,2,1,0:T(8,128)S(1)}, f32[72,2,8,128]{3,2,1,0:T(8,128)S(1)}, u32[]{:S(2)}, u32[]{:S(2)}) collective-permute-start(f32[72,2,8,128]{3,2,1,0:T(8,128)S(1)} %bitcast.17), channel_id=1, source_target_pairs={{1,0},{0,1},{3,2},{2,3},{5,4},{4,5},{7,6},{6,7},{9,8},{8,9},{11,10... | collective-permute-start | bytes 1769480 | tf_op jit(solution)/shard_map/ppermute | solution.py:458
  29.1 4.9 %collective-permute-start.9 = (f32[72,2,4,128]{3,2,1,0:T(4,128)S(1)}, f32[72,2,4,128]{3,2,1,0:T(4,128)S(1)}, u32[]{:S(2)}, u32[]{:S(2)}) collective-permute-start(f32[72,2,4,128]{3,2,1,0:T(4,128)S(1)} %pad_maximum_fusion.h), channel_id=1, source_target_pairs={{1,0},{0,1},{3,2},{2,3},{5,4},{4,5},{7,6},{6,7},{9,8},{8,9},{11,10... | collective-permute-start | bytes 884744 | tf_op jit(solution)/shard_map/ppermute | solution.py:458
  29.2 4.3 %collective-permute-start.10 = (f32[18,2,2,128]{3,2,1,0:T(2,128)S(1)}, f32[18,2,2,128]{3,2,1,0:T(2,128)S(1)}, u32[]{:S(2)}, u32[]{:S(2)}) collective-permute-start(f32[18,2,2,128]{3,2,1,0:T(2,128)S(1)} %collective-permute-done.5.co), channel_id=1, source_target_pairs={{1,0},{0,1},{3,2},{2,3},{5,4},{4,5},{7,6},{6,7},{9,8},{8,9},{11,10... | collective-permute-start | bytes 110600 | tf_op jit(solution)/shard_map/ppermute | solution.py:458
  29.7 7.0 %collective-permute-start.6 = (bf16[2,1,4,16,128]{4,3,2,1,0:T(8,128)(2,1)S(1)}, bf16[2,1,4,16,128]{4,3,2,1,0:T(8,128)(2,1)S(1)}, u32[]{:S(2)}, u32[]{:S(2)}) collective-permute-start(bf16[2,1,4,16,128]{4,3,2,1,0:T(8,128)(2,1)S(1)} %get-tuple-element.86), channel_id=1, source_target_pairs={{12,0},{0,4},{4,8},{8,12},{13,1},{1,5},{5,9},{9,13},{14,2},{2,6},{... | collective-permute-start | bytes 98312 | tf_op jit(solution)/shard_map/ppermute | solution.py:458
  31.3 5.4 %collective-permute-start.7 = (bf16[2,1,4,16,128]{4,3,2,1,0:T(8,128)(2,1)S(1)}, bf16[2,1,4,16,128]{4,3,2,1,0:T(8,128)(2,1)S(1)}, u32[]{:S(2)}, u32[]{:S(2)}) collective-permute-start(bf16[2,1,4,16,128]{4,3,2,1,0:T(8,128)(2,1)S(1)} %get-tuple-element.85), channel_id=1, source_target_pairs={{4,0},{8,4},{12,8},{0,12},{5,1},{9,5},{13,9},{1,13},{6,2},{10,6},{... | collective-permute-start | bytes 98312 | tf_op jit(solution)/shard_map/ppermute | solution.py:458
  33.5 12.4 %collective-permute-start.12 = (f32[72,2,3,2,128]{4,0,3,2,1:T(8,128)S(1)}, f32[72,2,3,2,128]{4,0,3,2,1:T(8,128)S(1)}, u32[]{:S(2)}, u32[]{:S(2)}) collective-permute-start(f32[72,2,3,2,128]{4,0,3,2,1:T(8,128)S(1)} %bitcast.26), channel_id=1, source_target_pairs={{2,0},{0,2},{6,4},{4,6},{10,8},{8,10},{14,12},{12,14},{3,1},{1,3},... | collective-permute-start | bytes 1327112 | tf_op jit(solution)/shard_map/ppermute | solution.py:468
  36.7 1.5 %collective-permute-start.11 = (bf16[2,6,4,16,128]{4,3,2,1,0:T(8,128)(2,1)S(1)}, bf16[2,6,4,16,128]{4,3,2,1,0:T(8,128)(2,1)S(1)}, u32[]{:S(2)}, u32[]{:S(2)}) collective-permute-start(bf16[2,6,4,16,128]{4,3,2,1,0:T(8,128)(2,1)S(1)} %constant_dynamic-update-slice_fusion.f), channel_id=1, source_target_pairs={{1,0},{0,1},{3,2},{2,3},{5,4},{4,5},{7,6},{6,7},{9,8},{8,9},{11,10... | collective-permute-start | bytes 589832 | tf_op jit(solution)/shard_map/ppermute | solution.py:458
  41.4 8.9 %collective-permute-start.14 = (f32[36,3,2,128]{3,0,2,1:T(8,128)S(1)}, f32[36,3,2,128]{3,0,2,1:T(8,128)S(1)}, u32[]{:S(2)}, u32[]{:S(2)}) collective-permute-start(f32[36,3,2,128]{3,0,2,1:T(8,128)S(1)} %bitcast.29), channel_id=1, source_target_pairs={{2,0},{0,2},{6,4},{4,6},{10,8},{8,10},{14,12},{12,14},{3,1},{1,3},... | collective-permute-start | bytes 331784 | tf_op jit(solution)/shard_map/ppermute | solution.py:468
  43.0 7.4 %collective-permute-start.15 = (f32[36,3,2,128]{3,0,2,1:T(8,128)S(1)}, f32[36,3,2,128]{3,0,2,1:T(8,128)S(1)}, u32[]{:S(2)}, u32[]{:S(2)}) collective-permute-start(f32[36,3,2,128]{3,0,2,1:T(8,128)S(1)} %bitcast.31), channel_id=1, source_target_pairs={{6,0},{4,2},{10,4},{8,6},{14,8},{12,10},{2,12},{0,14},{7,1},{5,3},... | collective-permute-start | bytes 331784 | tf_op jit(solution)/shard_map/ppermute | solution.py:468
  45.5 5.8 %collective-permute-start.13 = (f32[36,6,128]{2,1,0:T(8,128)S(1)}, f32[36,6,128]{2,1,0:T(8,128)S(1)}, u32[]{:S(2)}, u32[]{:S(2)}) collective-permute-start(f32[36,6,128]{2,1,0:T(8,128)S(1)} %get-tuple-element.69), channel_id=1, source_target_pairs={{4,0},{8,4},{12,8},{0,12},{5,1},{9,5},{13,9},{1,13},{6,2},{10,6},{... | collective-permute-start | bytes 331784 | tf_op jit(solution)/shard_map/ppermute | solution.py:458
  52.7 2.1 %collective-permute-start.16 = (f32[72,2,8,128]{3,2,1,0:T(8,128)S(1)}, f32[72,2,8,128]{3,2,1,0:T(8,128)S(1)}, u32[]{:S(2)}, u32[]{:S(2)}) collective-permute-start(f32[72,2,8,128]{3,2,1,0:T(8,128)S(1)} %get-tuple-element.71.refs_0_.own), channel_id=1, source_target_pairs={{1,0},{0,1},{3,2},{2,3},{5,4},{4,5},{7,6},{6,7},{9,8},{8,9},{11,10... | collective-permute-start | bytes 1769480 | tf_op jit(solution)/shard_map/ppermute | solution.py:458
  52.7 2.8 %collective-permute-start.17 = (f32[72,2,8,128]{3,2,1,0:T(8,128)S(1)}, f32[72,2,8,128]{3,2,1,0:T(8,128)S(1)}, u32[]{:S(2)}, u32[]{:S(2)}) collective-permute-start(f32[72,2,8,128]{3,2,1,0:T(8,128)S(1)} %get-tuple-element.72.refs_2_.tp), channel_id=1, source_target_pairs={{1,0},{0,1},{3,2},{2,3},{5,4},{4,5},{7,6},{6,7},{9,8},{8,9},{11,10... | collective-permute-start | bytes 1769480 | tf_op jit(solution)/shard_map/ppermute | solution.py:458
  53.2 9.7 %collective-permute-start.20 = (f32[72,2,4,128]{3,2,1,0:T(4,128)S(1)}, f32[72,2,4,128]{3,2,1,0:T(4,128)S(1)}, u32[]{:S(2)}, u32[]{:S(2)}) collective-permute-start(f32[72,2,4,128]{3,2,1,0:T(4,128)S(1)} %get-tuple-element.73.refs_3_.h), channel_id=1, source_target_pairs={{1,0},{0,1},{3,2},{2,3},{5,4},{4,5},{7,6},{6,7},{9,8},{8,9},{11,10... | collective-permute-start | bytes 884744 | tf_op jit(solution)/shard_map/ppermute | solution.py:458
  53.3 9.6 %collective-permute-start.21 = (f32[18,2,2,128]{3,2,1,0:T(2,128)S(1)}, f32[18,2,2,128]{3,2,1,0:T(2,128)S(1)}, u32[]{:S(2)}, u32[]{:S(2)}) collective-permute-start(f32[18,2,2,128]{3,2,1,0:T(2,128)S(1)} %get-tuple-element.75.co), channel_id=1, source_target_pairs={{1,0},{0,1},{3,2},{2,3},{5,4},{4,5},{7,6},{6,7},{9,8},{8,9},{11,10... | collective-permute-start | bytes 110600 | tf_op jit(solution)/shard_map/ppermute | solution.py:458
  58.4 7.2 %collective-permute-start.18 = (bf16[2,1,4,16,128]{4,3,2,1,0:T(8,128)(2,1)S(1)}, bf16[2,1,4,16,128]{4,3,2,1,0:T(8,128)(2,1)S(1)}, u32[]{:S(2)}, u32[]{:S(2)}) collective-permute-start(bf16[2,1,4,16,128]{4,3,2,1,0:T(8,128)(2,1)S(1)} %get-tuple-element.84), channel_id=1, source_target_pairs={{12,0},{0,4},{4,8},{8,12},{13,1},{1,5},{5,9},{9,13},{14,2},{2,6},{... | collective-permute-start | bytes 98312 | tf_op jit(solution)/shard_map/ppermute | solution.py:458
  58.4 7.1 %collective-permute-start.19 = (bf16[2,1,4,16,128]{4,3,2,1,0:T(8,128)(2,1)S(1)}, bf16[2,1,4,16,128]{4,3,2,1,0:T(8,128)(2,1)S(1)}, u32[]{:S(2)}, u32[]{:S(2)}) collective-permute-start(bf16[2,1,4,16,128]{4,3,2,1,0:T(8,128)(2,1)S(1)} %get-tuple-element.83), channel_id=1, source_target_pairs={{4,0},{8,4},{12,8},{0,12},{5,1},{9,5},{13,9},{1,13},{6,2},{10,6},{... | collective-permute-start | bytes 98312 | tf_op jit(solution)/shard_map/ppermute | solution.py:458
  65.6 1.5 %collective-permute-start.22 = (bf16[2,6,4,16,128]{4,3,2,1,0:T(8,128)(2,1)S(1)}, bf16[2,6,4,16,128]{4,3,2,1,0:T(8,128)(2,1)S(1)}, u32[]{:S(2)}, u32[]{:S(2)}) collective-permute-start(bf16[2,6,4,16,128]{4,3,2,1,0:T(8,128)(2,1)S(1)} %pad_maximum_fusion.1.f), channel_id=1, source_target_pairs={{1,0},{0,1},{3,2},{2,3},{5,4},{4,5},{7,6},{6,7},{9,8},{8,9},{11,10... | collective-permute-start | bytes 589832 | tf_op jit(solution)/shard_map/ppermute | solution.py:458

commit v3 on v2

--- a/solution.py
+++ b/solution.py
@@ -58,88 +58,108 @@
     return pltpu.roll(value, (-step) % value.shape[-1], value.ndim - 1)
 
 
-def trace_kernel(at_right, halves, ya, *refs):
-    inputs, (out, v0, vup, trs) = refs[:-4], refs[-4:]
-    if halves == 1:
-        own, own_s, tp, right = inputs
-        parts = [(own, own_s, tp, right, at_right)]
+def trace_kernel(mode, ya, *refs):
+    if mode == "single":
+        own, own_s, tp, right, out, trs, placed = refs
+
+        def place(i, _):
+            for y in range(2):
+                placed[i, y, 6:8] = right[i, y]
+            return 0
+
+        lax.fori_loop(0, 72, place, 0, unroll=8)
     else:
-        own, own_s, tp, right, tp_s, right_tp = inputs
-        parts = [(own, own_s, tp, right, at_right), (tp, tp_s, own, right_tp, 0)]
-    even = lax.broadcasted_iota(jnp.int32, (8, 128), 0) % 2 == 0
-    count = 16 * halves
-
-    def prep(i, _):
-        for half, (link, link_s, later, after, at) in enumerate(parts):
-            k = 72 * half + i
-            for y in range(2):
-                o = link[i, y]
-                t = later[i, y]
-                v0[k, y, BASE : BASE + 8] = o
-                v0[k, y, BASE + 8 : BASE + 10] = after[i, y, at : at + 2]
-                vup[k, y] = jnp.where(even, pltpu.roll(o, 7, 0), pltpu.roll(t, 1, 0))
-            v0[k, 2, BASE : BASE + 8] = link_s[i, 0]
-        return 0
-
-    lax.fori_loop(0, 72, prep, 0, unroll=4)
+        packs, ex, out, trs = refs[:3], refs[3], refs[4], refs[5]
+    wide = mode == "wide"
+    parts = 3 if wide else 1
+    count = 16 * parts
+    row_of = lax.broadcasted_iota(jnp.int32, (8, 128), 0)
+    even = row_of % 2 == 0
+
+    def links(part, y, i):
+        if mode == "single":
+            return own_s[i, 0] if y == 2 else (own, tp)[part][i, y]
+        return packs[y][72 * part + i]
+
+    def later(part, y, i):
+        o = links(part, y, i)
+        t = pltpu.roll(o, 4, 0) if part == 2 else links(1 - part, y, i)
+        return jnp.where(even, pltpu.roll(o, 7, 0), pltpu.roll(t, 1, 0))
+
+    def right_of(part, y, i):
+        if part == 2:
+            return ex[i, y]
+        if mode == "single":
+            after = placed[i, y]
+        else:
+            after = links(2, y, i)
+            after = pltpu.roll(after, 4, 0) if part == 0 else after
+        return jnp.where(row_of < 6, pltpu.roll(links(part, y, i), 6, 0), after)
+
     trs[12 * count :] = jnp.zeros((4 * count, 128), F32)
-    row_of = lax.broadcasted_iota(jnp.int32, (8, 128), 0)
-    leaves = (row_of % 2, jnp.where(row_of >= 6, 1, 0), 1, 0)
-
-    def at_y(place, _):
-        half, y = place // 2, place % 2
-        active = [jnp.where(ya[m] == y, 1, 0) ^ half for m in range(4)]
-        first = 72 * half
-
-        def look(d, step):
-            base = first + 18 * d
-            if step == 0:
-                parts = [vup[base + c, y] for c in range(18)]
-            elif step == 1:
-                parts = [v0[base + c, y, BASE + 2 : BASE + 10] for c in range(18)]
-            elif step == 2:
-                parts = [v0[base + c, y + 1, BASE : BASE + 8] for c in range(18)]
+    for part in range(parts):
+        inner = jnp.where(row_of >= 6, 1, 0)
+        leaves = (row_of % 2, 1 - row_of // 2 % 2 if part == 2 else inner, 1, 0)
+        flip = jnp.where(row_of < 4, 1, 0) if part == 2 else part
+        for y in range(2):
+            active = [jnp.where(ya[m] == y, 1, 0) ^ flip for m in range(4)]
+
+            def look(d, step):
+                at = range(18 * d, 18 * d + 18)
+                if step == 0:
+                    return as_matrix([later(part, y, i) for i in at])
+                if step == 1:
+                    return as_matrix([right_of(part, y, i) for i in at])
+                if step == 2:
+                    return as_matrix([links(part, y + 1, i) for i in at])
+                values = [links(part, y, i) for i in at]
+                return as_matrix([zroll(v, 1) for v in values] if step == 3 else values)
+
+            for p, (m, n) in enumerate(PAIRS):
+                a = flat(mm(look(m, None), look(n, m)))
+                b = flat(mm(look(n, None), look(m, n)))
+                re = im = None
+                for k in range(9):
+                    r = a[k] * b[k] + a[9 + k] * b[9 + k]
+                    q = a[9 + k] * b[k] - a[k] * b[9 + k]
+                    re = r if re is None else re + r
+                    im = q if im is None else im + q
+                moved = (active[n] ^ leaves[m]) | (active[m] ^ leaves[n]) | active[m] | active[n]
+                frozen = jnp.broadcast_to(moved, (8, 128)) == 0
+                for k, value in enumerate((re, im)):
+                    row = (2 * p + k) * count + 16 * part + 8 * y
+                    trs[row : row + 8] = jnp.where(frozen, value * (1.0 / 3.0), 0.0)
+    for r in range(count):
+        place = r
+        if wide:
+            part, y, row = r // 16, r // 8 % 2, r % 8
+            if part < 2:
+                partner, x = part, 1 + row // 2
             else:
-                parts = [v0[base + c, y, BASE : BASE + 8] for c in range(18)]
-                if step == 3:
-                    parts = [zroll(p, 1) for p in parts]
-            return as_matrix(parts)
-
-        for p, (m, n) in enumerate(PAIRS):
-            a = flat(mm(look(m, None), look(n, m)))
-            b = flat(mm(look(n, None), look(m, n)))
-            re = im = None
-            for k in range(9):
-                r = a[k] * b[k] + a[9 + k] * b[9 + k]
-                q = a[9 + k] * b[k] - a[k] * b[9 + k]
-                re = r if re is None else re + r
-                im = q if im is None else im + q
-            moved = (active[n] ^ leaves[m]) | (active[m] ^ leaves[n]) | active[m] | active[n]
-            frozen = jnp.broadcast_to(moved, (8, 128)) == 0
-            row = pl.multiple_of(place * 8, 8)
-            trs[pl.ds((2 * p) * count + row, 8)] = jnp.where(frozen, re * (1.0 / 3.0), 0.0)
-            trs[pl.ds((2 * p + 1) * count + row, 8)] = jnp.where(frozen, im * (1.0 / 3.0), 0.0)
-        return 0
-
-    lax.fori_loop(0, 2 * halves, at_y, 0)
-    for r in range(count):
-        half, yx, t = r // 16, r % 16 // 2, r % 2
-        place = r if halves == 1 else 4 * yx + ((3, 0)[t] if half else 1 + t)
+                partner, x = row // 4, (0, 5)[row // 2 % 2]
+            t = (3, 0)[row % 2] if partner else 1 + row % 2
+            place = (6 * y + x) * 4 + t
         out[place] = trs[pl.ds(r, 16, stride=count), :].astype(BF16)
 
 
-def staple_kernel(ya, own, own_s, tp, tp_s, h, h_s, co, co_s, out, v0, vup, vdn):
+def staple_kernel(mode, ya, *refs):
+    inputs, (out, v0, vup, vdn) = refs[:-4], refs[-4:]
     even = lax.broadcasted_iota(jnp.int32, (8, 128), 0) % 2 == 0
     places = ((1, 1), (0, 0), (0, 1), (1, 0))
+    if mode == "single":
+        own, own_s, tp, tp_s, h, h_s, co, co_s = inputs
 
     def prep(i, _):
         for y, (other, at) in enumerate(places):
-            o = (own, own_s)[other][i, at]
-            t = (tp, tp_s)[other][i, at]
-            hh = (h, h_s)[other]
+            if mode == "single":
+                o, t = (own, own_s)[other][i, at], (tp, tp_s)[other][i, at]
+                hh = (h, h_s)[other][i, at]
+            else:
+                pack = inputs[2 * other + at]
+                o, t, hh = pack[i], pack[72 + i], pack[144 + i]
             v0[i, y, BASE : BASE + 8] = o
-            v0[i, y, BASE - 2 : BASE] = hh[i, at, 0:2]
-            v0[i, y, BASE + 8 : BASE + 10] = hh[i, at, 2:4]
+            v0[i, y, BASE - 2 : BASE] = hh[0:2]
+            v0[i, y, BASE + 8 : BASE + 10] = hh[2:4]
             vup[i, y, BASE : BASE + 8] = jnp.where(even, pltpu.roll(o, 7, 0), pltpu.roll(t, 1, 0))
             vdn[i, y, BASE : BASE + 8] = jnp.where(even, pltpu.roll(t, 7, 0), pltpu.roll(o, 1, 0))
         return 0
@@ -148,11 +168,18 @@
 
     def corner(c, _):
         for y, (other, at) in enumerate(places):
-            hh, cc = (h, h_s)[other], (co, co_s)[other]
-            vup[18 + c, y, BASE - 2 : BASE - 1] = hh[18 + c, at, 1:2]
-            vup[18 + c, y, BASE - 1 : BASE] = cc[c, at, 0:1]
-            vdn[c, y, BASE + 8 : BASE + 9] = cc[c, at, 1:2]
-            vdn[c, y, BASE + 9 : BASE + 10] = hh[c, at, 2:3]
+            if mode == "single":
+                hh, cc = (h, h_s)[other], (co, co_s)[other]
+                x_links = hh[18 + c, at, 1:2], cc[c, at, 0:1]
+                t_links = cc[c, at, 1:2], hh[c, at, 2:3]
+            else:
+                pack = inputs[2 * other + at]
+                x_links = pack[162 + c, 1:2], pack[162 + c, 4:5]
+                t_links = pack[144 + c, 7:8], pack[144 + c, 2:3]
+            vup[18 + c, y, BASE - 2 : BASE - 1] = x_links[0]
+            vup[18 + c, y, BASE - 1 : BASE] = x_links[1]
+            vdn[c, y, BASE + 8 : BASE + 9] = t_links[0]
+            vdn[c, y, BASE + 9 : BASE + 10] = t_links[1]
         return 0
 
     lax.fori_loop(0, 18, corner, 0, unroll=2)
@@ -183,13 +210,24 @@
                 out[6 * m + 2 * j + 1, c] = value
 
 
-def unpack_kernel(x, own, last, head):
+def unpack_kernel(x, own, *rows):
     def body(i, _):
         for y in range(2):
             for t in range(2):
-                own[i, y, pl.ds(t, 4, stride=2)] = x[i, pl.ds(8 * t + y, 4, stride=2)]
-                head[i, y, pl.ds(t, 3, stride=2)] = x[i, pl.ds(8 * t + y, 3, stride=2)]
-                last[i, y, t : t + 1] = x[i, 8 * t + 6 + y : 8 * t + 7 + y]
+                at = 8 * t + y
+                own[i, y, pl.ds(t, 4, stride=2)] = x[i, pl.ds(at, 4, stride=2)]
+                if rows:
+                    rows[0][i, y, t : t + 1] = x[i, at : at + 1]
+                    rows[1][i, y, t : t + 1] = x[i, at + 6 : at + 7]
+        return 0
+
+    lax.fori_loop(0, 72, body, 0, unroll=8)
+
+
+def tail_kernel(own, tail):
+    def body(i, _):
+        for y in range(2):
+            tail[i, y] = own[i, y, 2:8]
         return 0
 
     lax.fori_loop(0, 72, body, 0, unroll=8)
@@ -225,12 +263,8 @@
     lax.fori_loop(0, 72, body, 0, unroll=8)
 
 
-def final_kernel(
-    ya, own, staples, f, f_s, w_in, b_in, w_out, b_out, out, q_head, q_tail, wts
-):
-    update(
-        ya, own, staples, f, f_s, w_in, b_in, w_out, b_out, out, wts, sent=(q_head, q_tail)
-    )
+def final_kernel(ya, own, staples, f, f_s, w_in, b_in, w_out, b_out, out, sent, wts):
+    update(ya, own, staples, f, f_s, w_in, b_in, w_out, b_out, out, wts, sent)
 
 
 def update(ya, own, staples, f, f_s, w_in, b_in, w_out, b_out, out, wts, sent=None):
@@ -275,8 +309,7 @@
         low += [-0.5 * (aim[i][i] - trace_im) for i in range(3)]
         if sent is not None:
             for c in range(9):
-                sent[0][9 * m + c] = low[c][0:6]
-                sent[1][9 * m + c] = low[c][2:8]
+                sent[9 * m + c] = low[c]
         for c, value in enumerate(rotated(low, link)):
             out[18 * m + c, y] = value
         for c in range(18):
@@ -320,40 +353,50 @@
     return real + imag
 
 
-def shift_kernel(ya, own, head, tp, far, q_head, q_tp, q_far, own_o, h_o, tp_o, co_o, right_tp_o):
+def shift_kernel(
+    ya, own, right, tail, tp, far, far_tail, q_next, q_tp, q_far, own_o, pack_0, pack_1, ex
+):
     for m in range(4):
         here = ya[m]
         there = 1 - here
-        rows = slice(18 * m, 18 * m + 18)
+        at = [18 * m + c for c in range(18)]
 
         def turn(q, links):
             return rotated([q[9 * m + c] for c in range(9)], as_matrix(links))
 
-        new = turn(q_head, [head[i, there] for i in range(rows.start, rows.stop)])
-        for c, i in enumerate(range(rows.start, rows.stop)):
-            for y in range(2):
-                own_o[i, y, 0:4] = own[i, y, 4:8]
-                h_o[i, y, 0:2] = own[i, y, 2:4]
-            own_o[i, there, 4:8] = new[c][0:4]
-            h_o[i, there, 2:4] = new[c][4:6]
-            own_o[i, here, 4:8] = head[i, here, 0:4]
-            h_o[i, here, 2:4] = head[i, here, 4:6]
-        new = turn(q_tp, [tp[i, there, 2:8] for i in range(rows.start, rows.stop)])
-        for c, i in enumerate(range(rows.start, rows.stop)):
-            tp_o[i, there, 0:4] = new[c][2:6]
-            tp_o[i, here, 0:4] = tp[i, here, 4:8]
-            if m == 1:
-                co_o[c, there, 0:1] = new[c][0:1]
-                co_o[c, here, 0:1] = tp[i, here, 2:3]
-        new = turn(q_far, [far[i, here] for i in range(rows.start, rows.stop)])
-        for c, i in enumerate(range(rows.start, rows.stop)):
-            tp_o[i, here, 4:8] = new[c][0:4]
-            tp_o[i, there, 4:8] = far[i, there, 0:4]
-            right_tp_o[i, here] = new[c][4:6]
-            right_tp_o[i, there] = far[i, there, 4:6]
-            if m == 0:
-                co_o[c, here, 1:2] = new[c][5:6]
-                co_o[c, there, 1:2] = far[i, there, 5:6]
+        def joined(one, more, y):
+            return [jnp.concatenate([one[i, y], more[i, y]], axis=0) for i in at]
+
+        at_0 = here == 0
+
+        def by_y(i, if_here, if_there):
+            return (
+                (pack_0, jnp.where(at_0, if_here, if_there)),
+                (pack_1, jnp.where(at_0, if_there, if_here)),
+            )
+
+        new, old = turn(q_next, joined(right, tail, there)), joined(right, tail, here)
+        for c, i in enumerate(at):
+            for y, (pack, rows) in enumerate(by_y(i, old[c], new[c])):
+                block = jnp.concatenate([own[i, y, 4:8], rows[0:4]], axis=0)
+                own_o[i, y] = block
+                pack[i] = block
+                pack[144 + i, 0:2] = own[i, y, 2:4]
+                pack[144 + i, 2:4] = rows[4:6]
+                ex[i, y, 0:2] = own[i, y, 4:6]
+                ex[i, y, 2:4] = rows[6:8]
+        new, old = turn(q_tp, [tp[i, there] for i in at]), [tp[i, here] for i in at]
+        for c, i in enumerate(at):
+            for y, (pack, rows) in enumerate(by_y(i, old[c], new[c])):
+                pack[72 + i, 0:4] = rows[4:8]
+                pack[144 + i, 4:6] = rows[2:4]
+                ex[i, y, 4:6] = rows[4:6]
+        new, old = turn(q_far, joined(far, far_tail, here)), joined(far, far_tail, there)
+        for c, i in enumerate(at):
+            for y, (pack, rows) in enumerate(by_y(i, new[c], old[c])):
+                pack[72 + i, 4:8] = rows[0:4]
+                pack[144 + i, 6:8] = rows[4:6]
+                ex[i, y, 6:8] = rows[6:8]
 
 
 VM = pl.BlockSpec(memory_space=pltpu.VMEM)
@@ -378,56 +421,64 @@
     )(conv_in, bias_in, conv_out, bias_out)
 
 
-def run_unpack(x):
+def run_unpack(x, rows):
+    lengths = (8, 2, 2) if rows else (8,)
     return pl.pallas_call(
         unpack_kernel,
-        out_shape=[
-            jax.ShapeDtypeStruct((72, 2, 8, 128), F32),
-            jax.ShapeDtypeStruct((72, 2, 2, 128), F32),
-            jax.ShapeDtypeStruct((72, 2, 6, 128), F32),
-        ],
+        out_shape=[jax.ShapeDtypeStruct((72, 2, n, 128), F32) for n in lengths],
         in_specs=[VM],
-        out_specs=[VM] * 3,
+        out_specs=[VM] * len(lengths),
         compiler_params=params(8),
         cost_estimate=pl.CostEstimate(flops=0, bytes_accessed=2_000_000, transcendentals=0),
         name="unpack",
-    )(x)
-
-
-def run_traces(ya, at_right, *inputs):
-    halves = 1 if len(inputs) == 4 else 2
+    )(x.reshape(72, 16, 128))
+
+
+def run_tail(own):
     return pl.pallas_call(
-        functools.partial(trace_kernel, at_right, halves),
-        out_shape=jax.ShapeDtypeStruct((16 * halves, 16, 128), BF16),
+        tail_kernel,
+        out_shape=jax.ShapeDtypeStruct((72, 2, 6, 128), F32),
+        in_specs=[VM],
+        out_specs=VM,
+        compiler_params=params(8),
+        cost_estimate=pl.CostEstimate(flops=0, bytes_accessed=1_000_000, transcendentals=0),
+        name="tail",
+    )(own)
+
+
+def run_traces(mode, ya, *inputs):
+    parts = 3 if mode == "wide" else 1
+    placed = [pltpu.VMEM((72, 2, 8, 128), F32)] if mode == "single" else []
+    return pl.pallas_call(
+        functools.partial(trace_kernel, mode),
+        out_shape=jax.ShapeDtypeStruct((16 * parts, 16, 128), BF16),
         in_specs=[SM] + [VM] * len(inputs),
         out_specs=VM,
-        scratch_shapes=[
-            pltpu.VMEM((72 * halves, 3, 24, 128), F32),
-            pltpu.VMEM((72 * halves, 2, 8, 128), F32),
-            pltpu.VMEM((256 * halves, 128), F32),
-        ],
-        compiler_params=params(8 + 8 * halves),
+        scratch_shapes=[pltpu.VMEM((256 * parts, 128), F32)] + placed,
+        compiler_params=params(10),
         cost_estimate=pl.CostEstimate(flops=8_000_000, bytes_accessed=6_000_000, transcendentals=0),
         name="traces",
     )(ya, *inputs)
 
 
-def run_staples(ya, own, own_s, tp, tp_s, h, h_s, co, co_s):
+def run_staples(mode, ya, *inputs):
     return pl.pallas_call(
-        staple_kernel,
+        functools.partial(staple_kernel, mode),
         out_shape=jax.ShapeDtypeStruct((24, 18, 8, 128), F32),
-        in_specs=[SM] + [VM] * 8,
+        in_specs=[SM] + [VM] * len(inputs),
         out_specs=VM,
         scratch_shapes=[pltpu.VMEM((72, 4, 24, 128), F32)] * 3,
         compiler_params=params(22),
-        cost_estimate=pl.CostEstimate(flops=20_000_000, bytes_accessed=16_000_000, transcendentals=0),
+        cost_estimate=pl.CostEstimate(
+            flops=20_000_000, bytes_accessed=16_000_000, transcendentals=0
+        ),
         name="staples",
-    )(ya, own, own_s, tp, tp_s, h, h_s, co, co_s)
+    )(ya, *inputs)
 
 
 def run_final(ya, own, staples, f, f_s, w_in, b_in, w_out, b_out, last):
     weights = [pltpu.VMEM((2, 192, 128), F32)]
-    shapes = [(72, 16, 128)] if last else [(72, 2, 8, 128), (36, 6, 128), (36, 6, 128)]
+    shapes = [(72, 16, 128)] if last else [(72, 2, 8, 128), (36, 8, 128)]
     return pl.pallas_call(
         last_kernel if last else final_kernel,
         out_shape=[jax.ShapeDtypeStruct(shape, F32) for shape in shapes],
@@ -441,13 +492,13 @@
 
 
 def run_shift(ya, *arrays):
-    shapes = [(72, 2, 8, 128), (72, 2, 4, 128), (72, 2, 8, 128), (18, 2, 2, 128), (72, 2, 2, 128)]
+    block, pack = (72, 2, 8, 128), (216, 8, 128)
     return pl.pallas_call(
         shift_kernel,
-        out_shape=[jax.ShapeDtypeStruct(shape, F32) for shape in shapes],
-        in_specs=[SM] + [VM] * 7,
-        out_specs=[VM] * 5,
-        compiler_params=params(10),
+        out_shape=[jax.ShapeDtypeStruct(shape, F32) for shape in (block, pack, pack, block)],
+        in_specs=[SM] + [VM] * 9,
+        out_specs=[VM] * 4,
+        compiler_params=params(12),
         cost_estimate=pl.CostEstimate(flops=8_000_000, bytes_accessed=6_000_000, transcendentals=0),
         name="shift",
     )(ya, *arrays)
@@ -488,44 +539,61 @@
 
 
 def per_device(gauge_links, active_blocks, conv_in, bias_in, conv_out, bias_out):
-    own, last, head = run_unpack(gauge_links.reshape(72, 16, 128))
+    tp_raw = other_time(gauge_links, 2)
+    own, first, last = run_unpack(gauge_links, True)
     ya = active_rows(active_blocks)
     weights = run_weights(conv_in, bias_in, conv_out, bias_out)
 
-    tp = other_rows(own)
-    head = step(head, "space", 1)
+    right = step(first, "space", 1)
     left = step(last, "space", -1)
+    tail = step(run_tail(own), "space", 1)
     own_s = step(own, "sub", 1)
-    head, left, ya, weights = lax.optimization_barrier((head, left, ya, weights))
+    right, left, ya, weights = lax.optimization_barrier((right, left, ya, weights))
     ya = [ya[0], ya[1]]
-    mixed = jnp.concatenate([left[18:36, :, 0:1], head[0:18, :, 1:2]], axis=2)
-    h = jnp.concatenate([left, head[:, :, 0:2]], axis=2)
+    mixed = jnp.concatenate([left[18:36, :, 0:1], right[0:18, :, 1:2]], axis=2)
     co = other_time(mixed, 2)
-    tr = run_traces(ya[0], 0, own, own_s, tp, head).reshape(2, 4, 2, 16, 128)
+    h = jnp.concatenate([left, right], axis=2)
+    h_s = step(h, "sub", 1)
+    (tp,) = run_unpack(tp_raw, False)
+    tr = run_traces("single", ya[0], own, own_s, tp, right).reshape(2, 4, 2, 16, 128)
+    far = other_rows(right)
     full = other_traces(tr)
-    full, co, h = lax.optimization_barrier((full, co, h))
-    own, q_head, q_tail = rest(full, own, own_s, tp, h, co, ya[0], weights[:4], False)
-    far = other_rows(head)
-
-    own, h, tp, co, right_tp = run_shift(
+    full, co, far, tail = lax.optimization_barrier((full, co, far, tail))
+    far_tail = other_rows(tail)
+    tp_s, co_s = step(tp, "sub", 1), step(co, "sub", 1)
+    f, staples = rim(
+        full, lambda: run_staples("single", ya[0], own, own_s, tp, tp_s, h, h_s, co, co_s)
+    )
+    f_s = step(f, "sub", 1)
+    own, q = run_final(ya[0], own, staples, f, f_s, *weights[:4], False)
+
+    own, pack_0, pack_1, ex = run_shift(
         ya[0],
         own,
-        head,
+        right,
+        tail,
         tp,
         far,
-        step(q_head, "space", 1),
-        other_rows(q_tail),
-        other_rows(q_head, 1),
+        far_tail,
+        step(q, "space", 1),
+        other_rows(q),
+        other_rows(q, 1),
     )
 
-    own_s, tp_s = step(own, "sub", 1), step(tp, "sub", 1)
+    other_0, other_1 = step(pack_0, "sub", 1), step(pack_1, "sub", 1)
+
+    def staples_1():
+        return run_staples("packs", ya[1], pack_0, pack_1, other_0, other_1)
+
     if lax.axis_size("tm") == 2:
-        full = run_traces(ya[1], 2, own, own_s, tp, h, tp_s, right_tp)
-        full = full.reshape(2, 4, 4, 16, 128)
+        f = run_traces("wide", ya[1], pack_0, pack_1, other_0, ex).reshape(2, 6, 4, 16, 128)
+        staples = staples_1()
     else:
-        full = other_traces(run_traces(ya[1], 2, own, own_s, tp, h).reshape(2, 4, 2, 16, 128))
-    (own,) = rest(full, own, own_s, tp, h, co, ya[1], weights[4:], True, tp_s)
-    return own.reshape(4, 18, 2, 4, 2, 128)
+        tr = run_traces("packs", ya[1], pack_0, pack_1, other_0, ex).reshape(2, 4, 2, 16, 128)
+        f, staples = rim(other_traces(tr), staples_1)
+    f_s = step(f, "sub", 1)
+    (out,) = run_final(ya[1], own, staples, f, f_s, *weights[4:], True)
+    return out.reshape(4, 18, 2, 4, 2, 128)
 
 
 def other_traces(tr):
@@ -533,17 +601,12 @@
     return jnp.concatenate([times[:, :, 1:2], tr, times[:, :, 0:1]], axis=2)
 
 
-def rest(full, own, own_s, tp, h, co, ya, weights, last, tp_s=None):
+def rim(full, meanwhile):
     before = step(full[:, 3:4], "space", -1)
     after = step(full[:, 0:1], "space", 1)
-    if tp_s is None:
-        tp_s = step(tp, "sub", 1)
-    h_s, co_s = step(h, "sub", 1), step(co, "sub", 1)
-    staples = run_staples(ya, own, own_s, tp, tp_s, h, h_s, co, co_s)
-    before, after, staples = lax.optimization_barrier((before, after, staples))
-    f = jnp.concatenate([before, full, after], axis=1)
-    f_s = step(f, "sub", 1)
-    return run_final(ya, own, staples, f, f_s, *weights, last)
+    other = meanwhile()
+    before, after, other = lax.optimization_barrier((before, after, other))
+    return jnp.concatenate([before, full, after], axis=1), other
 
 
 def solution(mesh):

time: 71.5 us -> 63.9 us (0.89)
  waiting for transfers between devices: 21.9 us -> 16.8 us
  starting transfers between devices: 23.6 us -> 21.4 us
  other arithmetic: 2.16 us -> 1.22 us
  Pallas kernels: 19.2 us -> 20 us
    ppermute x17 -> x14, waiting for transfers between devices: 14.6 us -> 6.42 us  [step(): lax.ppermute(value, axis, [((i + by) % count, i) for i in range(count)])]
    ppermute x6 -> x7, waiting for transfers between devices: 7.33 us -> 10.4 us  [diagonal(): return lax.ppermute(value, ('space', 'tm'), pairs)]
    ppermute x17 -> x14, starting transfers between devices: 15.3 us -> 12.3 us  [step(): lax.ppermute(value, axis, [((i + by) % count, i) for i in range(count)])]
    concatenate x3 -> x2, other arithmetic: 1.11 us -> 0.17 us  [the longest x1 0.14 us: per_device(): h = jnp.concatenate([left, right], axis=2)]
    ppermute x6 -> x7, starting transfers between devices: 8.25 us -> 9.12 us  [diagonal(): return lax.ppermute(value, ('space', 'tm'), pairs)]
    slice x6 -> x3, local copies, waits for them, and re-layouts: 0.87 us -> 0.04 us  [the longest x2 0.04 us: per_device(): mixed = jnp.concatenate([left[18:36, :, 0:1], right[0:18, :, 1:2]], axis=2)]
    pallas_call x5 -> x7, Pallas kernels: 10.2 us -> 10.9 us  [the longest x2 5.15 us: run_staples(): pl.pallas_call(functools.partial(staple_kernel, mode), out_shape=jax.Shap...]
  transfers between devices with their start and end apart: 23 -> 21, of which waited for: 9 -> 7; matrix products, arithmetic and copies ran while one was open for 7% -> 6% of each run, Pallas kernels for 19% -> 23%
where the time goes in v3:
time: 63.9 us; the launch traced here: 63.6 us
  starting transfers between devices  21.4 us (33%)
  Pallas kernels  20 us (31%)
  waiting for transfers between devices  16.8 us (26%)
  local copies, waits for them, and re-layouts  3.99 us (6%)
  other arithmetic  1.22 us (2%)
    ppermute x14, starting transfers between devices, step(): lax.ppermute(value, axis, [((i + by) % count, i) for i in range(count)])  12.3 us
    ppermute x7, waiting for transfers between devices, diagonal(): return lax.ppermute(value, ('space', 'tm'), pairs)  10.4 us
    ppermute x7, starting transfers between devices, diagonal(): return lax.ppermute(value, ('space', 'tm'), pairs)  9.12 us
    pallas_call x2, Pallas kernels, run_final(): pl.pallas_call(last_kernel if last else final_kernel, out_shape=[jax.Shap...  7.22 us
    ppermute x14, waiting for transfers between devices, step(): lax.ppermute(value, axis, [((i + by) % count, i) for i in range(count)])  6.42 us
    pallas_call x2, Pallas kernels, run_staples(): pl.pallas_call(functools.partial(staple_kernel, mode), out_shape=jax.Shap...  5.15 us
    pallas_call x2, Pallas kernels, run_traces(): pl.pallas_call(functools.partial(trace_kernel, mode), out_shape=jax.Shape...  5.04 us
    unnamed x12, local copies, waits for them, and re-layouts  2.8 us
  transfers between devices with their start and end apart: 21, of which 7 were waited for; matrix products, arithmetic and copies ran while one was open for 6% of the time, Pallas kernels for 23%

profile of v3, /device:TPU:0, one launch (start us, length us, event | category | flops | bytes accessed | tf_op | source)
XLA Modules:
  0.0 63.6 jit_solution(5624213897122307033)
XLA Ops:
  0.0 2.9 %collective-permute-start.3 = (f32[4,18,2,4,2,128]{5,4,3,2,1,0:T(2,128)}, f32[4,18,2,4,2,128]{5,4,3,2,1,0:T(2,128)S(1)}, u32[]{:S(2)}, u32[]{:S(2)}) collective-permute-start(f32[4,18,2,4,2,128]{5,4,3,2,1,0:T(2,128)} %param.6), channel_id=1, source_target_pairs={{2,0},{0,2},{6,4},{4,6},{10,8},{8,10},{14,12},{12,14},{3,1},{1,3},... | collective-permute-start | bytes 1769480 | tf_op jit(solution)/shard_map/ppermute | solution.py:519
  2.9 1.1 %copy-done = f32[4,18,2,4,2,128]{5,4,3,2,1,0:T(2,128)S(1)} copy-done((f32[4,18,2,4,2,128]{5,4,3,2,1,0:T(2,128)S(1)}, f32[4,18,2,4,2,128]{5,4,3,2,1,0:T(2,128)}, u32[]{:S(2)}) %copy-start) | copy-done | bytes 589848
  4.0 0.4 unpack.2
  4.6 3.7 %collective-permute-start = (f32[72,2,2,128]{3,2,1,0:T(2,128)S(1)}, f32[72,2,2,128]{3,2,1,0:T(2,128)S(1)}, u32[]{:S(2)}, u32[]{:S(2)}) collective-permute-start(f32[72,2,2,128]{3,2,1,0:T(2,128)S(1)} %get-tuple-element.40), channel_id=1, source_target_pairs={{4,0},{8,4},{12,8},{0,12},{5,1},{9,5},{13,9},{1,13},{6,2},{10,6},{... | collective-permute-start | bytes 442376 | tf_op jit(solution)/shard_map/ppermute | solution.py:509
  8.3 0.9 %copy.15 = f32[72,2,6,128]{3,0,2,1:T(8,128)} copy(f32[72,2,6,128]{3,2,1,0:T(8,128)S(1)} %tail.1) | data formatting | bytes 884736 | tf_op jit(solution)/shard_map/tail/pallas_call | solution.py:438
  9.2 3.8 %collective-permute-start.7 = (f32[72,2,6,128]{3,0,2,1:T(8,128)}, f32[72,2,6,128]{3,0,2,1:T(8,128)S(1)}, u32[]{:S(2)}, u32[]{:S(2)}) collective-permute-start(f32[72,2,6,128]{3,0,2,1:T(8,128)} %copy.15), channel_id=1, source_target_pairs={{4,0},{8,4},{12,8},{0,12},{5,1},{9,5},{13,9},{1,13},{6,2},{10,6},{... | collective-permute-start | bytes 1327112 | tf_op jit(solution)/shard_map/ppermute | solution.py:509
  13.1 1.6 %copy.13.conv_in = bf16[2,81,12,64]{3,2,1,0:T(8,128)(2,1)S(1)} copy(bf16[2,81,12,64]{1,3,2,0:T(8,128)(2,1)} %param.8) | data formatting | bytes 497664 | tf_op args[2]
  14.7 0.4 weights.1
  15.1 1.0 %fusion = s32[2,4]{1,0:T(2,128)S(1)} fusion(s32[2,4,2,4,4]{4,3,2,1,0:T(4,128)} %param.7, s32[]{:T(128)S(6)} %select_n.16, s32[]{:T(128)S(6)} %select_n.17, s32[]{:T(128)S(6)} %select_n.18), kind=kLoop, calls=%fused_computation.7 | loop fusion | flops 16 | bytes 76 | tf_op jit(solution)/shard_map/jit(_where)/select_n | solution.py:538
  16.2 0.6 collective-permute-done.1
  16.8 0.6 collective-permute-start.5
  17.4 1.5 %collective-permute-start.6 = (f32[72,2,1,2,128]{4,3,1,0,2:T(2,128)S(1)}, f32[72,2,1,2,128]{4,3,1,0,2:T(2,128)S(1)}, u32[]{:S(2)}, u32[]{:S(2)}) collective-permute-start(f32[72,2,1,2,128]{4,3,1,0,2:T(2,128)S(1)} %bitcast.16), channel_id=1, source_target_pairs={{2,0},{0,2},{6,4},{4,6},{10,8},{8,10},{14,12},{12,14},{3,1},{1,3},... | collective-permute-start | bytes 442376 | tf_op jit(solution)/shard_map/ppermute | solution.py:519
  19.2 1.6 %traces.2 = bf16[16,16,128]{2,1,0:T(8,128)(2,1)S(1)} custom-call(s32[4]{0:T(128)S(1)} %get-tuple-element.79.ya, f32[72,2,8,128]{3,2,1,0:T(8,128)S(1)} %get-tuple-element.51.refs_0_.own, f32[72,2,8,128]{3,2,1,0:T(8,128)S(1)} %collective-permute-done.2.refs_1_, f32[72,2,8,128]{3,2,1,0:T(8,128)S(1)} %unpack.3.refs_2_.tp, ...), custom_call_target="tpu_custom_call" | custom-call | flops 8000000 | bytes 6000000 | tf_op jit(solution)/shard_map/traces/pallas_call | solution.py:452
  20.8 0.6 collective-permute-start.4
  21.6 3.5 %collective-permute-done.4 = bf16[2,4,2,16,128]{4,3,2,1,0:T(8,128)(2,1)S(1)} collective-permute-done((bf16[2,4,2,16,128]{4,3,2,1,0:T(8,128)(2,1)S(1)}, bf16[2,4,2,16,128]{4,3,2,1,0:T(8,128)(2,1)S(1)}, u32[]{:S(2)}, u32[]{:S(2)}) %collective-permute-start.4) | collective-permute-done | bytes 65568 | tf_op jit(solution)/shard_map/ppermute | solution.py:519
  25.2 0.6 collective-permute-start.12
  25.7 3.2 %collective-permute-start.9 = (bf16[2,1,4,16,128]{4,3,2,1,0:T(8,128)(2,1)S(1)}, bf16[2,1,4,16,128]{4,3,2,1,0:T(8,128)(2,1)S(1)}, u32[]{:S(2)}, u32[]{:S(2)}) collective-permute-start(bf16[2,1,4,16,128]{4,3,2,1,0:T(8,128)(2,1)S(1)} %get-tuple-element.75), channel_id=1, source_target_pairs={{4,0},{8,4},{12,8},{0,12},{5,1},{9,5},{13,9},{1,13},{6,2},{10,6},{... | collective-permute-start | bytes 98312 | tf_op jit(solution)/shard_map/ppermute | solution.py:509
  29.0 0.6 collective-permute-start.14
  29.6 2.6 %staples.2 = f32[24,18,8,128]{3,2,1,0:T(8,128)S(1)} custom-call(s32[4]{0:T(128)S(1)} %get-tuple-element.79.ya, f32[72,2,8,128]{3,2,1,0:T(8,128)S(1)} %get-tuple-element.51.refs_0_.own, f32[72,2,8,128]{3,2,1,0:T(8,128)S(1)} %collective-permute-done.2.refs_1_, f32[72,2,8,128]{3,2,1,0:T(8,128)S(1)} %unpack.3.refs_2_.tp, ...), custom_call_target="tpu_custom_call" | custom-call | flops 20000000 | bytes 16000000 | tf_op jit(solution)/shard_map/staples/pallas_call | solution.py:465
  32.2 2.5 %collective-permute-done.8 = bf16[2,1,4,16,128]{4,3,2,1,0:T(8,128)(2,1)S(1)} collective-permute-done((bf16[2,1,4,16,128]{4,3,2,1,0:T(8,128)(2,1)S(1)}, bf16[2,1,4,16,128]{4,3,2,1,0:T(8,128)(2,1)S(1)}, u32[]{:S(2)}, u32[]{:S(2)}) %collective-permute-start.8) | collective-permute-done | bytes 32800 | tf_op jit(solution)/shard_map/ppermute | solution.py:509
  34.8 1.4 %collective-permute-done.13.f_s = bf16[2,6,4,16,128]{4,3,2,1,0:T(8,128)(2,1)S(1)} collective-permute-done((bf16[2,6,4,16,128]{4,3,2,1,0:T(8,128)(2,1)S(1)}, bf16[2,6,4,16,128]{4,3,2,1,0:T(8,128)(2,1)S(1)}, u32[]{:S(2)}, u32[]{:S(2)}) %collective-permute-start.13) | collective-permute-done | bytes 196640 | tf_op jit(solution)/shard_map/ppermute | solution.py:509
  36.2 3.1 %rotate.2 = (f32[72,2,8,128]{3,2,1,0:T(8,128)S(1)}, f32[36,8,128]{2,1,0:T(8,128)S(1)}) custom-call(s32[4]{0:T(128)S(1)} %get-tuple-element.79.ya, f32[72,2,8,128]{3,2,1,0:T(8,128)S(1)} %get-tuple-element.51.refs_0_.own, f32[24,18,8,128]{3,2,1,0:T(8,128)S(1)} %staples.2, bf16[2,6,4,16,128]{4,3,2,1,0:T(8,128)(2,1)S(1)} %constant_dynamic-update-slice_fusion.f, ...), custom_call_target="tpu_custom_call" | custom-call | flops 300000000 | bytes 4000000 | tf_op jit(solution)/shard_map/rotate/pallas_call | solution.py:482
  39.3 2.3 %collective-permute-start.17 = (f32[36,4,2,128]{3,2,1,0:T(2,128)S(1)}, f32[36,4,2,128]{3,2,1,0:T(2,128)S(1)}, u32[]{:S(2)}, u32[]{:S(2)}) collective-permute-start(f32[36,4,2,128]{3,2,1,0:T(2,128)S(1)} %bitcast.26), channel_id=1, source_target_pairs={{6,0},{4,2},{10,4},{8,6},{14,8},{12,10},{2,12},{0,14},{7,1},{5,3},... | collective-permute-start | bytes 442376 | tf_op jit(solution)/shard_map/ppermute | solution.py:519
  41.6 0.6 collective-permute-start.16
  42.5 4.5 %collective-permute-done.17 = f32[36,4,2,128]{3,2,1,0:T(2,128)S(1)} collective-permute-done((f32[36,4,2,128]{3,2,1,0:T(2,128)S(1)}, f32[36,4,2,128]{3,2,1,0:T(2,128)S(1)}, u32[]{:S(2)}, u32[]{:S(2)}) %collective-permute-start.17) | collective-permute-done | bytes 147488 | tf_op jit(solution)/shard_map/ppermute | solution.py:519
  47.0 2.4 %collective-permute-done.16 = f32[36,4,2,128]{3,2,1,0:T(2,128)S(1)} collective-permute-done((f32[36,4,2,128]{3,2,1,0:T(2,128)S(1)}, f32[36,4,2,128]{3,2,1,0:T(2,128)S(1)}, u32[]{:S(2)}, u32[]{:S(2)}) %collective-permute-start.16) | collective-permute-done | bytes 147488 | tf_op jit(solution)/shard_map/ppermute | solution.py:519
  49.3 1.5 %shift.1 = (f32[72,2,8,128]{3,2,1,0:T(8,128)S(1)}, f32[216,8,128]{2,1,0:T(8,128)S(1)}, f32[216,8,128]{2,1,0:T(8,128)S(1)}, f32[72,2,8,128]{3,2,1,0:T(8,128)S(1)}) custom-call(s32[4]{0:T(128)S(1)} %get-tuple-element.79.ya, f32[72,2,8,128]{3,2,1,0:T(8,128)S(1)} %get-tuple-element.63.own, f32[72,2,2,128]{3,2,1,0:T(2,128)S(1)} %collective-permute-done.refs_3_.right, ...), custom_call_target="tpu_custom_call" | custom-call | flops 8000000 | bytes 6000000 | tf_op jit(solution)/shard_map/shift/pallas_call | solution.py:496
  50.9 0.5 collective-permute-start.19
  51.4 1.9 %collective-permute-done.18.refs_2_ = f32[216,8,128]{2,1,0:T(8,128)S(1)} collective-permute-done((f32[216,8,128]{2,1,0:T(8,128)S(1)}, f32[216,8,128]{2,1,0:T(8,128)S(1)}, u32[]{:S(2)}, u32[]{:S(2)}) %collective-permute-start.18) | collective-permute-done | bytes 884768 | tf_op jit(solution)/shard_map/ppermute | solution.py:509
  53.3 3.4 %traces.3 = bf16[48,16,128]{2,1,0:T(8,128)(2,1)S(1)} custom-call(s32[4]{0:T(128)S(1)} %get-tuple-element.80.ya, f32[216,8,128]{2,1,0:T(8,128)S(1)} %get-tuple-element.68.refs_0_, f32[216,8,128]{2,1,0:T(8,128)S(1)} %get-tuple-element.69.refs_1_, f32[216,8,128]{2,1,0:T(8,128)S(1)} %collective-permute-done.18.refs_2_, ...), custom_call_target="tpu_custom_call" | custom-call | flops 8000000 | bytes 6000000 | tf_op jit(solution)/shard_map/traces/pallas_call | solution.py:452
  57.0 2.6 %staples.3 = f32[24,18,8,128]{3,2,1,0:T(8,128)S(1)} custom-call(s32[4]{0:T(128)S(1)} %get-tuple-element.80.ya, f32[216,8,128]{2,1,0:T(8,128)S(1)} %get-tuple-element.68.refs_0_, f32[216,8,128]{2,1,0:T(8,128)S(1)} %get-tuple-element.69.refs_1_, f32[216,8,128]{2,1,0:T(8,128)S(1)} %collective-permute-done.18.refs_2_, ...), custom_call_target="tpu_custom_call" | custom-call | flops 20000000 | bytes 16000000 | tf_op jit(solution)/shard_map/staples/pallas_call | solution.py:465
  59.5 4.1 %rotate.3 = f32[72,16,128]{2,1,0:T(8,128)} custom-call(s32[4]{0:T(128)S(1)} %get-tuple-element.80.ya, f32[72,2,8,128]{3,2,1,0:T(8,128)S(1)} %get-tuple-element.67.own, f32[24,18,8,128]{3,2,1,0:T(8,128)S(1)} %staples.3, bf16[2,6,4,16,128]{4,3,2,1,0:T(8,128)(2,1)S(1)} %bitcast.18, bf16[2,6,4,16,128]{4,3,2,1,0:T(8,128)(2,1)S(1)} %collective-permute-done.20.f_s, ...), custom_call_target="tpu_custom_call" | custom-call | flops 300000000 | bytes 4000000 | tf_op jit(solution)/shard_map/rotate/pallas_call | solution.py:482
  (46 shorter events, 1.5 us)
Async XLA Ops:
  0.0 18.9 %collective-permute-start.3 = (f32[4,18,2,4,2,128]{5,4,3,2,1,0:T(2,128)}, f32[4,18,2,4,2,128]{5,4,3,2,1,0:T(2,128)S(1)}, u32[]{:S(2)}, u32[]{:S(2)}) collective-permute-start(f32[4,18,2,4,2,128]{5,4,3,2,1,0:T(2,128)} %param.6), channel_id=1, source_target_pairs={{2,0},{0,2},{6,4},{4,6},{10,8},{8,10},{14,12},{12,14},{3,1},{1,3},... | collective-permute-start | bytes 1769480 | tf_op jit(solution)/shard_map/ppermute | solution.py:519
  2.9 1.1 %copy-start = (f32[4,18,2,4,2,128]{5,4,3,2,1,0:T(2,128)S(1)}, f32[4,18,2,4,2,128]{5,4,3,2,1,0:T(2,128)}, u32[]{:S(2)}) copy-start(f32[4,18,2,4,2,128]{5,4,3,2,1,0:T(2,128)} %param.6) | copy-start | bytes 1769476
  4.0 9.0 %copy-start.3 = (bf16[2,64,24]{1,2,0:T(8,128)(2,1)S(1)}, bf16[2,64,24]{1,2,0:T(8,128)(2,1)}, u32[]{:S(2)}) copy-start(bf16[2,64,24]{1,2,0:T(8,128)(2,1)} %param.10) | copy-start | bytes 18436
  4.5 10.2 %copy-start.1 = (f32[2,64]{1,0:T(2,128)S(1)}, f32[2,64]{1,0:T(2,128)}, u32[]{:S(2)}) copy-start(f32[2,64]{1,0:T(2,128)} %bias_in.1) | copy-start | bytes 1540
  4.5 10.2 %copy-start.2 = (f32[2,24]{1,0:T(2,128)S(1)}, f32[2,24]{1,0:T(2,128)}, u32[]{:S(2)}) copy-start(f32[2,24]{1,0:T(2,128)} %bias_out.1) | copy-start | bytes 580
  4.5 14.7 %collective-permute-start.2 = (f32[72,2,8,128]{3,2,1,0:T(8,128)S(1)}, f32[72,2,8,128]{3,2,1,0:T(8,128)S(1)}, u32[]{:S(2)}, u32[]{:S(2)}) collective-permute-start(f32[72,2,8,128]{3,2,1,0:T(8,128)S(1)} %get-tuple-element.51.refs_0_.own), channel_id=1, source_target_pairs={{1,0},{0,1},{3,2},{2,3},{5,4},{4,5},{7,6},{6,7},{9,8},{8,9},{11,10... | collective-permute-start | bytes 1769480 | tf_op jit(solution)/shard_map/ppermute | solution.py:509
  4.6 11.6 %collective-permute-start = (f32[72,2,2,128]{3,2,1,0:T(2,128)S(1)}, f32[72,2,2,128]{3,2,1,0:T(2,128)S(1)}, u32[]{:S(2)}, u32[]{:S(2)}) collective-permute-start(f32[72,2,2,128]{3,2,1,0:T(2,128)S(1)} %get-tuple-element.40), channel_id=1, source_target_pairs={{4,0},{8,4},{12,8},{0,12},{5,1},{9,5},{13,9},{1,13},{6,2},{10,6},{... | collective-permute-start | bytes 442376 | tf_op jit(solution)/shard_map/ppermute | solution.py:509
  8.2 8.5 %collective-permute-start.1 = (f32[72,2,2,128]{3,2,1,0:T(2,128)S(1)}, f32[72,2,2,128]{3,2,1,0:T(2,128)S(1)}, u32[]{:S(2)}, u32[]{:S(2)}) collective-permute-start(f32[72,2,2,128]{3,2,1,0:T(2,128)S(1)} %get-tuple-element.41), channel_id=1, source_target_pairs={{12,0},{0,4},{4,8},{8,12},{13,1},{1,5},{5,9},{9,13},{14,2},{2,6},{... | collective-permute-start | bytes 442376 | tf_op jit(solution)/shard_map/ppermute | solution.py:509
  9.2 15.9 %collective-permute-start.7 = (f32[72,2,6,128]{3,0,2,1:T(8,128)}, f32[72,2,6,128]{3,0,2,1:T(8,128)S(1)}, u32[]{:S(2)}, u32[]{:S(2)}) collective-permute-start(f32[72,2,6,128]{3,0,2,1:T(8,128)} %copy.15), channel_id=1, source_target_pairs={{4,0},{8,4},{12,8},{0,12},{5,1},{9,5},{13,9},{1,13},{6,2},{10,6},{... | collective-permute-start | bytes 1327112 | tf_op jit(solution)/shard_map/ppermute | solution.py:509
  16.8 8.3 %collective-permute-start.5 = (f32[18,2,2,128]{3,2,1,0:T(2,128)S(1)}, f32[18,2,2,128]{3,2,1,0:T(2,128)S(1)}, u32[]{:S(2)}, u32[]{:S(2)}) collective-permute-start(f32[18,2,2,128]{3,2,1,0:T(2,128)S(1)} %pad_maximum_fusion.2), channel_id=1, source_target_pairs={{2,0},{0,2},{6,4},{4,6},{10,8},{8,10},{14,12},{12,14},{3,1},{1,3},... | collective-permute-start | bytes 110600 | tf_op jit(solution)/shard_map/ppermute | solution.py:519
  17.4 7.7 %collective-permute-start.6 = (f32[72,2,1,2,128]{4,3,1,0,2:T(2,128)S(1)}, f32[72,2,1,2,128]{4,3,1,0,2:T(2,128)S(1)}, u32[]{:S(2)}, u32[]{:S(2)}) collective-permute-start(f32[72,2,1,2,128]{4,3,1,0,2:T(2,128)S(1)} %bitcast.16), channel_id=1, source_target_pairs={{2,0},{0,2},{6,4},{4,6},{10,8},{8,10},{14,12},{12,14},{3,1},{1,3},... | collective-permute-start | bytes 442376 | tf_op jit(solution)/shard_map/ppermute | solution.py:519
  20.8 4.3 %collective-permute-start.4 = (bf16[2,4,2,16,128]{4,3,2,1,0:T(8,128)(2,1)S(1)}, bf16[2,4,2,16,128]{4,3,2,1,0:T(8,128)(2,1)S(1)}, u32[]{:S(2)}, u32[]{:S(2)}) collective-permute-start(bf16[2,4,2,16,128]{4,3,2,1,0:T(8,128)(2,1)S(1)} %bitcast.21), channel_id=1, source_target_pairs={{2,0},{0,2},{6,4},{4,6},{10,8},{8,10},{14,12},{12,14},{3,1},{1,3},... | collective-permute-start | bytes 196616 | tf_op jit(solution)/shard_map/ppermute | solution.py:519
  21.5 7.5 %collective-permute-start.11 = (f32[72,2,4,128]{3,2,1,0:T(4,128)S(1)}, f32[72,2,4,128]{3,2,1,0:T(4,128)S(1)}, u32[]{:S(2)}, u32[]{:S(2)}) collective-permute-start(f32[72,2,4,128]{3,2,1,0:T(4,128)S(1)} %pad_maximum_fusion.refs_4_), channel_id=1, source_target_pairs={{1,0},{0,1},{3,2},{2,3},{5,4},{4,5},{7,6},{6,7},{9,8},{8,9},{11,10... | collective-permute-start | bytes 884744 | tf_op jit(solution)/shard_map/ppermute | solution.py:509
  25.1 4.5 %collective-permute-start.10 = (f32[72,2,8,128]{3,2,1,0:T(8,128)S(1)}, f32[72,2,8,128]{3,2,1,0:T(8,128)S(1)}, u32[]{:S(2)}, u32[]{:S(2)}) collective-permute-start(f32[72,2,8,128]{3,2,1,0:T(8,128)S(1)} %unpack.3.refs_2_.tp), channel_id=1, source_target_pairs={{1,0},{0,1},{3,2},{2,3},{5,4},{4,5},{7,6},{6,7},{9,8},{8,9},{11,10... | collective-permute-start | bytes 1769480 | tf_op jit(solution)/shard_map/ppermute | solution.py:509
  25.2 4.4 %collective-permute-start.12 = (f32[18,2,2,128]{3,2,1,0:T(2,128)S(1)}, f32[18,2,2,128]{3,2,1,0:T(2,128)S(1)}, u32[]{:S(2)}, u32[]{:S(2)}) collective-permute-start(f32[18,2,2,128]{3,2,1,0:T(2,128)S(1)} %collective-permute-done.5.refs_6_), channel_id=1, source_target_pairs={{1,0},{0,1},{3,2},{2,3},{5,4},{4,5},{7,6},{6,7},{9,8},{8,9},{11,10... | collective-permute-start | bytes 110600 | tf_op jit(solution)/shard_map/ppermute | solution.py:509
  25.7 6.5 %collective-permute-start.9 = (bf16[2,1,4,16,128]{4,3,2,1,0:T(8,128)(2,1)S(1)}, bf16[2,1,4,16,128]{4,3,2,1,0:T(8,128)(2,1)S(1)}, u32[]{:S(2)}, u32[]{:S(2)}) collective-permute-start(bf16[2,1,4,16,128]{4,3,2,1,0:T(8,128)(2,1)S(1)} %get-tuple-element.75), channel_id=1, source_target_pairs={{4,0},{8,4},{12,8},{0,12},{5,1},{9,5},{13,9},{1,13},{6,2},{10,6},{... | collective-permute-start | bytes 98312 | tf_op jit(solution)/shard_map/ppermute | solution.py:509
  29.0 5.7 %collective-permute-start.8 = (bf16[2,1,4,16,128]{4,3,2,1,0:T(8,128)(2,1)S(1)}, bf16[2,1,4,16,128]{4,3,2,1,0:T(8,128)(2,1)S(1)}, u32[]{:S(2)}, u32[]{:S(2)}) collective-permute-start(bf16[2,1,4,16,128]{4,3,2,1,0:T(8,128)(2,1)S(1)} %get-tuple-element.76), channel_id=1, source_target_pairs={{12,0},{0,4},{4,8},{8,12},{13,1},{1,5},{5,9},{9,13},{14,2},{2,6},{... | collective-permute-start | bytes 98312 | tf_op jit(solution)/shard_map/ppermute | solution.py:509
  29.0 13.4 %collective-permute-start.14 = (f32[72,2,3,2,128]{4,0,3,2,1:T(8,128)S(1)}, f32[72,2,3,2,128]{4,0,3,2,1:T(8,128)S(1)}, u32[]{:S(2)}, u32[]{:S(2)}) collective-permute-start(f32[72,2,3,2,128]{4,0,3,2,1:T(8,128)S(1)} %bitcast.28), channel_id=1, source_target_pairs={{2,0},{0,2},{6,4},{4,6},{10,8},{8,10},{14,12},{12,14},{3,1},{1,3},... | collective-permute-start | bytes 1327112 | tf_op jit(solution)/shard_map/ppermute | solution.py:519
  34.7 1.5 %collective-permute-start.13 = (bf16[2,6,4,16,128]{4,3,2,1,0:T(8,128)(2,1)S(1)}, bf16[2,6,4,16,128]{4,3,2,1,0:T(8,128)(2,1)S(1)}, u32[]{:S(2)}, u32[]{:S(2)}) collective-permute-start(bf16[2,6,4,16,128]{4,3,2,1,0:T(8,128)(2,1)S(1)} %constant_dynamic-update-slice_fusion.f), channel_id=1, source_target_pairs={{1,0},{0,1},{3,2},{2,3},{5,4},{4,5},{7,6},{6,7},{9,8},{8,9},{11,10... | collective-permute-start | bytes 589832 | tf_op jit(solution)/shard_map/ppermute | solution.py:509
  39.3 7.6 %collective-permute-start.17 = (f32[36,4,2,128]{3,2,1,0:T(2,128)S(1)}, f32[36,4,2,128]{3,2,1,0:T(2,128)S(1)}, u32[]{:S(2)}, u32[]{:S(2)}) collective-permute-start(f32[36,4,2,128]{3,2,1,0:T(2,128)S(1)} %bitcast.26), channel_id=1, source_target_pairs={{6,0},{4,2},{10,4},{8,6},{14,8},{12,10},{2,12},{0,14},{7,1},{5,3},... | collective-permute-start | bytes 442376 | tf_op jit(solution)/shard_map/ppermute | solution.py:519
  41.6 7.7 %collective-permute-start.16 = (f32[36,4,2,128]{3,2,1,0:T(2,128)S(1)}, f32[36,4,2,128]{3,2,1,0:T(2,128)S(1)}, u32[]{:S(2)}, u32[]{:S(2)}) collective-permute-start(f32[36,4,2,128]{3,2,1,0:T(2,128)S(1)} %bitcast.27), channel_id=1, source_target_pairs={{2,0},{0,2},{6,4},{4,6},{10,8},{8,10},{14,12},{12,14},{3,1},{1,3},... | collective-permute-start | bytes 442376 | tf_op jit(solution)/shard_map/ppermute | solution.py:519
  42.2 7.1 %collective-permute-start.15 = (f32[36,8,128]{2,1,0:T(8,128)S(1)}, f32[36,8,128]{2,1,0:T(8,128)S(1)}, u32[]{:S(2)}, u32[]{:S(2)}) collective-permute-start(f32[36,8,128]{2,1,0:T(8,128)S(1)} %get-tuple-element.66), channel_id=1, source_target_pairs={{4,0},{8,4},{12,8},{0,12},{5,1},{9,5},{13,9},{1,13},{6,2},{10,6},{... | collective-permute-start | bytes 442376 | tf_op jit(solution)/shard_map/ppermute | solution.py:509
  50.8 2.5 %collective-permute-start.18 = (f32[216,8,128]{2,1,0:T(8,128)S(1)}, f32[216,8,128]{2,1,0:T(8,128)S(1)}, u32[]{:S(2)}, u32[]{:S(2)}) collective-permute-start(f32[216,8,128]{2,1,0:T(8,128)S(1)} %get-tuple-element.68.refs_0_), channel_id=1, source_target_pairs={{1,0},{0,1},{3,2},{2,3},{5,4},{4,5},{7,6},{6,7},{9,8},{8,9},{11,10... | collective-permute-start | bytes 2654216 | tf_op jit(solution)/shard_map/ppermute | solution.py:509
  50.9 6.1 %collective-permute-start.19 = (f32[216,8,128]{2,1,0:T(8,128)S(1)}, f32[216,8,128]{2,1,0:T(8,128)S(1)}, u32[]{:S(2)}, u32[]{:S(2)}) collective-permute-start(f32[216,8,128]{2,1,0:T(8,128)S(1)} %get-tuple-element.69.refs_1_), channel_id=1, source_target_pairs={{1,0},{0,1},{3,2},{2,3},{5,4},{4,5},{7,6},{6,7},{9,8},{8,9},{11,10... | collective-permute-start | bytes 2654216 | tf_op jit(solution)/shard_map/ppermute | solution.py:509
  56.8 2.8 %collective-permute-start.20 = (bf16[2,6,4,16,128]{4,3,2,1,0:T(8,128)(2,1)S(1)}, bf16[2,6,4,16,128]{4,3,2,1,0:T(8,128)(2,1)S(1)}, u32[]{:S(2)}, u32[]{:S(2)}) collective-permute-start(bf16[2,6,4,16,128]{4,3,2,1,0:T(8,128)(2,1)S(1)} %bitcast.17), channel_id=1, source_target_pairs={{1,0},{0,1},{3,2},{2,3},{5,4},{4,5},{7,6},{6,7},{9,8},{8,9},{11,10... | collective-permute-start | bytes 589832 | tf_op jit(solution)/shard_map/ppermute | solution.py:509

commit v4 on v3

--- a/solution.py
+++ b/solution.py
@@ -269,28 +269,26 @@
 
 def update(ya, own, staples, f, f_s, w_in, b_in, w_out, b_out, out, wts, sent=None):
     places = ((1, 1), (0, 0), (0, 1), (1, 0))
-    for y in range(2):
-        for x in range(4):
-            columns = []
-            for t in range(2):
-                tiles = []
-                for a in range(3):
-                    for b in range(3):
-                        for c in range(3):
-                            other, at = places[y + c]
-                            tiles.append((f, f_s)[other][at, x + b, t + a])
-                columns.append(jnp.concatenate(tiles, axis=0))
-            patch = jnp.concatenate(columns, axis=1)
-            g = jnp.dot(w_in[...], patch, preferred_element_type=F32)
-            for t in range(2):
-                lanes = slice(128 * t, 128 * t + 128)
-                hidden = (
-                    zroll(g[0:64, lanes], -1) + g[64:128, lanes] + zroll(g[128:192, lanes], 1)
-                )
-                hidden = jnp.tanh(hidden + b_in[...]).astype(BF16)
-                weights = jnp.dot(w_out[...], hidden, preferred_element_type=F32) + b_out[...]
-                row = 24 * (2 * x + t)
-                wts[y, row : row + 24] = weights
+    sites = [(y, r // 2, r % 2) for y in range(2) for r in range(8)]
+    columns = []
+    for y, x, t in sites:
+        tiles = []
+        for a in range(3):
+            for b in range(3):
+                for c in range(3):
+                    other, at = places[y + c]
+                    tiles.append((f, f_s)[other][at, x + b, t + a])
+        columns.append(jnp.concatenate(tiles, axis=0))
+    g = jnp.dot(w_in[...], jnp.concatenate(columns, axis=1), preferred_element_type=F32)
+    hidden = []
+    for k in range(16):
+        lanes = slice(128 * k, 128 * k + 128)
+        part = zroll(g[0:64, lanes], -1) + g[64:128, lanes] + zroll(g[128:192, lanes], 1)
+        hidden.append(jnp.tanh(part + b_in[...]).astype(BF16))
+    weights = jnp.dot(w_out[...], jnp.concatenate(hidden, axis=1), preferred_element_type=F32)
+    for k in range(16):
+        row = 24 * (k % 8)
+        wts[k // 8, row : row + 24] = weights[:, 128 * k : 128 * k + 128] + b_out[...]
 
     for m in range(4):
         y = ya[m]
@@ -567,17 +565,11 @@
     f_s = step(f, "sub", 1)
     own, q = run_final(ya[0], own, staples, f, f_s, *weights[:4], False)
 
+    q_tp = other_rows(q)
+    q_far = other_rows(q, 1)
+    q_next = step(q, "space", 1)
     own, pack_0, pack_1, ex = run_shift(
-        ya[0],
-        own,
-        right,
-        tail,
-        tp,
-        far,
-        far_tail,
-        step(q, "space", 1),
-        other_rows(q),
-        other_rows(q, 1),
+        ya[0], own, right, tail, tp, far, far_tail, q_next, q_tp, q_far
     )
 
     other_0, other_1 = step(pack_0, "sub", 1), step(pack_1, "sub", 1)

time: 63.9 us -> 61.3 us (0.959)
  Pallas kernels: 20 us -> 17.4 us
    pallas_call x2, Pallas kernels: 7.22 us -> 4.61 us  [run_final(): pl.pallas_call(last_kernel if last else final_kernel, out_shape=[jax.Shap...]
  transfers between devices with their start and end apart: 21 -> 21, of which waited for: 7 -> 8; matrix products, arithmetic and copies ran while one was open for 6% -> 7% of each run, Pallas kernels for 23% -> 21%
where the time goes in v4:
time: 61.3 us; the launch traced here: 61 us
  starting transfers between devices  21.4 us (35%)
  Pallas kernels  17.4 us (28%)
  waiting for transfers between devices  16.8 us (27%)
  local copies, waits for them, and re-layouts  3.99 us (7%)
  other arithmetic  1.22 us (2%)
    ppermute x14, starting transfers between devices, step(): lax.ppermute(value, axis, [((i + by) % count, i) for i in range(count)])  12.3 us
    ppermute x7, waiting for transfers between devices, diagonal(): return lax.ppermute(value, ('space', 'tm'), pairs)  10.4 us
    ppermute x7, starting transfers between devices, diagonal(): return lax.ppermute(value, ('space', 'tm'), pairs)  9.12 us
    ppermute x14, waiting for transfers between devices, step(): lax.ppermute(value, axis, [((i + by) % count, i) for i in range(count)])  6.43 us
    pallas_call x2, Pallas kernels, run_staples(): pl.pallas_call(functools.partial(staple_kernel, mode), out_shape=jax.Shap...  5.13 us
    pallas_call x2, Pallas kernels, run_traces(): pl.pallas_call(functools.partial(trace_kernel, mode), out_shape=jax.Shape...  5.04 us
    pallas_call x2, Pallas kernels, run_final(): pl.pallas_call(last_kernel if last else final_kernel, out_shape=[jax.Shap...  4.61 us
    unnamed x12, local copies, waits for them, and re-layouts  2.8 us
  transfers between devices with their start and end apart: 21, of which 8 were waited for; matrix products, arithmetic and copies ran while one was open for 7% of the time, Pallas kernels for 21%

profile of v4, /device:TPU:0, one launch (start us, length us, event | category | flops | bytes accessed | tf_op | source)
XLA Modules:
  0.0 61.0 jit_solution(6926598449920301910)
XLA Ops:
  0.0 2.9 %collective-permute-start.3 = (f32[4,18,2,4,2,128]{5,4,3,2,1,0:T(2,128)}, f32[4,18,2,4,2,128]{5,4,3,2,1,0:T(2,128)S(1)}, u32[]{:S(2)}, u32[]{:S(2)}) collective-permute-start(f32[4,18,2,4,2,128]{5,4,3,2,1,0:T(2,128)} %param.6), channel_id=1, source_target_pairs={{2,0},{0,2},{6,4},{4,6},{10,8},{8,10},{14,12},{12,14},{3,1},{1,3},... | collective-permute-start | bytes 1769480 | tf_op jit(solution)/shard_map/ppermute | solution.py:517
  2.9 1.1 %copy-done = f32[4,18,2,4,2,128]{5,4,3,2,1,0:T(2,128)S(1)} copy-done((f32[4,18,2,4,2,128]{5,4,3,2,1,0:T(2,128)S(1)}, f32[4,18,2,4,2,128]{5,4,3,2,1,0:T(2,128)}, u32[]{:S(2)}) %copy-start) | copy-done | bytes 589848
  4.0 0.4 unpack.2
  4.6 3.7 %collective-permute-start = (f32[72,2,2,128]{3,2,1,0:T(2,128)S(1)}, f32[72,2,2,128]{3,2,1,0:T(2,128)S(1)}, u32[]{:S(2)}, u32[]{:S(2)}) collective-permute-start(f32[72,2,2,128]{3,2,1,0:T(2,128)S(1)} %get-tuple-element.40), channel_id=1, source_target_pairs={{4,0},{8,4},{12,8},{0,12},{5,1},{9,5},{13,9},{1,13},{6,2},{10,6},{... | collective-permute-start | bytes 442376 | tf_op jit(solution)/shard_map/ppermute | solution.py:507
  8.3 0.9 %copy.15 = f32[72,2,6,128]{3,0,2,1:T(8,128)} copy(f32[72,2,6,128]{3,2,1,0:T(8,128)S(1)} %tail.1) | data formatting | bytes 884736 | tf_op jit(solution)/shard_map/tail/pallas_call | solution.py:436
  9.2 3.8 %collective-permute-start.7 = (f32[72,2,6,128]{3,0,2,1:T(8,128)}, f32[72,2,6,128]{3,0,2,1:T(8,128)S(1)}, u32[]{:S(2)}, u32[]{:S(2)}) collective-permute-start(f32[72,2,6,128]{3,0,2,1:T(8,128)} %copy.15), channel_id=1, source_target_pairs={{4,0},{8,4},{12,8},{0,12},{5,1},{9,5},{13,9},{1,13},{6,2},{10,6},{... | collective-permute-start | bytes 1327112 | tf_op jit(solution)/shard_map/ppermute | solution.py:507
  13.1 1.6 %copy.13.conv_in = bf16[2,81,12,64]{3,2,1,0:T(8,128)(2,1)S(1)} copy(bf16[2,81,12,64]{1,3,2,0:T(8,128)(2,1)} %param.8) | data formatting | bytes 497664 | tf_op args[2]
  14.7 0.4 weights.1
  15.1 1.0 %fusion = s32[2,4]{1,0:T(2,128)S(1)} fusion(s32[2,4,2,4,4]{4,3,2,1,0:T(4,128)} %param.7, s32[]{:T(128)S(6)} %select_n.16, s32[]{:T(128)S(6)} %select_n.17, s32[]{:T(128)S(6)} %select_n.18), kind=kLoop, calls=%fused_computation.7 | loop fusion | flops 16 | bytes 76 | tf_op jit(solution)/shard_map/jit(_where)/select_n | solution.py:536
  16.2 0.6 collective-permute-done.1
  16.8 0.6 collective-permute-start.5
  17.4 1.5 %collective-permute-start.6 = (f32[72,2,1,2,128]{4,3,1,0,2:T(2,128)S(1)}, f32[72,2,1,2,128]{4,3,1,0,2:T(2,128)S(1)}, u32[]{:S(2)}, u32[]{:S(2)}) collective-permute-start(f32[72,2,1,2,128]{4,3,1,0,2:T(2,128)S(1)} %bitcast.16), channel_id=1, source_target_pairs={{2,0},{0,2},{6,4},{4,6},{10,8},{8,10},{14,12},{12,14},{3,1},{1,3},... | collective-permute-start | bytes 442376 | tf_op jit(solution)/shard_map/ppermute | solution.py:517
  19.2 1.6 %traces.2 = bf16[16,16,128]{2,1,0:T(8,128)(2,1)S(1)} custom-call(s32[4]{0:T(128)S(1)} %get-tuple-element.79.ya, f32[72,2,8,128]{3,2,1,0:T(8,128)S(1)} %get-tuple-element.51.refs_0_.own, f32[72,2,8,128]{3,2,1,0:T(8,128)S(1)} %collective-permute-done.2.refs_1_, f32[72,2,8,128]{3,2,1,0:T(8,128)S(1)} %unpack.3.refs_2_.tp, ...), custom_call_target="tpu_custom_call" | custom-call | flops 8000000 | bytes 6000000 | tf_op jit(solution)/shard_map/traces/pallas_call | solution.py:450
  20.8 0.6 collective-permute-start.4
  21.6 3.5 %collective-permute-done.4 = bf16[2,4,2,16,128]{4,3,2,1,0:T(8,128)(2,1)S(1)} collective-permute-done((bf16[2,4,2,16,128]{4,3,2,1,0:T(8,128)(2,1)S(1)}, bf16[2,4,2,16,128]{4,3,2,1,0:T(8,128)(2,1)S(1)}, u32[]{:S(2)}, u32[]{:S(2)}) %collective-permute-start.4) | collective-permute-done | bytes 65568 | tf_op jit(solution)/shard_map/ppermute | solution.py:517
  25.2 0.6 collective-permute-start.12
  25.7 3.2 %collective-permute-start.9 = (bf16[2,1,4,16,128]{4,3,2,1,0:T(8,128)(2,1)S(1)}, bf16[2,1,4,16,128]{4,3,2,1,0:T(8,128)(2,1)S(1)}, u32[]{:S(2)}, u32[]{:S(2)}) collective-permute-start(bf16[2,1,4,16,128]{4,3,2,1,0:T(8,128)(2,1)S(1)} %get-tuple-element.75), channel_id=1, source_target_pairs={{4,0},{8,4},{12,8},{0,12},{5,1},{9,5},{13,9},{1,13},{6,2},{10,6},{... | collective-permute-start | bytes 98312 | tf_op jit(solution)/shard_map/ppermute | solution.py:507
  29.0 0.6 %collective-permute-start.14 = (f32[72,2,3,2,128]{4,0,3,2,1:T(8,128)S(1)}, f32[72,2,3,2,128]{4,0,3,2,1:T(8,128)S(1)}, u32[]{:S(2)}, u32[]{:S(2)}) collective-permute-start(f32[72,2,3,2,128]{4,0,3,2,1:T(8,128)S(1)} %bitcast.28), channel_id=1, source_target_pairs={{2,0},{0,2},{6,4},{4,6},{10,8},{8,10},{14,12},{12,14},{3,1},{1,3},... | collective-permute-start | bytes 1327112 | tf_op jit(solution)/shard_map/ppermute | solution.py:517
  29.6 2.6 %staples.2 = f32[24,18,8,128]{3,2,1,0:T(8,128)S(1)} custom-call(s32[4]{0:T(128)S(1)} %get-tuple-element.79.ya, f32[72,2,8,128]{3,2,1,0:T(8,128)S(1)} %get-tuple-element.51.refs_0_.own, f32[72,2,8,128]{3,2,1,0:T(8,128)S(1)} %collective-permute-done.2.refs_1_, f32[72,2,8,128]{3,2,1,0:T(8,128)S(1)} %unpack.3.refs_2_.tp, ...), custom_call_target="tpu_custom_call" | custom-call | flops 20000000 | bytes 16000000 | tf_op jit(solution)/shard_map/staples/pallas_call | solution.py:463
  32.2 2.5 %collective-permute-done.8 = bf16[2,1,4,16,128]{4,3,2,1,0:T(8,128)(2,1)S(1)} collective-permute-done((bf16[2,1,4,16,128]{4,3,2,1,0:T(8,128)(2,1)S(1)}, bf16[2,1,4,16,128]{4,3,2,1,0:T(8,128)(2,1)S(1)}, u32[]{:S(2)}, u32[]{:S(2)}) %collective-permute-start.8) | collective-permute-done | bytes 32800 | tf_op jit(solution)/shard_map/ppermute | solution.py:507
  34.8 1.4 %collective-permute-done.13.f_s = bf16[2,6,4,16,128]{4,3,2,1,0:T(8,128)(2,1)S(1)} collective-permute-done((bf16[2,6,4,16,128]{4,3,2,1,0:T(8,128)(2,1)S(1)}, bf16[2,6,4,16,128]{4,3,2,1,0:T(8,128)(2,1)S(1)}, u32[]{:S(2)}, u32[]{:S(2)}) %collective-permute-start.13) | collective-permute-done | bytes 196640 | tf_op jit(solution)/shard_map/ppermute | solution.py:507
  36.2 1.8 %rotate.2 = (f32[72,2,8,128]{3,2,1,0:T(8,128)S(1)}, f32[36,8,128]{2,1,0:T(8,128)S(1)}) custom-call(s32[4]{0:T(128)S(1)} %get-tuple-element.79.ya, f32[72,2,8,128]{3,2,1,0:T(8,128)S(1)} %get-tuple-element.51.refs_0_.own, f32[24,18,8,128]{3,2,1,0:T(8,128)S(1)} %staples.2, bf16[2,6,4,16,128]{4,3,2,1,0:T(8,128)(2,1)S(1)} %constant_dynamic-update-slice_fusion.f, ...), custom_call_target="tpu_custom_call" | custom-call | flops 300000000 | bytes 4000000 | tf_op jit(solution)/shard_map/rotate/pallas_call | solution.py:480
  38.0 2.3 %collective-permute-start.17 = (f32[36,4,2,128]{3,2,1,0:T(2,128)S(1)}, f32[36,4,2,128]{3,2,1,0:T(2,128)S(1)}, u32[]{:S(2)}, u32[]{:S(2)}) collective-permute-start(f32[36,4,2,128]{3,2,1,0:T(2,128)S(1)} %bitcast.26), channel_id=1, source_target_pairs={{6,0},{4,2},{10,4},{8,6},{14,8},{12,10},{2,12},{0,14},{7,1},{5,3},... | collective-permute-start | bytes 442376 | tf_op jit(solution)/shard_map/ppermute | solution.py:517
  40.3 0.6 collective-permute-start.16
  41.3 4.3 %collective-permute-done.17 = f32[36,4,2,128]{3,2,1,0:T(2,128)S(1)} collective-permute-done((f32[36,4,2,128]{3,2,1,0:T(2,128)S(1)}, f32[36,4,2,128]{3,2,1,0:T(2,128)S(1)}, u32[]{:S(2)}, u32[]{:S(2)}) %collective-permute-start.17) | collective-permute-done | bytes 147488 | tf_op jit(solution)/shard_map/ppermute | solution.py:517
  45.7 2.4 %collective-permute-done.16 = f32[36,4,2,128]{3,2,1,0:T(2,128)S(1)} collective-permute-done((f32[36,4,2,128]{3,2,1,0:T(2,128)S(1)}, f32[36,4,2,128]{3,2,1,0:T(2,128)S(1)}, u32[]{:S(2)}, u32[]{:S(2)}) %collective-permute-start.16) | collective-permute-done | bytes 147488 | tf_op jit(solution)/shard_map/ppermute | solution.py:517
  48.0 1.5 %shift.1 = (f32[72,2,8,128]{3,2,1,0:T(8,128)S(1)}, f32[216,8,128]{2,1,0:T(8,128)S(1)}, f32[216,8,128]{2,1,0:T(8,128)S(1)}, f32[72,2,8,128]{3,2,1,0:T(8,128)S(1)}) custom-call(s32[4]{0:T(128)S(1)} %get-tuple-element.79.ya, f32[72,2,8,128]{3,2,1,0:T(8,128)S(1)} %get-tuple-element.63.own, f32[72,2,2,128]{3,2,1,0:T(2,128)S(1)} %collective-permute-done.refs_3_.right, ...), custom_call_target="tpu_custom_call" | custom-call | flops 8000000 | bytes 6000000 | tf_op jit(solution)/shard_map/shift/pallas_call | solution.py:494
  49.6 0.5 collective-permute-start.19
  50.1 1.9 %collective-permute-done.18.refs_2_ = f32[216,8,128]{2,1,0:T(8,128)S(1)} collective-permute-done((f32[216,8,128]{2,1,0:T(8,128)S(1)}, f32[216,8,128]{2,1,0:T(8,128)S(1)}, u32[]{:S(2)}, u32[]{:S(2)}) %collective-permute-start.18) | collective-permute-done | bytes 884768 | tf_op jit(solution)/shard_map/ppermute | solution.py:507
  52.0 3.4 %traces.3 = bf16[48,16,128]{2,1,0:T(8,128)(2,1)S(1)} custom-call(s32[4]{0:T(128)S(1)} %get-tuple-element.80.ya, f32[216,8,128]{2,1,0:T(8,128)S(1)} %get-tuple-element.68.refs_0_, f32[216,8,128]{2,1,0:T(8,128)S(1)} %get-tuple-element.69.refs_1_, f32[216,8,128]{2,1,0:T(8,128)S(1)} %collective-permute-done.18.refs_2_, ...), custom_call_target="tpu_custom_call" | custom-call | flops 8000000 | bytes 6000000 | tf_op jit(solution)/shard_map/traces/pallas_call | solution.py:450
  55.7 2.5 %staples.3 = f32[24,18,8,128]{3,2,1,0:T(8,128)S(1)} custom-call(s32[4]{0:T(128)S(1)} %get-tuple-element.80.ya, f32[216,8,128]{2,1,0:T(8,128)S(1)} %get-tuple-element.68.refs_0_, f32[216,8,128]{2,1,0:T(8,128)S(1)} %get-tuple-element.69.refs_1_, f32[216,8,128]{2,1,0:T(8,128)S(1)} %collective-permute-done.18.refs_2_, ...), custom_call_target="tpu_custom_call" | custom-call | flops 20000000 | bytes 16000000 | tf_op jit(solution)/shard_map/staples/pallas_call | solution.py:463
  58.2 2.8 %rotate.3 = f32[72,16,128]{2,1,0:T(8,128)} custom-call(s32[4]{0:T(128)S(1)} %get-tuple-element.80.ya, f32[72,2,8,128]{3,2,1,0:T(8,128)S(1)} %get-tuple-element.67.own, f32[24,18,8,128]{3,2,1,0:T(8,128)S(1)} %staples.3, bf16[2,6,4,16,128]{4,3,2,1,0:T(8,128)(2,1)S(1)} %bitcast.18, bf16[2,6,4,16,128]{4,3,2,1,0:T(8,128)(2,1)S(1)} %collective-permute-done.20.f_s, ...), custom_call_target="tpu_custom_call" | custom-call | flops 300000000 | bytes 4000000 | tf_op jit(solution)/shard_map/rotate/pallas_call | solution.py:480
  (46 shorter events, 1.6 us)
Async XLA Ops:
  0.0 18.9 %collective-permute-start.3 = (f32[4,18,2,4,2,128]{5,4,3,2,1,0:T(2,128)}, f32[4,18,2,4,2,128]{5,4,3,2,1,0:T(2,128)S(1)}, u32[]{:S(2)}, u32[]{:S(2)}) collective-permute-start(f32[4,18,2,4,2,128]{5,4,3,2,1,0:T(2,128)} %param.6), channel_id=1, source_target_pairs={{2,0},{0,2},{6,4},{4,6},{10,8},{8,10},{14,12},{12,14},{3,1},{1,3},... | collective-permute-start | bytes 1769480 | tf_op jit(solution)/shard_map/ppermute | solution.py:517
  2.9 1.1 %copy-start = (f32[4,18,2,4,2,128]{5,4,3,2,1,0:T(2,128)S(1)}, f32[4,18,2,4,2,128]{5,4,3,2,1,0:T(2,128)}, u32[]{:S(2)}) copy-start(f32[4,18,2,4,2,128]{5,4,3,2,1,0:T(2,128)} %param.6) | copy-start | bytes 1769476
  4.0 9.0 %copy-start.3 = (bf16[2,64,24]{1,2,0:T(8,128)(2,1)S(1)}, bf16[2,64,24]{1,2,0:T(8,128)(2,1)}, u32[]{:S(2)}) copy-start(bf16[2,64,24]{1,2,0:T(8,128)(2,1)} %param.10) | copy-start | bytes 18436
  4.5 10.2 %copy-start.1 = (f32[2,64]{1,0:T(2,128)S(1)}, f32[2,64]{1,0:T(2,128)}, u32[]{:S(2)}) copy-start(f32[2,64]{1,0:T(2,128)} %bias_in.1) | copy-start | bytes 1540
  4.5 10.2 %copy-start.2 = (f32[2,24]{1,0:T(2,128)S(1)}, f32[2,24]{1,0:T(2,128)}, u32[]{:S(2)}) copy-start(f32[2,24]{1,0:T(2,128)} %bias_out.1) | copy-start | bytes 580
  4.5 14.7 %collective-permute-start.2 = (f32[72,2,8,128]{3,2,1,0:T(8,128)S(1)}, f32[72,2,8,128]{3,2,1,0:T(8,128)S(1)}, u32[]{:S(2)}, u32[]{:S(2)}) collective-permute-start(f32[72,2,8,128]{3,2,1,0:T(8,128)S(1)} %get-tuple-element.51.refs_0_.own), channel_id=1, source_target_pairs={{1,0},{0,1},{3,2},{2,3},{5,4},{4,5},{7,6},{6,7},{9,8},{8,9},{11,10... | collective-permute-start | bytes 1769480 | tf_op jit(solution)/shard_map/ppermute | solution.py:507
  4.6 11.6 %collective-permute-start = (f32[72,2,2,128]{3,2,1,0:T(2,128)S(1)}, f32[72,2,2,128]{3,2,1,0:T(2,128)S(1)}, u32[]{:S(2)}, u32[]{:S(2)}) collective-permute-start(f32[72,2,2,128]{3,2,1,0:T(2,128)S(1)} %get-tuple-element.40), channel_id=1, source_target_pairs={{4,0},{8,4},{12,8},{0,12},{5,1},{9,5},{13,9},{1,13},{6,2},{10,6},{... | collective-permute-start | bytes 442376 | tf_op jit(solution)/shard_map/ppermute | solution.py:507
  8.2 8.5 %collective-permute-start.1 = (f32[72,2,2,128]{3,2,1,0:T(2,128)S(1)}, f32[72,2,2,128]{3,2,1,0:T(2,128)S(1)}, u32[]{:S(2)}, u32[]{:S(2)}) collective-permute-start(f32[72,2,2,128]{3,2,1,0:T(2,128)S(1)} %get-tuple-element.41), channel_id=1, source_target_pairs={{12,0},{0,4},{4,8},{8,12},{13,1},{1,5},{5,9},{9,13},{14,2},{2,6},{... | collective-permute-start | bytes 442376 | tf_op jit(solution)/shard_map/ppermute | solution.py:507
  9.2 15.9 %collective-permute-start.7 = (f32[72,2,6,128]{3,0,2,1:T(8,128)}, f32[72,2,6,128]{3,0,2,1:T(8,128)S(1)}, u32[]{:S(2)}, u32[]{:S(2)}) collective-permute-start(f32[72,2,6,128]{3,0,2,1:T(8,128)} %copy.15), channel_id=1, source_target_pairs={{4,0},{8,4},{12,8},{0,12},{5,1},{9,5},{13,9},{1,13},{6,2},{10,6},{... | collective-permute-start | bytes 1327112 | tf_op jit(solution)/shard_map/ppermute | solution.py:507
  16.8 8.3 %collective-permute-start.5 = (f32[18,2,2,128]{3,2,1,0:T(2,128)S(1)}, f32[18,2,2,128]{3,2,1,0:T(2,128)S(1)}, u32[]{:S(2)}, u32[]{:S(2)}) collective-permute-start(f32[18,2,2,128]{3,2,1,0:T(2,128)S(1)} %pad_maximum_fusion.2), channel_id=1, source_target_pairs={{2,0},{0,2},{6,4},{4,6},{10,8},{8,10},{14,12},{12,14},{3,1},{1,3},... | collective-permute-start | bytes 110600 | tf_op jit(solution)/shard_map/ppermute | solution.py:517
  17.4 7.7 %collective-permute-start.6 = (f32[72,2,1,2,128]{4,3,1,0,2:T(2,128)S(1)}, f32[72,2,1,2,128]{4,3,1,0,2:T(2,128)S(1)}, u32[]{:S(2)}, u32[]{:S(2)}) collective-permute-start(f32[72,2,1,2,128]{4,3,1,0,2:T(2,128)S(1)} %bitcast.16), channel_id=1, source_target_pairs={{2,0},{0,2},{6,4},{4,6},{10,8},{8,10},{14,12},{12,14},{3,1},{1,3},... | collective-permute-start | bytes 442376 | tf_op jit(solution)/shard_map/ppermute | solution.py:517
  20.8 4.3 %collective-permute-start.4 = (bf16[2,4,2,16,128]{4,3,2,1,0:T(8,128)(2,1)S(1)}, bf16[2,4,2,16,128]{4,3,2,1,0:T(8,128)(2,1)S(1)}, u32[]{:S(2)}, u32[]{:S(2)}) collective-permute-start(bf16[2,4,2,16,128]{4,3,2,1,0:T(8,128)(2,1)S(1)} %bitcast.21), channel_id=1, source_target_pairs={{2,0},{0,2},{6,4},{4,6},{10,8},{8,10},{14,12},{12,14},{3,1},{1,3},... | collective-permute-start | bytes 196616 | tf_op jit(solution)/shard_map/ppermute | solution.py:517
  21.5 7.5 %collective-permute-start.11 = (f32[72,2,4,128]{3,2,1,0:T(4,128)S(1)}, f32[72,2,4,128]{3,2,1,0:T(4,128)S(1)}, u32[]{:S(2)}, u32[]{:S(2)}) collective-permute-start(f32[72,2,4,128]{3,2,1,0:T(4,128)S(1)} %pad_maximum_fusion.refs_4_), channel_id=1, source_target_pairs={{1,0},{0,1},{3,2},{2,3},{5,4},{4,5},{7,6},{6,7},{9,8},{8,9},{11,10... | collective-permute-start | bytes 884744 | tf_op jit(solution)/shard_map/ppermute | solution.py:507
  25.1 4.5 %collective-permute-start.10 = (f32[72,2,8,128]{3,2,1,0:T(8,128)S(1)}, f32[72,2,8,128]{3,2,1,0:T(8,128)S(1)}, u32[]{:S(2)}, u32[]{:S(2)}) collective-permute-start(f32[72,2,8,128]{3,2,1,0:T(8,128)S(1)} %unpack.3.refs_2_.tp), channel_id=1, source_target_pairs={{1,0},{0,1},{3,2},{2,3},{5,4},{4,5},{7,6},{6,7},{9,8},{8,9},{11,10... | collective-permute-start | bytes 1769480 | tf_op jit(solution)/shard_map/ppermute | solution.py:507
  25.2 4.4 %collective-permute-start.12 = (f32[18,2,2,128]{3,2,1,0:T(2,128)S(1)}, f32[18,2,2,128]{3,2,1,0:T(2,128)S(1)}, u32[]{:S(2)}, u32[]{:S(2)}) collective-permute-start(f32[18,2,2,128]{3,2,1,0:T(2,128)S(1)} %collective-permute-done.5.refs_6_), channel_id=1, source_target_pairs={{1,0},{0,1},{3,2},{2,3},{5,4},{4,5},{7,6},{6,7},{9,8},{8,9},{11,10... | collective-permute-start | bytes 110600 | tf_op jit(solution)/shard_map/ppermute | solution.py:507
  25.7 6.5 %collective-permute-start.9 = (bf16[2,1,4,16,128]{4,3,2,1,0:T(8,128)(2,1)S(1)}, bf16[2,1,4,16,128]{4,3,2,1,0:T(8,128)(2,1)S(1)}, u32[]{:S(2)}, u32[]{:S(2)}) collective-permute-start(bf16[2,1,4,16,128]{4,3,2,1,0:T(8,128)(2,1)S(1)} %get-tuple-element.75), channel_id=1, source_target_pairs={{4,0},{8,4},{12,8},{0,12},{5,1},{9,5},{13,9},{1,13},{6,2},{10,6},{... | collective-permute-start | bytes 98312 | tf_op jit(solution)/shard_map/ppermute | solution.py:507
  29.0 5.7 %collective-permute-start.8 = (bf16[2,1,4,16,128]{4,3,2,1,0:T(8,128)(2,1)S(1)}, bf16[2,1,4,16,128]{4,3,2,1,0:T(8,128)(2,1)S(1)}, u32[]{:S(2)}, u32[]{:S(2)}) collective-permute-start(bf16[2,1,4,16,128]{4,3,2,1,0:T(8,128)(2,1)S(1)} %get-tuple-element.76), channel_id=1, source_target_pairs={{12,0},{0,4},{4,8},{8,12},{13,1},{1,5},{5,9},{9,13},{14,2},{2,6},{... | collective-permute-start | bytes 98312 | tf_op jit(solution)/shard_map/ppermute | solution.py:507
  29.0 12.2 %collective-permute-start.14 = (f32[72,2,3,2,128]{4,0,3,2,1:T(8,128)S(1)}, f32[72,2,3,2,128]{4,0,3,2,1:T(8,128)S(1)}, u32[]{:S(2)}, u32[]{:S(2)}) collective-permute-start(f32[72,2,3,2,128]{4,0,3,2,1:T(8,128)S(1)} %bitcast.28), channel_id=1, source_target_pairs={{2,0},{0,2},{6,4},{4,6},{10,8},{8,10},{14,12},{12,14},{3,1},{1,3},... | collective-permute-start | bytes 1327112 | tf_op jit(solution)/shard_map/ppermute | solution.py:517
  34.7 1.5 %collective-permute-start.13 = (bf16[2,6,4,16,128]{4,3,2,1,0:T(8,128)(2,1)S(1)}, bf16[2,6,4,16,128]{4,3,2,1,0:T(8,128)(2,1)S(1)}, u32[]{:S(2)}, u32[]{:S(2)}) collective-permute-start(bf16[2,6,4,16,128]{4,3,2,1,0:T(8,128)(2,1)S(1)} %constant_dynamic-update-slice_fusion.f), channel_id=1, source_target_pairs={{1,0},{0,1},{3,2},{2,3},{5,4},{4,5},{7,6},{6,7},{9,8},{8,9},{11,10... | collective-permute-start | bytes 589832 | tf_op jit(solution)/shard_map/ppermute | solution.py:507
  38.0 7.6 %collective-permute-start.17 = (f32[36,4,2,128]{3,2,1,0:T(2,128)S(1)}, f32[36,4,2,128]{3,2,1,0:T(2,128)S(1)}, u32[]{:S(2)}, u32[]{:S(2)}) collective-permute-start(f32[36,4,2,128]{3,2,1,0:T(2,128)S(1)} %bitcast.26), channel_id=1, source_target_pairs={{6,0},{4,2},{10,4},{8,6},{14,8},{12,10},{2,12},{0,14},{7,1},{5,3},... | collective-permute-start | bytes 442376 | tf_op jit(solution)/shard_map/ppermute | solution.py:517
  40.3 7.7 %collective-permute-start.16 = (f32[36,4,2,128]{3,2,1,0:T(2,128)S(1)}, f32[36,4,2,128]{3,2,1,0:T(2,128)S(1)}, u32[]{:S(2)}, u32[]{:S(2)}) collective-permute-start(f32[36,4,2,128]{3,2,1,0:T(2,128)S(1)} %bitcast.27), channel_id=1, source_target_pairs={{2,0},{0,2},{6,4},{4,6},{10,8},{8,10},{14,12},{12,14},{3,1},{1,3},... | collective-permute-start | bytes 442376 | tf_op jit(solution)/shard_map/ppermute | solution.py:517
  40.9 7.1 %collective-permute-start.15 = (f32[36,8,128]{2,1,0:T(8,128)S(1)}, f32[36,8,128]{2,1,0:T(8,128)S(1)}, u32[]{:S(2)}, u32[]{:S(2)}) collective-permute-start(f32[36,8,128]{2,1,0:T(8,128)S(1)} %get-tuple-element.66), channel_id=1, source_target_pairs={{4,0},{8,4},{12,8},{0,12},{5,1},{9,5},{13,9},{1,13},{6,2},{10,6},{... | collective-permute-start | bytes 442376 | tf_op jit(solution)/shard_map/ppermute | solution.py:507
  49.5 2.5 %collective-permute-start.18 = (f32[216,8,128]{2,1,0:T(8,128)S(1)}, f32[216,8,128]{2,1,0:T(8,128)S(1)}, u32[]{:S(2)}, u32[]{:S(2)}) collective-permute-start(f32[216,8,128]{2,1,0:T(8,128)S(1)} %get-tuple-element.68.refs_0_), channel_id=1, source_target_pairs={{1,0},{0,1},{3,2},{2,3},{5,4},{4,5},{7,6},{6,7},{9,8},{8,9},{11,10... | collective-permute-start | bytes 2654216 | tf_op jit(solution)/shard_map/ppermute | solution.py:507
  49.6 6.1 %collective-permute-start.19 = (f32[216,8,128]{2,1,0:T(8,128)S(1)}, f32[216,8,128]{2,1,0:T(8,128)S(1)}, u32[]{:S(2)}, u32[]{:S(2)}) collective-permute-start(f32[216,8,128]{2,1,0:T(8,128)S(1)} %get-tuple-element.69.refs_1_), channel_id=1, source_target_pairs={{1,0},{0,1},{3,2},{2,3},{5,4},{4,5},{7,6},{6,7},{9,8},{8,9},{11,10... | collective-permute-start | bytes 2654216 | tf_op jit(solution)/shard_map/ppermute | solution.py:507
  55.5 2.8 %collective-permute-start.20 = (bf16[2,6,4,16,128]{4,3,2,1,0:T(8,128)(2,1)S(1)}, bf16[2,6,4,16,128]{4,3,2,1,0:T(8,128)(2,1)S(1)}, u32[]{:S(2)}, u32[]{:S(2)}) collective-permute-start(bf16[2,6,4,16,128]{4,3,2,1,0:T(8,128)(2,1)S(1)} %bitcast.17), channel_id=1, source_target_pairs={{1,0},{0,1},{3,2},{2,3},{5,4},{4,5},{7,6},{6,7},{9,8},{8,9},{11,10... | collective-permute-start | bytes 589832 | tf_op jit(solution)/shard_map/ppermute | solution.py:507

commit v5 on v4

--- a/solution.py
+++ b/solution.py
@@ -8,6 +8,7 @@
 from jax.sharding import PartitionSpec as P
 
 PAIRS = ((0, 1), (0, 2), (0, 3), (1, 2), (1, 3), (2, 3))
+HALVES = (((3, 4, 5), (0, 1, 2)), ((0, 2, 4), (1, 3, 5)))
 F32 = jnp.float32
 BF16 = jnp.bfloat16
 BASE = 8
@@ -58,9 +59,11 @@
     return pltpu.roll(value, (-step) % value.shape[-1], value.ndim - 1)
 
 
-def trace_kernel(mode, ya, *refs):
+def trace_kernel(mode, planes, merge, ya, *refs):
+    if merge:
+        others, refs = refs[0], refs[1:]
     if mode == "single":
-        own, own_s, tp, right, out, trs, placed = refs
+        own, own_s, tp, right, *outs, placed = refs
 
         def place(i, _):
             for y in range(2):
@@ -69,7 +72,8 @@
 
         lax.fori_loop(0, 72, place, 0, unroll=8)
     else:
-        packs, ex, out, trs = refs[:3], refs[3], refs[4], refs[5]
+        packs, ex, outs = refs[:3], refs[3], refs[4:]
+    trs = outs[-1]
     wide = mode == "wide"
     parts = 3 if wide else 1
     count = 16 * parts
@@ -96,7 +100,7 @@
             after = pltpu.roll(after, 4, 0) if part == 0 else after
         return jnp.where(row_of < 6, pltpu.roll(links(part, y, i), 6, 0), after)
 
-    trs[12 * count :] = jnp.zeros((4 * count, 128), F32)
+    trs[6 * count :] = jnp.zeros((2 * count, 128), F32)
     for part in range(parts):
         inner = jnp.where(row_of >= 6, 1, 0)
         leaves = (row_of % 2, 1 - row_of // 2 % 2 if part == 2 else inner, 1, 0)
@@ -115,7 +119,7 @@
                 values = [links(part, y, i) for i in at]
                 return as_matrix([zroll(v, 1) for v in values] if step == 3 else values)
 
-            for p, (m, n) in enumerate(PAIRS):
+            for p, (m, n) in enumerate(PAIRS[plane] for plane in planes):
                 a = flat(mm(look(m, None), look(n, m)))
                 b = flat(mm(look(n, None), look(m, n)))
                 re = im = None
@@ -129,7 +133,7 @@
                 for k, value in enumerate((re, im)):
                     row = (2 * p + k) * count + 16 * part + 8 * y
                     trs[row : row + 8] = jnp.where(frozen, value * (1.0 / 3.0), 0.0)
-    for r in range(count):
+    for r in range(count if merge else 0):
         place = r
         if wide:
             part, y, row = r // 16, r // 8 % 2, r % 8
@@ -139,7 +143,8 @@
                 partner, x = row // 4, (0, 5)[row // 2 % 2]
             t = (3, 0)[row % 2] if partner else 1 + row % 2
             place = (6 * y + x) * 4 + t
-        out[place] = trs[pl.ds(r, 16, stride=count), :].astype(BF16)
+        halves = [ref[pl.ds(r, 8, stride=count), :] for ref in (others, trs)]
+        outs[0][place] = jnp.concatenate(halves, axis=0).astype(BF16)
 
 
 def staple_kernel(mode, ya, *refs):
@@ -210,13 +215,23 @@
                 out[6 * m + 2 * j + 1, c] = value
 
 
+def even_rows():
+    return lax.broadcasted_iota(jnp.int32, (8, 128), 0) % 2 == 0
+
+
+def exchanged(a, b, even):
+    return jnp.where(even, a, pltpu.roll(b, 1, 0)), jnp.where(even, pltpu.roll(a, 7, 0), b)
+
+
 def unpack_kernel(x, own, *rows):
+    even = even_rows()
+
     def body(i, _):
-        for y in range(2):
-            for t in range(2):
-                at = 8 * t + y
-                own[i, y, pl.ds(t, 4, stride=2)] = x[i, pl.ds(at, 4, stride=2)]
-                if rows:
+        own[i, 0], own[i, 1] = exchanged(x[i, 0:8], x[i, 8:16], even)
+        if rows:
+            for y in range(2):
+                for t in range(2):
+                    at = 8 * t + y
                     rows[0][i, y, t : t + 1] = x[i, at : at + 1]
                     rows[1][i, y, t : t + 1] = x[i, at + 6 : at + 7]
         return 0
@@ -241,7 +256,11 @@
         w_in, b_in, w_out, b_out = outs[4 * layer : 4 * layer + 4]
         for k in range(27):
             taps = [conv_in[layer, 3 * k + z].astype(F32) for z in range(3)]
-            big[16 * k : 16 * k + 12, 0:192] = jnp.concatenate(taps, axis=1)
+            taps = jnp.concatenate(taps, axis=1)
+            for half, planes in enumerate(HALVES[layer]):
+                for a, plane in enumerate(planes):
+                    at = 16 * k + 8 * half + 2 * a
+                    big[at : at + 2, 0:192] = taps[2 * plane : 2 * plane + 2]
         w_in[...] = jnp.transpose(big[...])[0:192, 0:432].astype(BF16)
         small[0:64, 0:24] = conv_out[layer].astype(F32)
         w_out[...] = jnp.transpose(small[...])[0:24, 0:64].astype(BF16)
@@ -251,23 +270,37 @@
         b_out[...] = jnp.transpose(small[...])[0:24]
 
 
-def last_kernel(ya, own, staples, f, f_s, w_in, b_in, w_out, b_out, packed, out, wts):
-    update(ya, own, staples, f, f_s, w_in, b_in, w_out, b_out, out, wts)
-
-    def body(i, _):
-        for y in range(2):
-            for t in range(2):
-                packed[i, pl.ds(8 * t + y, 4, stride=2)] = out[i, y, pl.ds(t, 4, stride=2)]
-        return 0
-
-    lax.fori_loop(0, 72, body, 0, unroll=8)
+def last_kernel(ya, own, staples, f, f_s, w_in, b_in, w_out, b_out, out, packed, wts, sems):
+    even = even_rows()
+
+    def store(i, y, value, old):
+        at_0 = y == 0
+        tiles = jnp.where(at_0, value, old), jnp.where(at_0, old, value)
+        packed[i, 0:8], packed[i, 8:16] = exchanged(*tiles, even)
+
+    def copy(m):
+        part = slice(18 * m, 18 * m + 18)
+        return pltpu.make_async_copy(packed.at[part], out.at[part], sems.at[m])
+
+    update(
+        ya, own, staples, f, f_s, w_in, b_in, w_out, b_out, wts, store,
+        done=lambda m: copy(m).start(),
+    )
+    for m in range(4):
+        copy(m).wait()
 
 
 def final_kernel(ya, own, staples, f, f_s, w_in, b_in, w_out, b_out, out, sent, wts):
-    update(ya, own, staples, f, f_s, w_in, b_in, w_out, b_out, out, wts, sent)
-
-
-def update(ya, own, staples, f, f_s, w_in, b_in, w_out, b_out, out, wts, sent=None):
+    def store(i, y, value, old):
+        out[i, y] = value
+        out[i, 1 - y] = old
+
+    update(ya, own, staples, f, f_s, w_in, b_in, w_out, b_out, wts, store, sent)
+
+
+def update(
+    ya, own, staples, f, f_s, w_in, b_in, w_out, b_out, wts, store, sent=None, done=None
+):
     places = ((1, 1), (0, 0), (0, 1), (1, 0))
     sites = [(y, r // 2, r % 2) for y in range(2) for r in range(8)]
     columns = []
@@ -309,9 +342,9 @@
             for c in range(9):
                 sent[9 * m + c] = low[c]
         for c, value in enumerate(rotated(low, link)):
-            out[18 * m + c, y] = value
-        for c in range(18):
-            out[18 * m + c, 1 - y] = own[18 * m + c, 1 - y]
+            store(18 * m + c, y, value, own[18 * m + c, 1 - y])
+        if done is not None:
+            done(m)
 
 
 def rotated(low, link):
@@ -444,17 +477,19 @@
     )(own)
 
 
-def run_traces(mode, ya, *inputs):
-    parts = 3 if mode == "wide" else 1
+def run_traces(mode, half, ya, *inputs):
+    rows = (16 if mode == "single" else 48 if mode == "wide" else 16)
+    channels = (8 * rows, 128)
     placed = [pltpu.VMEM((72, 2, 8, 128), F32)] if mode == "single" else []
+    shape = ((rows, 16, 128), BF16) if half else (channels, F32)
     return pl.pallas_call(
-        functools.partial(trace_kernel, mode),
-        out_shape=jax.ShapeDtypeStruct((16 * parts, 16, 128), BF16),
+        functools.partial(trace_kernel, mode, HALVES[mode != "single"][half], half == 1),
+        out_shape=jax.ShapeDtypeStruct(*shape),
         in_specs=[SM] + [VM] * len(inputs),
         out_specs=VM,
-        scratch_shapes=[pltpu.VMEM((256 * parts, 128), F32)] + placed,
+        scratch_shapes=([pltpu.VMEM(channels, F32)] if half else []) + placed,
         compiler_params=params(10),
-        cost_estimate=pl.CostEstimate(flops=8_000_000, bytes_accessed=6_000_000, transcendentals=0),
+        cost_estimate=pl.CostEstimate(flops=4_000_000, bytes_accessed=4_000_000, transcendentals=0),
         name="traces",
     )(ya, *inputs)
 
@@ -481,8 +516,12 @@
         last_kernel if last else final_kernel,
         out_shape=[jax.ShapeDtypeStruct(shape, F32) for shape in shapes],
         in_specs=[SM] + [VM] * 8,
-        out_specs=[VM] * len(shapes),
-        scratch_shapes=([pltpu.VMEM((72, 2, 8, 128), F32)] if last else []) + weights,
+        out_specs=[pl.BlockSpec(memory_space=pl.ANY) if last else VM] + [VM] * (len(shapes) - 1),
+        scratch_shapes=(
+            [pltpu.VMEM((72, 16, 128), F32)] + weights + [pltpu.SemaphoreType.DMA((4,))]
+            if last
+            else weights
+        ),
         compiler_params=params(14),
         cost_estimate=pl.CostEstimate(flops=300_000_000, bytes_accessed=4_000_000, transcendentals=131072),
         name="rotate",
@@ -553,7 +592,8 @@
     h = jnp.concatenate([left, right], axis=2)
     h_s = step(h, "sub", 1)
     (tp,) = run_unpack(tp_raw, False)
-    tr = run_traces("single", ya[0], own, own_s, tp, right).reshape(2, 4, 2, 16, 128)
+    half = run_traces("single", 0, ya[0], own, own_s, own, right)
+    tr = run_traces("single", 1, ya[0], half, own, own_s, tp, right).reshape(2, 4, 2, 16, 128)
     far = other_rows(right)
     full = other_traces(tr)
     full, co, far, tail = lax.optimization_barrier((full, co, far, tail))
@@ -577,12 +617,14 @@
     def staples_1():
         return run_staples("packs", ya[1], pack_0, pack_1, other_0, other_1)
 
-    if lax.axis_size("tm") == 2:
-        f = run_traces("wide", ya[1], pack_0, pack_1, other_0, ex).reshape(2, 6, 4, 16, 128)
+    mode = "wide" if lax.axis_size("tm") == 2 else "packs"
+    half = run_traces(mode, 0, ya[1], pack_0, pack_1, pack_0, ex)
+    tr = run_traces(mode, 1, ya[1], half, pack_0, pack_1, other_0, ex)
+    if mode == "wide":
+        f = tr.reshape(2, 6, 4, 16, 128)
         staples = staples_1()
     else:
-        tr = run_traces("packs", ya[1], pack_0, pack_1, other_0, ex).reshape(2, 4, 2, 16, 128)
-        f, staples = rim(other_traces(tr), staples_1)
+        f, staples = rim(other_traces(tr.reshape(2, 4, 2, 16, 128)), staples_1)
     f_s = step(f, "sub", 1)
     (out,) = run_final(ya[1], own, staples, f, f_s, *weights[4:], True)
     return out.reshape(4, 18, 2, 4, 2, 128)

time: 61.3 us -> 59.7 us (0.974)
  waiting for transfers between devices: 16.8 us -> 13.3 us
  starting transfers between devices: 21.4 us -> 22.3 us
  Pallas kernels: 17.4 us -> 18.2 us
    ppermute x14, waiting for transfers between devices: 6.43 us -> 3.71 us  [step(): lax.ppermute(value, axis, [((i + by) % count, i) for i in range(count)])]
    ppermute x7, starting transfers between devices: 9.12 us -> 10.6 us  [diagonal(): return lax.ppermute(value, ('space', 'tm'), pairs)]
    pallas_call x2 -> x4, Pallas kernels: 5.04 us -> 6.31 us  [run_traces(): pl.pallas_call(functools.partial(trace_kernel, mode, HALVES[mode != 'sing...]
    ppermute x7, waiting for transfers between devices: 10.4 us -> 9.63 us  [diagonal(): return lax.ppermute(value, ('space', 'tm'), pairs)]
    ppermute x14, starting transfers between devices: 12.3 us -> 11.7 us  [step(): lax.ppermute(value, axis, [((i + by) % count, i) for i in range(count)])]
  transfers between devices with their start and end apart: 21 -> 21, of which waited for: 8 -> 6; matrix products, arithmetic and copies ran while one was open for 7% -> 7% of each run, Pallas kernels for 21% -> 24%
where the time goes in v5:
time: 59.7 us; the launch traced here: 59.4 us
  starting transfers between devices  22.3 us (37%)
  Pallas kernels  18.2 us (30%)
  waiting for transfers between devices  13.3 us (22%)
  local copies, waits for them, and re-layouts  3.99 us (7%)
  other arithmetic  1.22 us (2%)
    ppermute x14, starting transfers between devices, step(): lax.ppermute(value, axis, [((i + by) % count, i) for i in range(count)])  11.7 us
    ppermute x7, starting transfers between devices, diagonal(): return lax.ppermute(value, ('space', 'tm'), pairs)  10.6 us
    ppermute x7, waiting for transfers between devices, diagonal(): return lax.ppermute(value, ('space', 'tm'), pairs)  9.63 us
    pallas_call x4, Pallas kernels, run_traces(): pl.pallas_call(functools.partial(trace_kernel, mode, HALVES[mode != 'sing...  6.31 us
    pallas_call x2, Pallas kernels, run_staples(): pl.pallas_call(functools.partial(staple_kernel, mode), out_shape=jax.Shap...  5.11 us
    pallas_call x2, Pallas kernels, run_final(): pl.pallas_call(last_kernel if last else final_kernel, out_shape=[jax.Shap...  4.33 us
    ppermute x14, waiting for transfers between devices, step(): lax.ppermute(value, axis, [((i + by) % count, i) for i in range(count)])  3.71 us
    unnamed x12, local copies, waits for them, and re-layouts  2.8 us
  transfers between devices with their start and end apart: 21, of which 6 were waited for; matrix products, arithmetic and copies ran while one was open for 7% of the time, Pallas kernels for 24%

profile of v5, /device:TPU:0, one launch (start us, length us, event | category | flops | bytes accessed | tf_op | source)
XLA Modules:
  0.0 59.4 jit_solution(17058544701359842272)
XLA Ops:
  0.0 2.9 %collective-permute-start.3 = (f32[4,18,2,4,2,128]{5,4,3,2,1,0:T(2,128)}, f32[4,18,2,4,2,128]{5,4,3,2,1,0:T(2,128)S(1)}, u32[]{:S(2)}, u32[]{:S(2)}) collective-permute-start(f32[4,18,2,4,2,128]{5,4,3,2,1,0:T(2,128)} %param.6), channel_id=1, source_target_pairs={{2,0},{0,2},{6,4},{4,6},{10,8},{8,10},{14,12},{12,14},{3,1},{1,3},... | collective-permute-start | bytes 1769480 | tf_op jit(solution)/shard_map/ppermute | solution.py:556
  2.9 1.1 %copy-done = f32[4,18,2,4,2,128]{5,4,3,2,1,0:T(2,128)S(1)} copy-done((f32[4,18,2,4,2,128]{5,4,3,2,1,0:T(2,128)S(1)}, f32[4,18,2,4,2,128]{5,4,3,2,1,0:T(2,128)}, u32[]{:S(2)}) %copy-start) | copy-done | bytes 589848
  4.4 3.7 %collective-permute-start = (f32[72,2,2,128]{3,2,1,0:T(2,128)S(1)}, f32[72,2,2,128]{3,2,1,0:T(2,128)S(1)}, u32[]{:S(2)}, u32[]{:S(2)}) collective-permute-start(f32[72,2,2,128]{3,2,1,0:T(2,128)S(1)} %get-tuple-element.40), channel_id=1, source_target_pairs={{4,0},{8,4},{12,8},{0,12},{5,1},{9,5},{13,9},{1,13},{6,2},{10,6},{... | collective-permute-start | bytes 442376 | tf_op jit(solution)/shard_map/ppermute | solution.py:546
  8.2 0.9 %copy.15 = f32[72,2,6,128]{3,0,2,1:T(8,128)} copy(f32[72,2,6,128]{3,2,1,0:T(8,128)S(1)} %tail.1) | data formatting | bytes 884736 | tf_op jit(solution)/shard_map/tail/pallas_call | solution.py:469
  9.1 3.8 %collective-permute-start.7 = (f32[72,2,6,128]{3,0,2,1:T(8,128)}, f32[72,2,6,128]{3,0,2,1:T(8,128)S(1)}, u32[]{:S(2)}, u32[]{:S(2)}) collective-permute-start(f32[72,2,6,128]{3,0,2,1:T(8,128)} %copy.15), channel_id=1, source_target_pairs={{4,0},{8,4},{12,8},{0,12},{5,1},{9,5},{13,9},{1,13},{6,2},{10,6},{... | collective-permute-start | bytes 1327112 | tf_op jit(solution)/shard_map/ppermute | solution.py:546
  13.0 1.6 %copy.13.conv_in = bf16[2,81,12,64]{3,2,1,0:T(8,128)(2,1)S(1)} copy(bf16[2,81,12,64]{1,3,2,0:T(8,128)(2,1)} %param.8) | data formatting | bytes 497664 | tf_op args[2]
  14.6 0.5 weights.1
  15.1 1.0 %fusion = s32[2,4]{1,0:T(2,128)S(1)} fusion(s32[2,4,2,4,4]{4,3,2,1,0:T(4,128)} %param.7, s32[]{:T(128)S(6)} %select_n.16, s32[]{:T(128)S(6)} %select_n.17, s32[]{:T(128)S(6)} %select_n.18), kind=kLoop, calls=%fused_computation.7 | loop fusion | flops 16 | bytes 76 | tf_op jit(solution)/shard_map/jit(_where)/select_n | solution.py:575
  16.1 0.5 collective-permute-done.1
  16.7 0.6 %collective-permute-start.5 = (f32[18,2,2,128]{3,2,1,0:T(2,128)S(1)}, f32[18,2,2,128]{3,2,1,0:T(2,128)S(1)}, u32[]{:S(2)}, u32[]{:S(2)}) collective-permute-start(f32[18,2,2,128]{3,2,1,0:T(2,128)S(1)} %pad_maximum_fusion.2), channel_id=1, source_target_pairs={{2,0},{0,2},{6,4},{4,6},{10,8},{8,10},{14,12},{12,14},{3,1},{1,3},... | collective-permute-start | bytes 110600 | tf_op jit(solution)/shard_map/ppermute | solution.py:556
  17.3 1.5 %collective-permute-start.6 = (f32[72,2,1,2,128]{4,3,1,0,2:T(2,128)S(1)}, f32[72,2,1,2,128]{4,3,1,0,2:T(2,128)S(1)}, u32[]{:S(2)}, u32[]{:S(2)}) collective-permute-start(f32[72,2,1,2,128]{4,3,1,0,2:T(2,128)S(1)} %bitcast.16), channel_id=1, source_target_pairs={{2,0},{0,2},{6,4},{4,6},{10,8},{8,10},{14,12},{12,14},{3,1},{1,3},... | collective-permute-start | bytes 442376 | tf_op jit(solution)/shard_map/ppermute | solution.py:556
  18.9 1.1 %traces.4.refs_0_ = f32[128,128]{1,0:T(8,128)S(1)} custom-call(s32[4]{0:T(128)S(1)} %get-tuple-element.79.ya, f32[72,2,8,128]{3,2,1,0:T(8,128)S(1)} %get-tuple-element.51.refs_0_.refs_2_.refs_1_.own, f32[72,2,8,128]{3,2,1,0:T(8,128)S(1)} %collective-permute-done.2.refs_1_.refs_2_, f32[72,2,8,128]{3,2,1,0:T(8,128)S(1)} %get-tuple-element.51.refs_0_.refs_2_.refs_1_.own, ...), custom_call_target="tpu_custom_call" | custom-call | flops 4000000 | bytes 4000000 | tf_op jit(solution)/shard_map/traces/pallas_call | solution.py:485
  20.0 1.2 %traces.5 = bf16[16,16,128]{2,1,0:T(8,128)(2,1)S(1)} custom-call(s32[4]{0:T(128)S(1)} %get-tuple-element.79.ya, f32[128,128]{1,0:T(8,128)S(1)} %traces.4.refs_0_, f32[72,2,8,128]{3,2,1,0:T(8,128)S(1)} %get-tuple-element.51.refs_0_.refs_2_.refs_1_.own, f32[72,2,8,128]{3,2,1,0:T(8,128)S(1)} %collective-permute-done.2.refs_1_.refs_2_, ...), custom_call_target="tpu_custom_call" | custom-call | flops 4000000 | bytes 4000000 | tf_op jit(solution)/shard_map/traces/pallas_call | solution.py:485
  21.2 0.6 %collective-permute-start.4 = (bf16[2,4,2,16,128]{4,3,2,1,0:T(8,128)(2,1)S(1)}, bf16[2,4,2,16,128]{4,3,2,1,0:T(8,128)(2,1)S(1)}, u32[]{:S(2)}, u32[]{:S(2)}) collective-permute-start(bf16[2,4,2,16,128]{4,3,2,1,0:T(8,128)(2,1)S(1)} %bitcast.21), channel_id=1, source_target_pairs={{2,0},{0,2},{6,4},{4,6},{10,8},{8,10},{14,12},{12,14},{3,1},{1,3},... | collective-permute-start | bytes 196616 | tf_op jit(solution)/shard_map/ppermute | solution.py:556
  22.0 3.5 %collective-permute-done.4 = bf16[2,4,2,16,128]{4,3,2,1,0:T(8,128)(2,1)S(1)} collective-permute-done((bf16[2,4,2,16,128]{4,3,2,1,0:T(8,128)(2,1)S(1)}, bf16[2,4,2,16,128]{4,3,2,1,0:T(8,128)(2,1)S(1)}, u32[]{:S(2)}, u32[]{:S(2)}) %collective-permute-start.4) | collective-permute-done | bytes 65568 | tf_op jit(solution)/shard_map/ppermute | solution.py:556
  25.6 0.6 collective-permute-start.12
  26.1 2.7 %collective-permute-start.9 = (bf16[2,1,4,16,128]{4,3,2,1,0:T(8,128)(2,1)S(1)}, bf16[2,1,4,16,128]{4,3,2,1,0:T(8,128)(2,1)S(1)}, u32[]{:S(2)}, u32[]{:S(2)}) collective-permute-start(bf16[2,1,4,16,128]{4,3,2,1,0:T(8,128)(2,1)S(1)} %get-tuple-element.75), channel_id=1, source_target_pairs={{4,0},{8,4},{12,8},{0,12},{5,1},{9,5},{13,9},{1,13},{6,2},{10,6},{... | collective-permute-start | bytes 98312 | tf_op jit(solution)/shard_map/ppermute | solution.py:546
  28.9 1.4 %collective-permute-start.14 = (f32[72,2,3,2,128]{4,0,3,2,1:T(8,128)S(1)}, f32[72,2,3,2,128]{4,0,3,2,1:T(8,128)S(1)}, u32[]{:S(2)}, u32[]{:S(2)}) collective-permute-start(f32[72,2,3,2,128]{4,0,3,2,1:T(8,128)S(1)} %bitcast.28), channel_id=1, source_target_pairs={{2,0},{0,2},{6,4},{4,6},{10,8},{8,10},{14,12},{12,14},{3,1},{1,3},... | collective-permute-start | bytes 1327112 | tf_op jit(solution)/shard_map/ppermute | solution.py:556
  30.2 2.6 %staples.2 = f32[24,18,8,128]{3,2,1,0:T(8,128)S(1)} custom-call(s32[4]{0:T(128)S(1)} %get-tuple-element.79.ya, f32[72,2,8,128]{3,2,1,0:T(8,128)S(1)} %get-tuple-element.51.refs_0_.refs_2_.refs_1_.own, f32[72,2,8,128]{3,2,1,0:T(8,128)S(1)} %collective-permute-done.2.refs_1_.refs_2_, f32[72,2,8,128]{3,2,1,0:T(8,128)S(1)} %unpack.3.refs_3_.refs_2_.tp, ...), custom_call_target="tpu_custom_call" | custom-call | flops 20000000 | bytes 16000000 | tf_op jit(solution)/shard_map/staples/pallas_call | solution.py:498
  32.8 1.7 %collective-permute-done.8 = bf16[2,1,4,16,128]{4,3,2,1,0:T(8,128)(2,1)S(1)} collective-permute-done((bf16[2,1,4,16,128]{4,3,2,1,0:T(8,128)(2,1)S(1)}, bf16[2,1,4,16,128]{4,3,2,1,0:T(8,128)(2,1)S(1)}, u32[]{:S(2)}, u32[]{:S(2)}) %collective-permute-start.8) | collective-permute-done | bytes 32800 | tf_op jit(solution)/shard_map/ppermute | solution.py:546
  34.7 1.4 %collective-permute-done.13.f_s = bf16[2,6,4,16,128]{4,3,2,1,0:T(8,128)(2,1)S(1)} collective-permute-done((bf16[2,6,4,16,128]{4,3,2,1,0:T(8,128)(2,1)S(1)}, bf16[2,6,4,16,128]{4,3,2,1,0:T(8,128)(2,1)S(1)}, u32[]{:S(2)}, u32[]{:S(2)}) %collective-permute-start.13) | collective-permute-done | bytes 196640 | tf_op jit(solution)/shard_map/ppermute | solution.py:546
  36.1 1.8 %rotate.2 = (f32[72,2,8,128]{3,2,1,0:T(8,128)S(1)}, f32[36,8,128]{2,1,0:T(8,128)S(1)}) custom-call(s32[4]{0:T(128)S(1)} %get-tuple-element.79.ya, f32[72,2,8,128]{3,2,1,0:T(8,128)S(1)} %get-tuple-element.51.refs_0_.refs_2_.refs_1_.own, f32[24,18,8,128]{3,2,1,0:T(8,128)S(1)} %staples.2, bf16[2,6,4,16,128]{4,3,2,1,0:T(8,128)(2,1)S(1)} %constant_dynamic-update-slice_fusion.f, ...), custom_call_target="tpu_custom_call" | custom-call | flops 300000000 | bytes 4000000 | tf_op jit(solution)/shard_map/rotate/pallas_call | solution.py:515
  37.9 2.2 %collective-permute-start.17 = (f32[36,4,2,128]{3,2,1,0:T(2,128)S(1)}, f32[36,4,2,128]{3,2,1,0:T(2,128)S(1)}, u32[]{:S(2)}, u32[]{:S(2)}) collective-permute-start(f32[36,4,2,128]{3,2,1,0:T(2,128)S(1)} %bitcast.26), channel_id=1, source_target_pairs={{6,0},{4,2},{10,4},{8,6},{14,8},{12,10},{2,12},{0,14},{7,1},{5,3},... | collective-permute-start | bytes 442376 | tf_op jit(solution)/shard_map/ppermute | solution.py:556
  40.2 1.4 %collective-permute-start.16 = (f32[36,4,2,128]{3,2,1,0:T(2,128)S(1)}, f32[36,4,2,128]{3,2,1,0:T(2,128)S(1)}, u32[]{:S(2)}, u32[]{:S(2)}) collective-permute-start(f32[36,4,2,128]{3,2,1,0:T(2,128)S(1)} %bitcast.27), channel_id=1, source_target_pairs={{2,0},{0,2},{6,4},{4,6},{10,8},{8,10},{14,12},{12,14},{3,1},{1,3},... | collective-permute-start | bytes 442376 | tf_op jit(solution)/shard_map/ppermute | solution.py:556
  41.8 3.8 %collective-permute-done.17 = f32[36,4,2,128]{3,2,1,0:T(2,128)S(1)} collective-permute-done((f32[36,4,2,128]{3,2,1,0:T(2,128)S(1)}, f32[36,4,2,128]{3,2,1,0:T(2,128)S(1)}, u32[]{:S(2)}, u32[]{:S(2)}) %collective-permute-start.17) | collective-permute-done | bytes 147488 | tf_op jit(solution)/shard_map/ppermute | solution.py:556
  45.6 2.4 %collective-permute-done.16 = f32[36,4,2,128]{3,2,1,0:T(2,128)S(1)} collective-permute-done((f32[36,4,2,128]{3,2,1,0:T(2,128)S(1)}, f32[36,4,2,128]{3,2,1,0:T(2,128)S(1)}, u32[]{:S(2)}, u32[]{:S(2)}) %collective-permute-start.16) | collective-permute-done | bytes 147488 | tf_op jit(solution)/shard_map/ppermute | solution.py:556
  47.9 1.5 %shift.1 = (f32[72,2,8,128]{3,2,1,0:T(8,128)S(1)}, f32[216,8,128]{2,1,0:T(8,128)S(1)}, f32[216,8,128]{2,1,0:T(8,128)S(1)}, f32[72,2,8,128]{3,2,1,0:T(8,128)S(1)}) custom-call(s32[4]{0:T(128)S(1)} %get-tuple-element.79.ya, f32[72,2,8,128]{3,2,1,0:T(8,128)S(1)} %get-tuple-element.63.own, f32[72,2,2,128]{3,2,1,0:T(2,128)S(1)} %collective-permute-done.refs_3_.refs_4_.right, ...), custom_call_target="tpu_custom_call" | custom-call | flops 8000000 | bytes 6000000 | tf_op jit(solution)/shard_map/shift/pallas_call | solution.py:533
  49.5 0.5 collective-permute-start.19
  50.0 2.0 %traces.6.refs_0_ = f32[384,128]{1,0:T(8,128)S(1)} custom-call(s32[4]{0:T(128)S(1)} %get-tuple-element.80.ya, f32[216,8,128]{2,1,0:T(8,128)S(1)} %get-tuple-element.68.refs_0_.refs_2_.refs_1_, f32[216,8,128]{2,1,0:T(8,128)S(1)} %get-tuple-element.69.refs_1_.refs_2_, f32[216,8,128]{2,1,0:T(8,128)S(1)} %get-tuple-element.68.refs_0_.refs_2_.refs_1_, ...), custom_call_target="tpu_custom_call" | custom-call | flops 4000000 | bytes 4000000 | tf_op jit(solution)/shard_map/traces/pallas_call | solution.py:485
  52.0 2.0 %traces.7 = bf16[48,16,128]{2,1,0:T(8,128)(2,1)S(1)} custom-call(s32[4]{0:T(128)S(1)} %get-tuple-element.80.ya, f32[384,128]{1,0:T(8,128)S(1)} %traces.6.refs_0_, f32[216,8,128]{2,1,0:T(8,128)S(1)} %get-tuple-element.68.refs_0_.refs_2_.refs_1_, f32[216,8,128]{2,1,0:T(8,128)S(1)} %get-tuple-element.69.refs_1_.refs_2_, ...), custom_call_target="tpu_custom_call" | custom-call | flops 4000000 | bytes 4000000 | tf_op jit(solution)/shard_map/traces/pallas_call | solution.py:485
  54.2 2.5 %staples.3 = f32[24,18,8,128]{3,2,1,0:T(8,128)S(1)} custom-call(s32[4]{0:T(128)S(1)} %get-tuple-element.80.ya, f32[216,8,128]{2,1,0:T(8,128)S(1)} %get-tuple-element.68.refs_0_.refs_2_.refs_1_, f32[216,8,128]{2,1,0:T(8,128)S(1)} %get-tuple-element.69.refs_1_.refs_2_, f32[216,8,128]{2,1,0:T(8,128)S(1)} %collective-permute-done.18.refs_2_.refs_3_, ...), custom_call_target="tpu_custom_call" | custom-call | flops 20000000 | bytes 16000000 | tf_op jit(solution)/shard_map/staples/pallas_call | solution.py:498
  56.8 2.5 %rotate.3 = f32[72,16,128]{2,1,0:T(8,128)} custom-call(s32[4]{0:T(128)S(1)} %get-tuple-element.80.ya, f32[72,2,8,128]{3,2,1,0:T(8,128)S(1)} %get-tuple-element.67.own, f32[24,18,8,128]{3,2,1,0:T(8,128)S(1)} %staples.3, bf16[2,6,4,16,128]{4,3,2,1,0:T(8,128)(2,1)S(1)} %bitcast.18, bf16[2,6,4,16,128]{4,3,2,1,0:T(8,128)(2,1)S(1)} %collective-permute-done.20.f_s, ...), custom_call_target="tpu_custom_call" | custom-call | flops 300000000 | bytes 4000000 | tf_op jit(solution)/shard_map/rotate/pallas_call | solution.py:515
  (48 shorter events, 1.6 us)
Async XLA Ops:
  0.0 18.8 %collective-permute-start.3 = (f32[4,18,2,4,2,128]{5,4,3,2,1,0:T(2,128)}, f32[4,18,2,4,2,128]{5,4,3,2,1,0:T(2,128)S(1)}, u32[]{:S(2)}, u32[]{:S(2)}) collective-permute-start(f32[4,18,2,4,2,128]{5,4,3,2,1,0:T(2,128)} %param.6), channel_id=1, source_target_pairs={{2,0},{0,2},{6,4},{4,6},{10,8},{8,10},{14,12},{12,14},{3,1},{1,3},... | collective-permute-start | bytes 1769480 | tf_op jit(solution)/shard_map/ppermute | solution.py:556
  2.9 1.1 %copy-start = (f32[4,18,2,4,2,128]{5,4,3,2,1,0:T(2,128)S(1)}, f32[4,18,2,4,2,128]{5,4,3,2,1,0:T(2,128)}, u32[]{:S(2)}) copy-start(f32[4,18,2,4,2,128]{5,4,3,2,1,0:T(2,128)} %param.6) | copy-start | bytes 1769476
  4.0 8.9 %copy-start.3 = (bf16[2,64,24]{1,2,0:T(8,128)(2,1)S(1)}, bf16[2,64,24]{1,2,0:T(8,128)(2,1)}, u32[]{:S(2)}) copy-start(bf16[2,64,24]{1,2,0:T(8,128)(2,1)} %param.10) | copy-start | bytes 18436
  4.3 10.2 %copy-start.1 = (f32[2,64]{1,0:T(2,128)S(1)}, f32[2,64]{1,0:T(2,128)}, u32[]{:S(2)}) copy-start(f32[2,64]{1,0:T(2,128)} %bias_in.1) | copy-start | bytes 1540
  4.4 10.2 %copy-start.2 = (f32[2,24]{1,0:T(2,128)S(1)}, f32[2,24]{1,0:T(2,128)}, u32[]{:S(2)}) copy-start(f32[2,24]{1,0:T(2,128)} %bias_out.1) | copy-start | bytes 580
  4.4 14.6 %collective-permute-start.2 = (f32[72,2,8,128]{3,2,1,0:T(8,128)S(1)}, f32[72,2,8,128]{3,2,1,0:T(8,128)S(1)}, u32[]{:S(2)}, u32[]{:S(2)}) collective-permute-start(f32[72,2,8,128]{3,2,1,0:T(8,128)S(1)} %get-tuple-element.51.refs_0_.refs_2_.refs_1_.own), channel_id=1, source_target_pairs={{1,0},{0,1},{3,2},{2,3},{5,4},{4,5},{7,6},{6,7},{9,8},{8,9},{11,10... | collective-permute-start | bytes 1769480 | tf_op jit(solution)/shard_map/ppermute | solution.py:546
  4.4 11.7 %collective-permute-start = (f32[72,2,2,128]{3,2,1,0:T(2,128)S(1)}, f32[72,2,2,128]{3,2,1,0:T(2,128)S(1)}, u32[]{:S(2)}, u32[]{:S(2)}) collective-permute-start(f32[72,2,2,128]{3,2,1,0:T(2,128)S(1)} %get-tuple-element.40), channel_id=1, source_target_pairs={{4,0},{8,4},{12,8},{0,12},{5,1},{9,5},{13,9},{1,13},{6,2},{10,6},{... | collective-permute-start | bytes 442376 | tf_op jit(solution)/shard_map/ppermute | solution.py:546
  8.1 8.5 %collective-permute-start.1 = (f32[72,2,2,128]{3,2,1,0:T(2,128)S(1)}, f32[72,2,2,128]{3,2,1,0:T(2,128)S(1)}, u32[]{:S(2)}, u32[]{:S(2)}) collective-permute-start(f32[72,2,2,128]{3,2,1,0:T(2,128)S(1)} %get-tuple-element.41), channel_id=1, source_target_pairs={{12,0},{0,4},{4,8},{8,12},{13,1},{1,5},{5,9},{9,13},{14,2},{2,6},{... | collective-permute-start | bytes 442376 | tf_op jit(solution)/shard_map/ppermute | solution.py:546
  9.1 16.5 %collective-permute-start.7 = (f32[72,2,6,128]{3,0,2,1:T(8,128)}, f32[72,2,6,128]{3,0,2,1:T(8,128)S(1)}, u32[]{:S(2)}, u32[]{:S(2)}) collective-permute-start(f32[72,2,6,128]{3,0,2,1:T(8,128)} %copy.15), channel_id=1, source_target_pairs={{4,0},{8,4},{12,8},{0,12},{5,1},{9,5},{13,9},{1,13},{6,2},{10,6},{... | collective-permute-start | bytes 1327112 | tf_op jit(solution)/shard_map/ppermute | solution.py:546
  16.7 8.8 %collective-permute-start.5 = (f32[18,2,2,128]{3,2,1,0:T(2,128)S(1)}, f32[18,2,2,128]{3,2,1,0:T(2,128)S(1)}, u32[]{:S(2)}, u32[]{:S(2)}) collective-permute-start(f32[18,2,2,128]{3,2,1,0:T(2,128)S(1)} %pad_maximum_fusion.2), channel_id=1, source_target_pairs={{2,0},{0,2},{6,4},{4,6},{10,8},{8,10},{14,12},{12,14},{3,1},{1,3},... | collective-permute-start | bytes 110600 | tf_op jit(solution)/shard_map/ppermute | solution.py:556
  17.3 8.2 %collective-permute-start.6 = (f32[72,2,1,2,128]{4,3,1,0,2:T(2,128)S(1)}, f32[72,2,1,2,128]{4,3,1,0,2:T(2,128)S(1)}, u32[]{:S(2)}, u32[]{:S(2)}) collective-permute-start(f32[72,2,1,2,128]{4,3,1,0,2:T(2,128)S(1)} %bitcast.16), channel_id=1, source_target_pairs={{2,0},{0,2},{6,4},{4,6},{10,8},{8,10},{14,12},{12,14},{3,1},{1,3},... | collective-permute-start | bytes 442376 | tf_op jit(solution)/shard_map/ppermute | solution.py:556
  21.2 4.3 %collective-permute-start.4 = (bf16[2,4,2,16,128]{4,3,2,1,0:T(8,128)(2,1)S(1)}, bf16[2,4,2,16,128]{4,3,2,1,0:T(8,128)(2,1)S(1)}, u32[]{:S(2)}, u32[]{:S(2)}) collective-permute-start(bf16[2,4,2,16,128]{4,3,2,1,0:T(8,128)(2,1)S(1)} %bitcast.21), channel_id=1, source_target_pairs={{2,0},{0,2},{6,4},{4,6},{10,8},{8,10},{14,12},{12,14},{3,1},{1,3},... | collective-permute-start | bytes 196616 | tf_op jit(solution)/shard_map/ppermute | solution.py:556
  21.9 6.9 %collective-permute-start.11 = (f32[72,2,4,128]{3,2,1,0:T(4,128)S(1)}, f32[72,2,4,128]{3,2,1,0:T(4,128)S(1)}, u32[]{:S(2)}, u32[]{:S(2)}) collective-permute-start(f32[72,2,4,128]{3,2,1,0:T(4,128)S(1)} %pad_maximum_fusion.refs_4_), channel_id=1, source_target_pairs={{1,0},{0,1},{3,2},{2,3},{5,4},{4,5},{7,6},{6,7},{9,8},{8,9},{11,10... | collective-permute-start | bytes 884744 | tf_op jit(solution)/shard_map/ppermute | solution.py:546
  25.5 4.7 %collective-permute-start.10 = (f32[72,2,8,128]{3,2,1,0:T(8,128)S(1)}, f32[72,2,8,128]{3,2,1,0:T(8,128)S(1)}, u32[]{:S(2)}, u32[]{:S(2)}) collective-permute-start(f32[72,2,8,128]{3,2,1,0:T(8,128)S(1)} %unpack.3.refs_3_.refs_2_.tp), channel_id=1, source_target_pairs={{1,0},{0,1},{3,2},{2,3},{5,4},{4,5},{7,6},{6,7},{9,8},{8,9},{11,10... | collective-permute-start | bytes 1769480 | tf_op jit(solution)/shard_map/ppermute | solution.py:546
  25.6 4.7 %collective-permute-start.12 = (f32[18,2,2,128]{3,2,1,0:T(2,128)S(1)}, f32[18,2,2,128]{3,2,1,0:T(2,128)S(1)}, u32[]{:S(2)}, u32[]{:S(2)}) collective-permute-start(f32[18,2,2,128]{3,2,1,0:T(2,128)S(1)} %collective-permute-done.5.refs_6_), channel_id=1, source_target_pairs={{1,0},{0,1},{3,2},{2,3},{5,4},{4,5},{7,6},{6,7},{9,8},{8,9},{11,10... | collective-permute-start | bytes 110600 | tf_op jit(solution)/shard_map/ppermute | solution.py:546
  26.1 6.7 %collective-permute-start.9 = (bf16[2,1,4,16,128]{4,3,2,1,0:T(8,128)(2,1)S(1)}, bf16[2,1,4,16,128]{4,3,2,1,0:T(8,128)(2,1)S(1)}, u32[]{:S(2)}, u32[]{:S(2)}) collective-permute-start(bf16[2,1,4,16,128]{4,3,2,1,0:T(8,128)(2,1)S(1)} %get-tuple-element.75), channel_id=1, source_target_pairs={{4,0},{8,4},{12,8},{0,12},{5,1},{9,5},{13,9},{1,13},{6,2},{10,6},{... | collective-permute-start | bytes 98312 | tf_op jit(solution)/shard_map/ppermute | solution.py:546
  28.8 5.7 %collective-permute-start.8 = (bf16[2,1,4,16,128]{4,3,2,1,0:T(8,128)(2,1)S(1)}, bf16[2,1,4,16,128]{4,3,2,1,0:T(8,128)(2,1)S(1)}, u32[]{:S(2)}, u32[]{:S(2)}) collective-permute-start(bf16[2,1,4,16,128]{4,3,2,1,0:T(8,128)(2,1)S(1)} %get-tuple-element.76), channel_id=1, source_target_pairs={{12,0},{0,4},{4,8},{8,12},{13,1},{1,5},{5,9},{9,13},{14,2},{2,6},{... | collective-permute-start | bytes 98312 | tf_op jit(solution)/shard_map/ppermute | solution.py:546
  28.9 12.8 %collective-permute-start.14 = (f32[72,2,3,2,128]{4,0,3,2,1:T(8,128)S(1)}, f32[72,2,3,2,128]{4,0,3,2,1:T(8,128)S(1)}, u32[]{:S(2)}, u32[]{:S(2)}) collective-permute-start(f32[72,2,3,2,128]{4,0,3,2,1:T(8,128)S(1)} %bitcast.28), channel_id=1, source_target_pairs={{2,0},{0,2},{6,4},{4,6},{10,8},{8,10},{14,12},{12,14},{3,1},{1,3},... | collective-permute-start | bytes 1327112 | tf_op jit(solution)/shard_map/ppermute | solution.py:556
  34.6 1.5 %collective-permute-start.13 = (bf16[2,6,4,16,128]{4,3,2,1,0:T(8,128)(2,1)S(1)}, bf16[2,6,4,16,128]{4,3,2,1,0:T(8,128)(2,1)S(1)}, u32[]{:S(2)}, u32[]{:S(2)}) collective-permute-start(bf16[2,6,4,16,128]{4,3,2,1,0:T(8,128)(2,1)S(1)} %constant_dynamic-update-slice_fusion.f), channel_id=1, source_target_pairs={{1,0},{0,1},{3,2},{2,3},{5,4},{4,5},{7,6},{6,7},{9,8},{8,9},{11,10... | collective-permute-start | bytes 589832 | tf_op jit(solution)/shard_map/ppermute | solution.py:546
  37.9 7.6 %collective-permute-start.17 = (f32[36,4,2,128]{3,2,1,0:T(2,128)S(1)}, f32[36,4,2,128]{3,2,1,0:T(2,128)S(1)}, u32[]{:S(2)}, u32[]{:S(2)}) collective-permute-start(f32[36,4,2,128]{3,2,1,0:T(2,128)S(1)} %bitcast.26), channel_id=1, source_target_pairs={{6,0},{4,2},{10,4},{8,6},{14,8},{12,10},{2,12},{0,14},{7,1},{5,3},... | collective-permute-start | bytes 442376 | tf_op jit(solution)/shard_map/ppermute | solution.py:556
  40.2 7.8 %collective-permute-start.16 = (f32[36,4,2,128]{3,2,1,0:T(2,128)S(1)}, f32[36,4,2,128]{3,2,1,0:T(2,128)S(1)}, u32[]{:S(2)}, u32[]{:S(2)}) collective-permute-start(f32[36,4,2,128]{3,2,1,0:T(2,128)S(1)} %bitcast.27), channel_id=1, source_target_pairs={{2,0},{0,2},{6,4},{4,6},{10,8},{8,10},{14,12},{12,14},{3,1},{1,3},... | collective-permute-start | bytes 442376 | tf_op jit(solution)/shard_map/ppermute | solution.py:556
  41.6 6.4 %collective-permute-start.15 = (f32[36,8,128]{2,1,0:T(8,128)S(1)}, f32[36,8,128]{2,1,0:T(8,128)S(1)}, u32[]{:S(2)}, u32[]{:S(2)}) collective-permute-start(f32[36,8,128]{2,1,0:T(8,128)S(1)} %get-tuple-element.66), channel_id=1, source_target_pairs={{4,0},{8,4},{12,8},{0,12},{5,1},{9,5},{13,9},{1,13},{6,2},{10,6},{... | collective-permute-start | bytes 442376 | tf_op jit(solution)/shard_map/ppermute | solution.py:546
  49.4 2.6 %collective-permute-start.18 = (f32[216,8,128]{2,1,0:T(8,128)S(1)}, f32[216,8,128]{2,1,0:T(8,128)S(1)}, u32[]{:S(2)}, u32[]{:S(2)}) collective-permute-start(f32[216,8,128]{2,1,0:T(8,128)S(1)} %get-tuple-element.68.refs_0_.refs_2_.refs_1_), channel_id=1, source_target_pairs={{1,0},{0,1},{3,2},{2,3},{5,4},{4,5},{7,6},{6,7},{9,8},{8,9},{11,10... | collective-permute-start | bytes 2654216 | tf_op jit(solution)/shard_map/ppermute | solution.py:546
  49.5 4.7 %collective-permute-start.19 = (f32[216,8,128]{2,1,0:T(8,128)S(1)}, f32[216,8,128]{2,1,0:T(8,128)S(1)}, u32[]{:S(2)}, u32[]{:S(2)}) collective-permute-start(f32[216,8,128]{2,1,0:T(8,128)S(1)} %get-tuple-element.69.refs_1_.refs_2_), channel_id=1, source_target_pairs={{1,0},{0,1},{3,2},{2,3},{5,4},{4,5},{7,6},{6,7},{9,8},{8,9},{11,10... | collective-permute-start | bytes 2654216 | tf_op jit(solution)/shard_map/ppermute | solution.py:546
  54.1 2.7 %collective-permute-start.20 = (bf16[2,6,4,16,128]{4,3,2,1,0:T(8,128)(2,1)S(1)}, bf16[2,6,4,16,128]{4,3,2,1,0:T(8,128)(2,1)S(1)}, u32[]{:S(2)}, u32[]{:S(2)}) collective-permute-start(bf16[2,6,4,16,128]{4,3,2,1,0:T(8,128)(2,1)S(1)} %bitcast.17), channel_id=1, source_target_pairs={{1,0},{0,1},{3,2},{2,3},{5,4},{4,5},{7,6},{6,7},{9,8},{8,9},{11,10... | collective-permute-start | bytes 589832 | tf_op jit(solution)/shard_map/ppermute | solution.py:546

commit v6 on v5

--- a/solution.py
+++ b/solution.py
@@ -60,7 +60,8 @@
 
 
 def trace_kernel(mode, planes, merge, ya, *refs):
-    if merge:
+    whole = len(planes) == 6
+    if merge and not whole:
         others, refs = refs[0], refs[1:]
     if mode == "single":
         own, own_s, tp, right, *outs, placed = refs
@@ -100,7 +101,9 @@
             after = pltpu.roll(after, 4, 0) if part == 0 else after
         return jnp.where(row_of < 6, pltpu.roll(links(part, y, i), 6, 0), after)
 
-    trs[6 * count :] = jnp.zeros((2 * count, 128), F32)
+    for group in range(2 if whole else 1):
+        first = (8 * group + 6) * count
+        trs[first : first + 2 * count] = jnp.zeros((2 * count, 128), F32)
     for part in range(parts):
         inner = jnp.where(row_of >= 6, 1, 0)
         leaves = (row_of % 2, 1 - row_of // 2 % 2 if part == 2 else inner, 1, 0)
@@ -131,7 +134,7 @@
                 moved = (active[n] ^ leaves[m]) | (active[m] ^ leaves[n]) | active[m] | active[n]
                 frozen = jnp.broadcast_to(moved, (8, 128)) == 0
                 for k, value in enumerate((re, im)):
-                    row = (2 * p + k) * count + 16 * part + 8 * y
+                    row = (2 * p + k + 2 * (p // 3)) * count + 16 * part + 8 * y
                     trs[row : row + 8] = jnp.where(frozen, value * (1.0 / 3.0), 0.0)
     for r in range(count if merge else 0):
         place = r
@@ -143,8 +146,12 @@
                 partner, x = row // 4, (0, 5)[row // 2 % 2]
             t = (3, 0)[row % 2] if partner else 1 + row % 2
             place = (6 * y + x) * 4 + t
-        halves = [ref[pl.ds(r, 8, stride=count), :] for ref in (others, trs)]
-        outs[0][place] = jnp.concatenate(halves, axis=0).astype(BF16)
+        if whole:
+            channels = trs[pl.ds(r, 16, stride=count), :]
+        else:
+            halves = [ref[pl.ds(r, 8, stride=count), :] for ref in (others, trs)]
+            channels = jnp.concatenate(halves, axis=0)
+        outs[0][place] = channels.astype(BF16)
 
 
 def staple_kernel(mode, ya, *refs):
@@ -165,8 +172,14 @@
             v0[i, y, BASE : BASE + 8] = o
             v0[i, y, BASE - 2 : BASE] = hh[0:2]
             v0[i, y, BASE + 8 : BASE + 10] = hh[2:4]
-            vup[i, y, BASE : BASE + 8] = jnp.where(even, pltpu.roll(o, 7, 0), pltpu.roll(t, 1, 0))
-            vdn[i, y, BASE : BASE + 8] = jnp.where(even, pltpu.roll(t, 7, 0), pltpu.roll(o, 1, 0))
+            if y < 3:
+                vup[i, y, BASE : BASE + 8] = jnp.where(
+                    even, pltpu.roll(o, 7, 0), pltpu.roll(t, 1, 0)
+                )
+            if y > 0:
+                vdn[i, y, BASE : BASE + 8] = jnp.where(
+                    even, pltpu.roll(t, 7, 0), pltpu.roll(o, 1, 0)
+                )
         return 0
 
     lax.fori_loop(0, 72, prep, 0, unroll=4)
@@ -479,11 +492,13 @@
 
 def run_traces(mode, half, ya, *inputs):
     rows = (16 if mode == "single" else 48 if mode == "wide" else 16)
-    channels = (8 * rows, 128)
+    planes = HALVES[mode != "single"]
+    planes = planes[0] + planes[1] if half == 2 else planes[half]
+    channels = (8 * rows * (len(planes) // 3), 128)
     placed = [pltpu.VMEM((72, 2, 8, 128), F32)] if mode == "single" else []
     shape = ((rows, 16, 128), BF16) if half else (channels, F32)
     return pl.pallas_call(
-        functools.partial(trace_kernel, mode, HALVES[mode != "single"][half], half == 1),
+        functools.partial(trace_kernel, mode, planes, half > 0),
         out_shape=jax.ShapeDtypeStruct(*shape),
         in_specs=[SM] + [VM] * len(inputs),
         out_specs=VM,
@@ -592,8 +607,7 @@
     h = jnp.concatenate([left, right], axis=2)
     h_s = step(h, "sub", 1)
     (tp,) = run_unpack(tp_raw, False)
-    half = run_traces("single", 0, ya[0], own, own_s, own, right)
-    tr = run_traces("single", 1, ya[0], half, own, own_s, tp, right).reshape(2, 4, 2, 16, 128)
+    tr = run_traces("single", 2, ya[0], own, own_s, tp, right).reshape(2, 4, 2, 16, 128)
     far = other_rows(right)
     full = other_traces(tr)
     full, co, far, tail = lax.optimization_barrier((full, co, far, tail))

time: 59.7 us -> 59.5 us (level)
  waiting for transfers between devices: 13.3 us -> 14.7 us
  Pallas kernels: 18.2 us -> 17.3 us
  starting transfers between devices: 22.3 us -> 21.6 us
    ppermute x7, starting transfers between devices: 10.6 us -> 9.33 us  [diagonal(): return lax.ppermute(value, ('space', 'tm'), pairs)]
    pallas_call x4 -> x3, Pallas kernels: 6.31 us -> 5.57 us  [run_traces(): pl.pallas_call(functools.partial(trace_kernel, mode, planes, half > 0), o...]
    ppermute x7, waiting for transfers between devices: 9.63 us -> 10.3 us  [diagonal(): return lax.ppermute(value, ('space', 'tm'), pairs)]
    ppermute x14, waiting for transfers between devices: 3.71 us -> 4.36 us  [step(): lax.ppermute(value, axis, [((i + by) % count, i) for i in range(count)])]
    ppermute x14, starting transfers between devices: 11.7 us -> 12.3 us  [step(): lax.ppermute(value, axis, [((i + by) % count, i) for i in range(count)])]
  transfers between devices with their start and end apart: 21 -> 21, of which waited for: 6 -> 7; matrix products, arithmetic and copies ran while one was open for 7% -> 7% of each run, Pallas kernels for 24% -> 23%
where the time goes in v6:
time: 59.5 us; the launch traced here: 59.3 us
  starting transfers between devices  21.6 us (36%)
  Pallas kernels  17.3 us (29%)
  waiting for transfers between devices  14.7 us (25%)
  local copies, waits for them, and re-layouts  3.99 us (7%)
  other arithmetic  1.22 us (2%)
    ppermute x14, starting transfers between devices, step(): lax.ppermute(value, axis, [((i + by) % count, i) for i in range(count)])  12.3 us
    ppermute x7, waiting for transfers between devices, diagonal(): return lax.ppermute(value, ('space', 'tm'), pairs)  10.3 us
    ppermute x7, starting transfers between devices, diagonal(): return lax.ppermute(value, ('space', 'tm'), pairs)  9.33 us
    pallas_call x3, Pallas kernels, run_traces(): pl.pallas_call(functools.partial(trace_kernel, mode, planes, half > 0), o...  5.57 us
    pallas_call x2, Pallas kernels, run_staples(): pl.pallas_call(functools.partial(staple_kernel, mode), out_shape=jax.Shap...  5.03 us
    ppermute x14, waiting for transfers between devices, step(): lax.ppermute(value, axis, [((i + by) % count, i) for i in range(count)])  4.36 us
    pallas_call x2, Pallas kernels, run_final(): pl.pallas_call(last_kernel if last else final_kernel, out_shape=[jax.Shap...  4.33 us
    unnamed x12, local copies, waits for them, and re-layouts  2.8 us
  transfers between devices with their start and end apart: 21, of which 7 were waited for; matrix products, arithmetic and copies ran while one was open for 7% of the time, Pallas kernels for 23%

profile of v6, /device:TPU:0, one launch (start us, length us, event | category | flops | bytes accessed | tf_op | source)
XLA Modules:
  0.0 59.3 jit_solution(13403240301161990895)
XLA Ops:
  0.0 2.9 %collective-permute-start.3 = (f32[4,18,2,4,2,128]{5,4,3,2,1,0:T(2,128)}, f32[4,18,2,4,2,128]{5,4,3,2,1,0:T(2,128)S(1)}, u32[]{:S(2)}, u32[]{:S(2)}) collective-permute-start(f32[4,18,2,4,2,128]{5,4,3,2,1,0:T(2,128)} %param.6), channel_id=1, source_target_pairs={{2,0},{0,2},{6,4},{4,6},{10,8},{8,10},{14,12},{12,14},{3,1},{1,3},... | collective-permute-start | bytes 1769480 | tf_op jit(solution)/shard_map/ppermute | solution.py:571
  2.9 1.1 %copy-done = f32[4,18,2,4,2,128]{5,4,3,2,1,0:T(2,128)S(1)} copy-done((f32[4,18,2,4,2,128]{5,4,3,2,1,0:T(2,128)S(1)}, f32[4,18,2,4,2,128]{5,4,3,2,1,0:T(2,128)}, u32[]{:S(2)}) %copy-start) | copy-done | bytes 589848
  4.0 0.3 unpack.2
  4.4 3.7 %collective-permute-start = (f32[72,2,2,128]{3,2,1,0:T(2,128)S(1)}, f32[72,2,2,128]{3,2,1,0:T(2,128)S(1)}, u32[]{:S(2)}, u32[]{:S(2)}) collective-permute-start(f32[72,2,2,128]{3,2,1,0:T(2,128)S(1)} %get-tuple-element.40), channel_id=1, source_target_pairs={{4,0},{8,4},{12,8},{0,12},{5,1},{9,5},{13,9},{1,13},{6,2},{10,6},{... | collective-permute-start | bytes 442376 | tf_op jit(solution)/shard_map/ppermute | solution.py:561
  8.2 0.9 %copy.15 = f32[72,2,6,128]{3,0,2,1:T(8,128)} copy(f32[72,2,6,128]{3,2,1,0:T(8,128)S(1)} %tail.1) | data formatting | bytes 884736 | tf_op jit(solution)/shard_map/tail/pallas_call | solution.py:482
  9.1 3.8 %collective-permute-start.7 = (f32[72,2,6,128]{3,0,2,1:T(8,128)}, f32[72,2,6,128]{3,0,2,1:T(8,128)S(1)}, u32[]{:S(2)}, u32[]{:S(2)}) collective-permute-start(f32[72,2,6,128]{3,0,2,1:T(8,128)} %copy.15), channel_id=1, source_target_pairs={{4,0},{8,4},{12,8},{0,12},{5,1},{9,5},{13,9},{1,13},{6,2},{10,6},{... | collective-permute-start | bytes 1327112 | tf_op jit(solution)/shard_map/ppermute | solution.py:561
  13.0 1.6 %copy.13.conv_in = bf16[2,81,12,64]{3,2,1,0:T(8,128)(2,1)S(1)} copy(bf16[2,81,12,64]{1,3,2,0:T(8,128)(2,1)} %param.8) | data formatting | bytes 497664 | tf_op args[2]
  14.6 0.5 weights.1
  15.1 1.0 %fusion = s32[2,4]{1,0:T(2,128)S(1)} fusion(s32[2,4,2,4,4]{4,3,2,1,0:T(4,128)} %param.7, s32[]{:T(128)S(6)} %select_n.16, s32[]{:T(128)S(6)} %select_n.17, s32[]{:T(128)S(6)} %select_n.18), kind=kLoop, calls=%fused_computation.7 | loop fusion | flops 16 | bytes 76 | tf_op jit(solution)/shard_map/jit(_where)/select_n | solution.py:590
  16.1 0.5 collective-permute-done.1
  16.7 0.6 %collective-permute-start.5 = (f32[18,2,2,128]{3,2,1,0:T(2,128)S(1)}, f32[18,2,2,128]{3,2,1,0:T(2,128)S(1)}, u32[]{:S(2)}, u32[]{:S(2)}) collective-permute-start(f32[18,2,2,128]{3,2,1,0:T(2,128)S(1)} %pad_maximum_fusion.2), channel_id=1, source_target_pairs={{2,0},{0,2},{6,4},{4,6},{10,8},{8,10},{14,12},{12,14},{3,1},{1,3},... | collective-permute-start | bytes 110600 | tf_op jit(solution)/shard_map/ppermute | solution.py:571
  17.3 1.5 %collective-permute-start.6 = (f32[72,2,1,2,128]{4,3,1,0,2:T(2,128)S(1)}, f32[72,2,1,2,128]{4,3,1,0,2:T(2,128)S(1)}, u32[]{:S(2)}, u32[]{:S(2)}) collective-permute-start(f32[72,2,1,2,128]{4,3,1,0,2:T(2,128)S(1)} %bitcast.16), channel_id=1, source_target_pairs={{2,0},{0,2},{6,4},{4,6},{10,8},{8,10},{14,12},{12,14},{3,1},{1,3},... | collective-permute-start | bytes 442376 | tf_op jit(solution)/shard_map/ppermute | solution.py:571
  18.9 1.6 %traces.3 = bf16[16,16,128]{2,1,0:T(8,128)(2,1)S(1)} custom-call(s32[4]{0:T(128)S(1)} %get-tuple-element.79.ya, f32[72,2,8,128]{3,2,1,0:T(8,128)S(1)} %get-tuple-element.51.refs_0_.own, f32[72,2,8,128]{3,2,1,0:T(8,128)S(1)} %collective-permute-done.2.refs_1_, f32[72,2,8,128]{3,2,1,0:T(8,128)S(1)} %unpack.3.refs_2_.tp, ...), custom_call_target="tpu_custom_call" | custom-call | flops 4000000 | bytes 4000000 | tf_op jit(solution)/shard_map/traces/pallas_call | solution.py:500
  20.5 0.6 %collective-permute-start.4 = (bf16[2,4,2,16,128]{4,3,2,1,0:T(8,128)(2,1)S(1)}, bf16[2,4,2,16,128]{4,3,2,1,0:T(8,128)(2,1)S(1)}, u32[]{:S(2)}, u32[]{:S(2)}) collective-permute-start(bf16[2,4,2,16,128]{4,3,2,1,0:T(8,128)(2,1)S(1)} %bitcast.21), channel_id=1, source_target_pairs={{2,0},{0,2},{6,4},{4,6},{10,8},{8,10},{14,12},{12,14},{3,1},{1,3},... | collective-permute-start | bytes 196616 | tf_op jit(solution)/shard_map/ppermute | solution.py:571
  21.4 3.5 %collective-permute-done.4 = bf16[2,4,2,16,128]{4,3,2,1,0:T(8,128)(2,1)S(1)} collective-permute-done((bf16[2,4,2,16,128]{4,3,2,1,0:T(8,128)(2,1)S(1)}, bf16[2,4,2,16,128]{4,3,2,1,0:T(8,128)(2,1)S(1)}, u32[]{:S(2)}, u32[]{:S(2)}) %collective-permute-start.4) | collective-permute-done | bytes 65568 | tf_op jit(solution)/shard_map/ppermute | solution.py:571
  24.9 0.6 collective-permute-start.12
  25.5 3.3 %collective-permute-start.9 = (bf16[2,1,4,16,128]{4,3,2,1,0:T(8,128)(2,1)S(1)}, bf16[2,1,4,16,128]{4,3,2,1,0:T(8,128)(2,1)S(1)}, u32[]{:S(2)}, u32[]{:S(2)}) collective-permute-start(bf16[2,1,4,16,128]{4,3,2,1,0:T(8,128)(2,1)S(1)} %get-tuple-element.75), channel_id=1, source_target_pairs={{4,0},{8,4},{12,8},{0,12},{5,1},{9,5},{13,9},{1,13},{6,2},{10,6},{... | collective-permute-start | bytes 98312 | tf_op jit(solution)/shard_map/ppermute | solution.py:561
  28.9 0.7 %collective-permute-start.14 = (f32[72,2,3,2,128]{4,0,3,2,1:T(8,128)S(1)}, f32[72,2,3,2,128]{4,0,3,2,1:T(8,128)S(1)}, u32[]{:S(2)}, u32[]{:S(2)}) collective-permute-start(f32[72,2,3,2,128]{4,0,3,2,1:T(8,128)S(1)} %bitcast.28), channel_id=1, source_target_pairs={{2,0},{0,2},{6,4},{4,6},{10,8},{8,10},{14,12},{12,14},{3,1},{1,3},... | collective-permute-start | bytes 1327112 | tf_op jit(solution)/shard_map/ppermute | solution.py:571
  29.6 2.5 %staples.2 = f32[24,18,8,128]{3,2,1,0:T(8,128)S(1)} custom-call(s32[4]{0:T(128)S(1)} %get-tuple-element.79.ya, f32[72,2,8,128]{3,2,1,0:T(8,128)S(1)} %get-tuple-element.51.refs_0_.own, f32[72,2,8,128]{3,2,1,0:T(8,128)S(1)} %collective-permute-done.2.refs_1_, f32[72,2,8,128]{3,2,1,0:T(8,128)S(1)} %unpack.3.refs_2_.tp, ...), custom_call_target="tpu_custom_call" | custom-call | flops 20000000 | bytes 16000000 | tf_op jit(solution)/shard_map/staples/pallas_call | solution.py:513
  32.2 2.4 %collective-permute-done.8 = bf16[2,1,4,16,128]{4,3,2,1,0:T(8,128)(2,1)S(1)} collective-permute-done((bf16[2,1,4,16,128]{4,3,2,1,0:T(8,128)(2,1)S(1)}, bf16[2,1,4,16,128]{4,3,2,1,0:T(8,128)(2,1)S(1)}, u32[]{:S(2)}, u32[]{:S(2)}) %collective-permute-start.8) | collective-permute-done | bytes 32800 | tf_op jit(solution)/shard_map/ppermute | solution.py:561
  34.7 1.4 %collective-permute-done.13.f_s = bf16[2,6,4,16,128]{4,3,2,1,0:T(8,128)(2,1)S(1)} collective-permute-done((bf16[2,6,4,16,128]{4,3,2,1,0:T(8,128)(2,1)S(1)}, bf16[2,6,4,16,128]{4,3,2,1,0:T(8,128)(2,1)S(1)}, u32[]{:S(2)}, u32[]{:S(2)}) %collective-permute-start.13) | collective-permute-done | bytes 196640 | tf_op jit(solution)/shard_map/ppermute | solution.py:561
  36.1 1.8 %rotate.2 = (f32[72,2,8,128]{3,2,1,0:T(8,128)S(1)}, f32[36,8,128]{2,1,0:T(8,128)S(1)}) custom-call(s32[4]{0:T(128)S(1)} %get-tuple-element.79.ya, f32[72,2,8,128]{3,2,1,0:T(8,128)S(1)} %get-tuple-element.51.refs_0_.own, f32[24,18,8,128]{3,2,1,0:T(8,128)S(1)} %staples.2, bf16[2,6,4,16,128]{4,3,2,1,0:T(8,128)(2,1)S(1)} %constant_dynamic-update-slice_fusion.f, ...), custom_call_target="tpu_custom_call" | custom-call | flops 300000000 | bytes 4000000 | tf_op jit(solution)/shard_map/rotate/pallas_call | solution.py:530
  37.9 2.2 %collective-permute-start.17 = (f32[36,4,2,128]{3,2,1,0:T(2,128)S(1)}, f32[36,4,2,128]{3,2,1,0:T(2,128)S(1)}, u32[]{:S(2)}, u32[]{:S(2)}) collective-permute-start(f32[36,4,2,128]{3,2,1,0:T(2,128)S(1)} %bitcast.26), channel_id=1, source_target_pairs={{6,0},{4,2},{10,4},{8,6},{14,8},{12,10},{2,12},{0,14},{7,1},{5,3},... | collective-permute-start | bytes 442376 | tf_op jit(solution)/shard_map/ppermute | solution.py:571
  40.1 0.7 %collective-permute-start.16 = (f32[36,4,2,128]{3,2,1,0:T(2,128)S(1)}, f32[36,4,2,128]{3,2,1,0:T(2,128)S(1)}, u32[]{:S(2)}, u32[]{:S(2)}) collective-permute-start(f32[36,4,2,128]{3,2,1,0:T(2,128)S(1)} %bitcast.27), channel_id=1, source_target_pairs={{2,0},{0,2},{6,4},{4,6},{10,8},{8,10},{14,12},{12,14},{3,1},{1,3},... | collective-permute-start | bytes 442376 | tf_op jit(solution)/shard_map/ppermute | solution.py:571
  41.2 4.4 %collective-permute-done.17 = f32[36,4,2,128]{3,2,1,0:T(2,128)S(1)} collective-permute-done((f32[36,4,2,128]{3,2,1,0:T(2,128)S(1)}, f32[36,4,2,128]{3,2,1,0:T(2,128)S(1)}, u32[]{:S(2)}, u32[]{:S(2)}) %collective-permute-start.17) | collective-permute-done | bytes 147488 | tf_op jit(solution)/shard_map/ppermute | solution.py:571
  45.6 2.4 %collective-permute-done.16 = f32[36,4,2,128]{3,2,1,0:T(2,128)S(1)} collective-permute-done((f32[36,4,2,128]{3,2,1,0:T(2,128)S(1)}, f32[36,4,2,128]{3,2,1,0:T(2,128)S(1)}, u32[]{:S(2)}, u32[]{:S(2)}) %collective-permute-start.16) | collective-permute-done | bytes 147488 | tf_op jit(solution)/shard_map/ppermute | solution.py:571
  47.9 1.5 %shift.1 = (f32[72,2,8,128]{3,2,1,0:T(8,128)S(1)}, f32[216,8,128]{2,1,0:T(8,128)S(1)}, f32[216,8,128]{2,1,0:T(8,128)S(1)}, f32[72,2,8,128]{3,2,1,0:T(8,128)S(1)}) custom-call(s32[4]{0:T(128)S(1)} %get-tuple-element.79.ya, f32[72,2,8,128]{3,2,1,0:T(8,128)S(1)} %get-tuple-element.63.own, f32[72,2,2,128]{3,2,1,0:T(2,128)S(1)} %collective-permute-done.refs_3_.right, ...), custom_call_target="tpu_custom_call" | custom-call | flops 8000000 | bytes 6000000 | tf_op jit(solution)/shard_map/shift/pallas_call | solution.py:548
  49.5 0.5 collective-permute-start.19
  50.0 2.0 %traces.4.refs_0_ = f32[384,128]{1,0:T(8,128)S(1)} custom-call(s32[4]{0:T(128)S(1)} %get-tuple-element.80.ya, f32[216,8,128]{2,1,0:T(8,128)S(1)} %get-tuple-element.68.refs_0_.refs_2_.refs_1_, f32[216,8,128]{2,1,0:T(8,128)S(1)} %get-tuple-element.69.refs_1_.refs_2_, f32[216,8,128]{2,1,0:T(8,128)S(1)} %get-tuple-element.68.refs_0_.refs_2_.refs_1_, ...), custom_call_target="tpu_custom_call" | custom-call | flops 4000000 | bytes 4000000 | tf_op jit(solution)/shard_map/traces/pallas_call | solution.py:500
  52.0 2.0 %traces.5 = bf16[48,16,128]{2,1,0:T(8,128)(2,1)S(1)} custom-call(s32[4]{0:T(128)S(1)} %get-tuple-element.80.ya, f32[384,128]{1,0:T(8,128)S(1)} %traces.4.refs_0_, f32[216,8,128]{2,1,0:T(8,128)S(1)} %get-tuple-element.68.refs_0_.refs_2_.refs_1_, f32[216,8,128]{2,1,0:T(8,128)S(1)} %get-tuple-element.69.refs_1_.refs_2_, ...), custom_call_target="tpu_custom_call" | custom-call | flops 4000000 | bytes 4000000 | tf_op jit(solution)/shard_map/traces/pallas_call | solution.py:500
  54.1 2.5 %staples.3 = f32[24,18,8,128]{3,2,1,0:T(8,128)S(1)} custom-call(s32[4]{0:T(128)S(1)} %get-tuple-element.80.ya, f32[216,8,128]{2,1,0:T(8,128)S(1)} %get-tuple-element.68.refs_0_.refs_2_.refs_1_, f32[216,8,128]{2,1,0:T(8,128)S(1)} %get-tuple-element.69.refs_1_.refs_2_, f32[216,8,128]{2,1,0:T(8,128)S(1)} %collective-permute-done.18.refs_2_.refs_3_, ...), custom_call_target="tpu_custom_call" | custom-call | flops 20000000 | bytes 16000000 | tf_op jit(solution)/shard_map/staples/pallas_call | solution.py:513
  56.6 2.5 %rotate.3 = f32[72,16,128]{2,1,0:T(8,128)} custom-call(s32[4]{0:T(128)S(1)} %get-tuple-element.80.ya, f32[72,2,8,128]{3,2,1,0:T(8,128)S(1)} %get-tuple-element.67.own, f32[24,18,8,128]{3,2,1,0:T(8,128)S(1)} %staples.3, bf16[2,6,4,16,128]{4,3,2,1,0:T(8,128)(2,1)S(1)} %bitcast.18, bf16[2,6,4,16,128]{4,3,2,1,0:T(8,128)(2,1)S(1)} %collective-permute-done.20.f_s, ...), custom_call_target="tpu_custom_call" | custom-call | flops 300000000 | bytes 4000000 | tf_op jit(solution)/shard_map/rotate/pallas_call | solution.py:530
  (47 shorter events, 1.4 us)
Async XLA Ops:
  0.0 18.8 %collective-permute-start.3 = (f32[4,18,2,4,2,128]{5,4,3,2,1,0:T(2,128)}, f32[4,18,2,4,2,128]{5,4,3,2,1,0:T(2,128)S(1)}, u32[]{:S(2)}, u32[]{:S(2)}) collective-permute-start(f32[4,18,2,4,2,128]{5,4,3,2,1,0:T(2,128)} %param.6), channel_id=1, source_target_pairs={{2,0},{0,2},{6,4},{4,6},{10,8},{8,10},{14,12},{12,14},{3,1},{1,3},... | collective-permute-start | bytes 1769480 | tf_op jit(solution)/shard_map/ppermute | solution.py:571
  2.9 1.1 %copy-start = (f32[4,18,2,4,2,128]{5,4,3,2,1,0:T(2,128)S(1)}, f32[4,18,2,4,2,128]{5,4,3,2,1,0:T(2,128)}, u32[]{:S(2)}) copy-start(f32[4,18,2,4,2,128]{5,4,3,2,1,0:T(2,128)} %param.6) | copy-start | bytes 1769476
  4.0 8.9 %copy-start.3 = (bf16[2,64,24]{1,2,0:T(8,128)(2,1)S(1)}, bf16[2,64,24]{1,2,0:T(8,128)(2,1)}, u32[]{:S(2)}) copy-start(bf16[2,64,24]{1,2,0:T(8,128)(2,1)} %param.10) | copy-start | bytes 18436
  4.3 10.2 %copy-start.1 = (f32[2,64]{1,0:T(2,128)S(1)}, f32[2,64]{1,0:T(2,128)}, u32[]{:S(2)}) copy-start(f32[2,64]{1,0:T(2,128)} %bias_in.1) | copy-start | bytes 1540
  4.4 10.2 %copy-start.2 = (f32[2,24]{1,0:T(2,128)S(1)}, f32[2,24]{1,0:T(2,128)}, u32[]{:S(2)}) copy-start(f32[2,24]{1,0:T(2,128)} %bias_out.1) | copy-start | bytes 580
  4.4 14.6 %collective-permute-start.2 = (f32[72,2,8,128]{3,2,1,0:T(8,128)S(1)}, f32[72,2,8,128]{3,2,1,0:T(8,128)S(1)}, u32[]{:S(2)}, u32[]{:S(2)}) collective-permute-start(f32[72,2,8,128]{3,2,1,0:T(8,128)S(1)} %get-tuple-element.51.refs_0_.own), channel_id=1, source_target_pairs={{1,0},{0,1},{3,2},{2,3},{5,4},{4,5},{7,6},{6,7},{9,8},{8,9},{11,10... | collective-permute-start | bytes 1769480 | tf_op jit(solution)/shard_map/ppermute | solution.py:561
  4.4 11.7 %collective-permute-start = (f32[72,2,2,128]{3,2,1,0:T(2,128)S(1)}, f32[72,2,2,128]{3,2,1,0:T(2,128)S(1)}, u32[]{:S(2)}, u32[]{:S(2)}) collective-permute-start(f32[72,2,2,128]{3,2,1,0:T(2,128)S(1)} %get-tuple-element.40), channel_id=1, source_target_pairs={{4,0},{8,4},{12,8},{0,12},{5,1},{9,5},{13,9},{1,13},{6,2},{10,6},{... | collective-permute-start | bytes 442376 | tf_op jit(solution)/shard_map/ppermute | solution.py:561
  8.1 8.5 %collective-permute-start.1 = (f32[72,2,2,128]{3,2,1,0:T(2,128)S(1)}, f32[72,2,2,128]{3,2,1,0:T(2,128)S(1)}, u32[]{:S(2)}, u32[]{:S(2)}) collective-permute-start(f32[72,2,2,128]{3,2,1,0:T(2,128)S(1)} %get-tuple-element.41), channel_id=1, source_target_pairs={{12,0},{0,4},{4,8},{8,12},{13,1},{1,5},{5,9},{9,13},{14,2},{2,6},{... | collective-permute-start | bytes 442376 | tf_op jit(solution)/shard_map/ppermute | solution.py:561
  9.1 15.8 %collective-permute-start.7 = (f32[72,2,6,128]{3,0,2,1:T(8,128)}, f32[72,2,6,128]{3,0,2,1:T(8,128)S(1)}, u32[]{:S(2)}, u32[]{:S(2)}) collective-permute-start(f32[72,2,6,128]{3,0,2,1:T(8,128)} %copy.15), channel_id=1, source_target_pairs={{4,0},{8,4},{12,8},{0,12},{5,1},{9,5},{13,9},{1,13},{6,2},{10,6},{... | collective-permute-start | bytes 1327112 | tf_op jit(solution)/shard_map/ppermute | solution.py:561
  16.7 8.2 %collective-permute-start.5 = (f32[18,2,2,128]{3,2,1,0:T(2,128)S(1)}, f32[18,2,2,128]{3,2,1,0:T(2,128)S(1)}, u32[]{:S(2)}, u32[]{:S(2)}) collective-permute-start(f32[18,2,2,128]{3,2,1,0:T(2,128)S(1)} %pad_maximum_fusion.2), channel_id=1, source_target_pairs={{2,0},{0,2},{6,4},{4,6},{10,8},{8,10},{14,12},{12,14},{3,1},{1,3},... | collective-permute-start | bytes 110600 | tf_op jit(solution)/shard_map/ppermute | solution.py:571
  17.3 7.6 %collective-permute-start.6 = (f32[72,2,1,2,128]{4,3,1,0,2:T(2,128)S(1)}, f32[72,2,1,2,128]{4,3,1,0,2:T(2,128)S(1)}, u32[]{:S(2)}, u32[]{:S(2)}) collective-permute-start(f32[72,2,1,2,128]{4,3,1,0,2:T(2,128)S(1)} %bitcast.16), channel_id=1, source_target_pairs={{2,0},{0,2},{6,4},{4,6},{10,8},{8,10},{14,12},{12,14},{3,1},{1,3},... | collective-permute-start | bytes 442376 | tf_op jit(solution)/shard_map/ppermute | solution.py:571
  20.5 4.3 %collective-permute-start.4 = (bf16[2,4,2,16,128]{4,3,2,1,0:T(8,128)(2,1)S(1)}, bf16[2,4,2,16,128]{4,3,2,1,0:T(8,128)(2,1)S(1)}, u32[]{:S(2)}, u32[]{:S(2)}) collective-permute-start(bf16[2,4,2,16,128]{4,3,2,1,0:T(8,128)(2,1)S(1)} %bitcast.21), channel_id=1, source_target_pairs={{2,0},{0,2},{6,4},{4,6},{10,8},{8,10},{14,12},{12,14},{3,1},{1,3},... | collective-permute-start | bytes 196616 | tf_op jit(solution)/shard_map/ppermute | solution.py:571
  21.3 7.6 %collective-permute-start.11 = (f32[72,2,4,128]{3,2,1,0:T(4,128)S(1)}, f32[72,2,4,128]{3,2,1,0:T(4,128)S(1)}, u32[]{:S(2)}, u32[]{:S(2)}) collective-permute-start(f32[72,2,4,128]{3,2,1,0:T(4,128)S(1)} %pad_maximum_fusion.refs_4_), channel_id=1, source_target_pairs={{1,0},{0,1},{3,2},{2,3},{5,4},{4,5},{7,6},{6,7},{9,8},{8,9},{11,10... | collective-permute-start | bytes 884744 | tf_op jit(solution)/shard_map/ppermute | solution.py:561
  24.9 4.7 %collective-permute-start.10 = (f32[72,2,8,128]{3,2,1,0:T(8,128)S(1)}, f32[72,2,8,128]{3,2,1,0:T(8,128)S(1)}, u32[]{:S(2)}, u32[]{:S(2)}) collective-permute-start(f32[72,2,8,128]{3,2,1,0:T(8,128)S(1)} %unpack.3.refs_2_.tp), channel_id=1, source_target_pairs={{1,0},{0,1},{3,2},{2,3},{5,4},{4,5},{7,6},{6,7},{9,8},{8,9},{11,10... | collective-permute-start | bytes 1769480 | tf_op jit(solution)/shard_map/ppermute | solution.py:561
  24.9 4.7 %collective-permute-start.12 = (f32[18,2,2,128]{3,2,1,0:T(2,128)S(1)}, f32[18,2,2,128]{3,2,1,0:T(2,128)S(1)}, u32[]{:S(2)}, u32[]{:S(2)}) collective-permute-start(f32[18,2,2,128]{3,2,1,0:T(2,128)S(1)} %collective-permute-done.5.refs_6_), channel_id=1, source_target_pairs={{1,0},{0,1},{3,2},{2,3},{5,4},{4,5},{7,6},{6,7},{9,8},{8,9},{11,10... | collective-permute-start | bytes 110600 | tf_op jit(solution)/shard_map/ppermute | solution.py:561
  25.5 6.6 %collective-permute-start.9 = (bf16[2,1,4,16,128]{4,3,2,1,0:T(8,128)(2,1)S(1)}, bf16[2,1,4,16,128]{4,3,2,1,0:T(8,128)(2,1)S(1)}, u32[]{:S(2)}, u32[]{:S(2)}) collective-permute-start(bf16[2,1,4,16,128]{4,3,2,1,0:T(8,128)(2,1)S(1)} %get-tuple-element.75), channel_id=1, source_target_pairs={{4,0},{8,4},{12,8},{0,12},{5,1},{9,5},{13,9},{1,13},{6,2},{10,6},{... | collective-permute-start | bytes 98312 | tf_op jit(solution)/shard_map/ppermute | solution.py:561
  28.8 5.7 %collective-permute-start.8 = (bf16[2,1,4,16,128]{4,3,2,1,0:T(8,128)(2,1)S(1)}, bf16[2,1,4,16,128]{4,3,2,1,0:T(8,128)(2,1)S(1)}, u32[]{:S(2)}, u32[]{:S(2)}) collective-permute-start(bf16[2,1,4,16,128]{4,3,2,1,0:T(8,128)(2,1)S(1)} %get-tuple-element.76), channel_id=1, source_target_pairs={{12,0},{0,4},{4,8},{8,12},{13,1},{1,5},{5,9},{9,13},{14,2},{2,6},{... | collective-permute-start | bytes 98312 | tf_op jit(solution)/shard_map/ppermute | solution.py:561
  28.9 12.2 %collective-permute-start.14 = (f32[72,2,3,2,128]{4,0,3,2,1:T(8,128)S(1)}, f32[72,2,3,2,128]{4,0,3,2,1:T(8,128)S(1)}, u32[]{:S(2)}, u32[]{:S(2)}) collective-permute-start(f32[72,2,3,2,128]{4,0,3,2,1:T(8,128)S(1)} %bitcast.28), channel_id=1, source_target_pairs={{2,0},{0,2},{6,4},{4,6},{10,8},{8,10},{14,12},{12,14},{3,1},{1,3},... | collective-permute-start | bytes 1327112 | tf_op jit(solution)/shard_map/ppermute | solution.py:571
  34.6 1.5 %collective-permute-start.13 = (bf16[2,6,4,16,128]{4,3,2,1,0:T(8,128)(2,1)S(1)}, bf16[2,6,4,16,128]{4,3,2,1,0:T(8,128)(2,1)S(1)}, u32[]{:S(2)}, u32[]{:S(2)}) collective-permute-start(bf16[2,6,4,16,128]{4,3,2,1,0:T(8,128)(2,1)S(1)} %constant_dynamic-update-slice_fusion.f), channel_id=1, source_target_pairs={{1,0},{0,1},{3,2},{2,3},{5,4},{4,5},{7,6},{6,7},{9,8},{8,9},{11,10... | collective-permute-start | bytes 589832 | tf_op jit(solution)/shard_map/ppermute | solution.py:561
  37.9 7.6 %collective-permute-start.17 = (f32[36,4,2,128]{3,2,1,0:T(2,128)S(1)}, f32[36,4,2,128]{3,2,1,0:T(2,128)S(1)}, u32[]{:S(2)}, u32[]{:S(2)}) collective-permute-start(f32[36,4,2,128]{3,2,1,0:T(2,128)S(1)} %bitcast.26), channel_id=1, source_target_pairs={{6,0},{4,2},{10,4},{8,6},{14,8},{12,10},{2,12},{0,14},{7,1},{5,3},... | collective-permute-start | bytes 442376 | tf_op jit(solution)/shard_map/ppermute | solution.py:571
  40.1 7.8 %collective-permute-start.16 = (f32[36,4,2,128]{3,2,1,0:T(2,128)S(1)}, f32[36,4,2,128]{3,2,1,0:T(2,128)S(1)}, u32[]{:S(2)}, u32[]{:S(2)}) collective-permute-start(f32[36,4,2,128]{3,2,1,0:T(2,128)S(1)} %bitcast.27), channel_id=1, source_target_pairs={{2,0},{0,2},{6,4},{4,6},{10,8},{8,10},{14,12},{12,14},{3,1},{1,3},... | collective-permute-start | bytes 442376 | tf_op jit(solution)/shard_map/ppermute | solution.py:571
  40.9 7.0 %collective-permute-start.15 = (f32[36,8,128]{2,1,0:T(8,128)S(1)}, f32[36,8,128]{2,1,0:T(8,128)S(1)}, u32[]{:S(2)}, u32[]{:S(2)}) collective-permute-start(f32[36,8,128]{2,1,0:T(8,128)S(1)} %get-tuple-element.66), channel_id=1, source_target_pairs={{4,0},{8,4},{12,8},{0,12},{5,1},{9,5},{13,9},{1,13},{6,2},{10,6},{... | collective-permute-start | bytes 442376 | tf_op jit(solution)/shard_map/ppermute | solution.py:561
  49.4 2.6 %collective-permute-start.18 = (f32[216,8,128]{2,1,0:T(8,128)S(1)}, f32[216,8,128]{2,1,0:T(8,128)S(1)}, u32[]{:S(2)}, u32[]{:S(2)}) collective-permute-start(f32[216,8,128]{2,1,0:T(8,128)S(1)} %get-tuple-element.68.refs_0_.refs_2_.refs_1_), channel_id=1, source_target_pairs={{1,0},{0,1},{3,2},{2,3},{5,4},{4,5},{7,6},{6,7},{9,8},{8,9},{11,10... | collective-permute-start | bytes 2654216 | tf_op jit(solution)/shard_map/ppermute | solution.py:561
  49.5 4.6 %collective-permute-start.19 = (f32[216,8,128]{2,1,0:T(8,128)S(1)}, f32[216,8,128]{2,1,0:T(8,128)S(1)}, u32[]{:S(2)}, u32[]{:S(2)}) collective-permute-start(f32[216,8,128]{2,1,0:T(8,128)S(1)} %get-tuple-element.69.refs_1_.refs_2_), channel_id=1, source_target_pairs={{1,0},{0,1},{3,2},{2,3},{5,4},{4,5},{7,6},{6,7},{9,8},{8,9},{11,10... | collective-permute-start | bytes 2654216 | tf_op jit(solution)/shard_map/ppermute | solution.py:561
  54.0 2.6 %collective-permute-start.20 = (bf16[2,6,4,16,128]{4,3,2,1,0:T(8,128)(2,1)S(1)}, bf16[2,6,4,16,128]{4,3,2,1,0:T(8,128)(2,1)S(1)}, u32[]{:S(2)}, u32[]{:S(2)}) collective-permute-start(bf16[2,6,4,16,128]{4,3,2,1,0:T(8,128)(2,1)S(1)} %bitcast.17), channel_id=1, source_target_pairs={{1,0},{0,1},{3,2},{2,3},{5,4},{4,5},{7,6},{6,7},{9,8},{8,9},{11,10... | collective-permute-start | bytes 589832 | tf_op jit(solution)/shard_map/ppermute | solution.py:561
